TPU v7x, 32 devices: a whole 2x2x4 slice. The times are simulated.
32 devices in a mesh: req: 8 (over z, y), tp: 4 (over x, core).
Axes of the slice: x: 2, y: 2, z: 4, core: 2. Of those that a mesh axis runs over, the one named last changes fastest.
Arguments:
- queries: bfloat16 [3072, 2048], P('req', 'tp'), may hold values from -32 to 32
- tree_kv: bfloat16 [3072, 256], P('req'), may hold values from -6 to 6
- suffix_kv: bfloat16 [48, 256, 256], P('req'), may hold values from -6 to 6
- suffix_len: int32 [48], P('req'), may hold values from 1 to 256
- group_ids: int32 [48], P('req'), may hold values from 0 to 1
- parents: int32 [48, 64], P('req'), may hold values from 0 to 62, as said below
- accepted: int32 [48, 8], P('req'), may hold values from 0 to 63, as said below
- prompt_kv: bfloat16 [2, 256, 256], P(None, 'req'), may hold values from -12 to 12
- out_weight: bfloat16 [2048, 2048], P('tp'), may hold values from -0.5 to 0.5
Outputs:
- layer_output: bfloat16 [3072, 2048], P(('req', 'tp'))
- path_cache: bfloat16 [48, 8, 256], P('req')
Inputs may be any that keep to these rules, and one draw needn't show every extreme that they name: parents[r, 0] = 0 and parents[r, i] < i for i >= 1, so node 0 is every tree's root. accepted[r] runs from the root down one branch: accepted[r, 0] = 0 and accepted[r, t - 1] = parents[r, accepted[r, t]].
All inputs are finite; a program needn't handle non-finite values.
Results may differ from a plain program's by a relative error of at most 0.017.
Values may be sent and summed in bfloat16 or wider, within the bound.
No kernel may reach another device: no remote copies, remote signals or barrier semaphores. Data moves between devices by JAX's collectives and lax.ppermute only.
A program may use at most 64 MiB of HBM per device.

v0:
```python
import jax
import jax.numpy as jnp
from jax import lax
from jax.sharding import PartitionSpec as P

neg_large = -1e30
block_len = 512


def ancestry(parents):
    node_count = parents.shape[1]
    positions = jnp.arange(node_count, dtype=jnp.int32)
    step_up = (parents[:, :, None] == positions[None, None, :]) & (positions[None, :, None] > 0)
    closure = (
        jnp.where(step_up, 1.0, 0.0).astype(jnp.float32)
        + jnp.eye(node_count, dtype=jnp.float32)[None]
    )
    for repeat in range(max(1, (node_count - 1).bit_length())):
        closure = jnp.minimum(
            closure + jnp.einsum("rij,rjk->rik", closure, closure, precision=lax.Precision.HIGHEST),
            1.0,
        )
    return closure > 0.5


def absorb(softmax_state, grouped, keys_vals, valid):
    running_max, denominator, weighted = softmax_state
    head_size = grouped.shape[-1]
    scores = jnp.einsum(
        "rthd,rnd->rthn", grouped, keys_vals[..., :head_size], preferred_element_type=jnp.float32
    ) * head_size ** (-0.5)
    if valid is not None:
        scores = jnp.where(valid[:, :, None, :], scores, neg_large)
    new_max = jnp.maximum(running_max, jnp.max(scores, axis=-1))
    weights = jnp.exp(scores - new_max[..., None])
    if valid is not None:
        weights = jnp.where(valid[:, :, None, :], weights, 0.0)
    factor = jnp.exp(running_max - new_max)
    denominator = denominator * factor + jnp.sum(weights, axis=-1)
    weighted = weighted * factor[..., None] + jnp.einsum(
        "rthn,rnd->rthd",
        weights.astype(jnp.bfloat16),
        keys_vals[..., head_size:],
        preferred_element_type=jnp.float32,
    )
    return (new_max, denominator, weighted)


def absorb_prompt(softmax_state, grouped, shard_kv, group_ids):
    length = shard_kv.shape[1]
    block_size = block_len if length % block_len == 0 else length
    block_count = length // block_size
    if block_count == 1:
        return absorb(softmax_state, grouped, jnp.take(shard_kv, group_ids, axis=0), None)

    def one_block(running, number):
        block_kv = lax.dynamic_slice_in_dim(shard_kv, number * block_size, block_size, 1)
        chosen = jnp.take(block_kv, group_ids, axis=0)
        return (absorb(running, grouped, chosen, None), None)

    softmax_state, unused = lax.scan(
        one_block, softmax_state, jnp.arange(block_count, dtype=jnp.int32)
    )
    return softmax_state


def local(
    queries, tree_kv, suffix_kv, suffix_len, group_ids, parents, accepted, prompt_kv, out_weight
):
    requests, node_count = parents.shape
    pair_width = tree_kv.shape[1]
    head_size = pair_width // 2
    head_count = queries.shape[1] // head_size
    grouped = queries.reshape(requests, node_count, head_count, head_size)
    own_keys = tree_kv.reshape(requests, node_count, pair_width)
    start_state = (
        jnp.full((requests, node_count, head_count), neg_large, jnp.float32),
        jnp.zeros((requests, node_count, head_count), jnp.float32),
        jnp.zeros((requests, node_count, head_count, head_size), jnp.float32),
    )
    softmax_state = absorb(start_state, grouped, own_keys, ancestry(parents))
    slot_count = suffix_kv.shape[1]
    used_slots = jnp.arange(slot_count, dtype=jnp.int32)[None, None, :] < suffix_len[:, None, None]
    softmax_state = absorb(softmax_state, grouped, suffix_kv, used_slots)
    softmax_state = absorb_prompt(
        softmax_state, grouped, lax.all_gather(prompt_kv, "req", axis=1, tiled=True), group_ids
    )
    running_max, denominator, weighted = softmax_state
    attended = (
        (weighted / denominator[..., None])
        .astype(jnp.bfloat16)
        .reshape(requests * node_count, head_count * head_size)
    )
    layer_output = lax.psum_scatter(
        jnp.dot(attended, out_weight, preferred_element_type=jnp.float32).astype(jnp.bfloat16),
        "tp",
        scatter_dimension=0,
        tiled=True,
    )
    path_cache = jnp.take_along_axis(own_keys, accepted[:, :, None], axis=1)
    return (layer_output, path_cache)


def solution(mesh):
    return jax.shard_map(
        local,
        mesh=mesh,
        in_specs=(
            P("req", "tp"),
            P("req", None),
            P("req", None, None),
            P("req"),
            P("req"),
            P("req", None),
            P("req", None),
            P(None, "req", None),
            P("tp", None),
        ),
        out_specs=(P(("req", "tp"), None), P("req", None, None)),
        check_vma=False,
    )
```

profile of v0, /device:TPU:0, one launch (start us, length us, event | category | flops | bytes accessed | tf_op | source)
XLA Modules:
  0.0 90.0 jit_solution(9328010878352869709)
XLA Ops:
  7.2 0.0 copy-start
  7.2 0.0 reduce-scatter.2.cloned.1.call-start
  7.3 0.8 compare_select_fusion.1
  8.0 0.7 compare_and_fusion.1
  8.7 0.0 copy-start.3
  8.7 1.2 %fusion.10 = f32[6,64,64]{2,1,0:T(8,128)S(1)} fusion(f32[64,64]{1,0:T(8,128)S(1)} %fusion.47, s32[6,64]{1,0:T(8,128)} %param.14, pred[64]{0:T(512)(128)(4,1)S(1)} %iota_compare_fusion.3), kind=kOutput, calls=%fused_computation.28 | convolution fusion | flops 19021824 | bytes 116288 | tf_op jit(solution)/shard_map/rij,rjk->rik/dot_general | solution.py:20
  10.0 0.3 fusion.11
  10.3 0.0 copy-start.7
  10.3 0.0 copy-start.5
  10.3 0.3 fusion.12
  10.6 0.3 fusion.13
  11.0 0.3 fusion.14
  11.3 0.3 fusion.16
  11.6 0.7 copy.16
  12.4 0.0 copy-done.3
  12.4 0.1 reshape.110
  12.5 0.0 copy-done.7
  12.5 0.1 iota_compare_fusion.2
  12.6 0.0 copy-done.5
  12.6 32.5 %all_gather.3 = bf16[2,256,256]{2,1,0:T(8,128)(2,1)S(1)} all-gather(bf16[2,32,256]{2,1,0:T(8,128)(2,1)S(1)} %copy-done.5), channel_id=1, replica_groups=mesh['req'=8,'tp'=4] {'req'}, dimensions={1}, use_global_device_ids=true | all-gather | bytes 294912 | tf_op jit(solution)/shard_map/all_gather | solution.py:86
  45.1 0.6 gather_fusion
  45.7 0.1 broadcast_select_fusion
  45.8 0.0 copy-start.1
  45.9 0.0 copy-start.2
  45.9 0.0 copy-start.4
  45.9 0.5 bitcast_reduce_fusion
  46.4 0.3 copy-done.1
  46.6 0.2 copy-done.2
  46.8 0.5 fusion.56
  47.3 0.0 copy-done.4
  47.3 0.5 fusion.55
  47.8 0.2 fusion.23
  48.1 1.0 %fusion.1 = (f32[6,64,4]{1,2,0:T(4,128)S(1)}, f32[6,64,4]{1,2,0:T(4,128)S(1)}) fusion(f32[6,256,64,4]{1,2,3,0:T(8,128)S(1)} %get-tuple-element.10, f32[6,64,4]{1,2,0:T(4,128)S(1)} %get-tuple-element.5, f32[6,64,4,256]{3,1,2,0:T(8,128)S(1)} %get-tuple-element.12, f32[6,64,4]{1,2,0:T(4,128)S(1)} %get-tuple-element.6, pred[6,256]{1,0:T(8,128)(4,1)S(1)} %iota_compare_fusion.2), kind=kLoop, calls=%fused_computation.9 | loop fusion | flops 1963008 | bytes 3171840 | tf_op jit(solution)/shard_map/reduce_sum | solution.py:39
  49.0 0.9 fusion.5
  49.9 0.9 %fusion.4 = f32[6,64,4,128]{3,1,2,0:T(8,128)S(1)} fusion(f32[6,64,4,128]{3,1,2,0:T(8,128)S(1)} %fusion.5, f32[6,64,4,256]{3,1,2,0:T(8,128)S(1)} %get-tuple-element.12, f32[6,64,4]{1,2,0:T(4,128)S(1)} %get-tuple-element.6, pred[6,256]{1,0:T(8,128)(4,1)S(1)} %iota_compare_fusion.2, f32[6,64,4]{1,2,0:T(4,128)S(1)} %get-tuple-element.3, ...), kind=kOutput, calls=%fused_computation.14 | convolution fusion | flops 102236160 | bytes 3565568 | tf_op jit(solution)/shard_map/rthn,rnd->rthd/dot_general | solution.py:40
  50.8 0.5 fusion.9
  51.4 0.3 copy.21
  51.7 0.0 copy-done
  51.7 2.2 %convolution_convert_fusion = bf16[384,2048]{1,0:T(8,128)(2,1)} fusion(bf16[512,2048]{1,0:T(8,128)(2,1)S(1)} %copy-done, bf16[48,8,4,128]{3,2,1,0:T(4,128)(2,1)S(1)} %bitcast.72), kind=kOutput, calls=%fused_computation.2 | convolution fusion | flops 806092800 | bytes 4063232 | tf_op jit(solution)/shard_map/dot_general | solution.py:95
  53.8 0.0 copy-start.6
  53.8 0.0 reduce-scatter.2.cloned.1.call-update
  53.9 0.7 copy-done.6
  54.5 0.1 reshape.121
  54.6 1.0 %gather_fusion.1 = bf16[48,256]{1,0:T(8,128)(2,1)S(1)} fusion(bf16[6,64,256]{2,1,0:T(8,128)(2,1)S(1)} %bitcast.71, s32[48]{0:T(128)S(1)} %reshape.121), kind=kCustom, calls=%fused_computation.1 | custom fusion | bytes 49536 | tf_op jit(solution)/shard_map/jit(take_along_axis)/gather | solution.py:100
  55.6 0.7 bitcast_select_fusion
  56.3 26.9 %reduce-scatter.2.cloned.1.call-done = bf16[96,2048]{1,0:T(8,128)(2,1)} async-done(((bf16[384,2048]{1,0:T(8,128)(2,1)}), bf16[96,2048]{1,0:T(8,128)(2,1)}) %reduce-scatter.2.cloned.1.call-update) | async-done | bytes 393232 | tf_op jit(solution)/shard_map/reduce_scatter | solution.py:94
  (7 shorter events, 0.1 us)
Async XLA Ops:
  7.2 44.5 %copy-start = (bf16[512,2048]{1,0:T(8,128)(2,1)S(1)}, bf16[512,2048]{1,0:T(8,128)(2,1)}, u32[]{:S(2)}) copy-start(bf16[512,2048]{1,0:T(8,128)(2,1)} %param.17) | copy-start | bytes 6291460
  7.2 76.0 %reduce-scatter.2.cloned.1.call-start = ((), (), s32[]{:S(2)}) async-start(), calls=%async_computation.1 | async-start | bytes 1966080 | tf_op jit(solution)/shard_map/reduce_scatter | solution.py:94
  8.7 3.7 %copy-start.3 = (bf16[384,512]{1,0:T(8,128)(2,1)S(1)}, bf16[384,512]{1,0:T(8,128)(2,1)}, u32[]{:S(2)}) copy-start(bf16[384,512]{1,0:T(8,128)(2,1)} %param.9) | copy-start | bytes 1179652
  10.3 2.2 %copy-start.7 = (s32[6]{0:T(128)S(1)}, s32[6]{0:T(128)}, u32[]{:S(2)}) copy-start(s32[6]{0:T(128)} %param.12) | copy-start | bytes 76
  10.3 2.3 %copy-start.5 = (bf16[2,32,256]{2,1,0:T(8,128)(2,1)S(1)}, bf16[2,32,256]{2,1,0:T(8,128)(2,1)}, u32[]{:S(2)}) copy-start(bf16[2,32,256]{2,1,0:T(8,128)(2,1)} %param.16) | copy-start | bytes 98308
  45.8 0.8 copy-start.1
  45.9 0.9 %copy-start.2 = (bf16[384,256]{1,0:T(8,128)(2,1)S(1)}, bf16[384,256]{1,0:T(8,128)(2,1)}, u32[]{:S(2)}) copy-start(bf16[384,256]{1,0:T(8,128)(2,1)} %param.10) | copy-start | bytes 589828
  45.9 1.5 %copy-start.4 = (bf16[6,256,256]{2,1,0:T(8,128)(2,1)S(1)}, bf16[6,256,256]{2,1,0:T(8,128)(2,1)}, u32[]{:S(2)}) copy-start(bf16[6,256,256]{2,1,0:T(8,128)(2,1)} %param.11) | copy-start | bytes 2359300
  53.8 0.7 copy-start.6
Sparse Core Ops, SparseCore 0:
  54.0 29.1 reduce-scatter.1
where the time goes:
time: 90.3 us; the launch traced here: 90 us
  blocking collectives  32.5 us (36%)
  waiting for transfers between devices  26.9 us (30%)
  between operations  14.2 us (16%)
  matrix products  8.77 us (10%)
  local copies, waits for them, and re-layouts  3.99 us (4%)
  other arithmetic  3.61 us (4%)
    all_gather x1, blocking collectives, local(): lax.all_gather(prompt_kv, 'req', axis=1, tiled=True)  32.5 us
    reduce_scatter x1, waiting for transfers between devices, local(): lax.psum_scatter(jnp.dot(attended, out_weight, preferred_element_type=jnp...  26.9 us
    dot_general x6, matrix products, ancestry(): jnp.einsum('rij,rjk->rik', closure, closure, precision=lax.Precision.HIGH...  2.86 us
    dot_general x3, matrix products, absorb(): jnp.einsum('rthn,rnd->rthd', weights.astype(jnp.bfloat16), keys_vals[...,...  2.3 us
    dot_general x1, matrix products, local(): jnp.dot(attended, out_weight, preferred_element_type=jnp.float32)  2.15 us
  transfers between devices with their start and end apart: 1, of which 1 were waited for; matrix products, arithmetic and copies ran while one was open for 2% of the time, Pallas kernels for 0%

commit v1 on v0

v1 whole, which is shorter than its diff:
```python
import functools
import math

import jax
import jax.numpy as jnp
from jax import lax
from jax.experimental import pallas as pl
from jax.experimental.pallas import tpu as pltpu
from jax.sharding import PartitionSpec as P

neg_large = -1e30
vmem_bytes = 40 * 1024 * 1024


def split_gather(shard, req_count, tp_count):
    if req_count != 8 or tp_count % 2:
        return [lax.all_gather(shard, "req", axis=1, tiled=True)[None]]
    masks = ((7, 6, 1), (5, 4, 3, 2))
    arrived = []
    for step in range(4):
        pairs = []
        for r in range(req_count):
            for t in range(tp_count):
                mine = masks[t % 2]
                if step < len(mine):
                    pairs.append((r * tp_count + t, (r ^ mine[step]) * tp_count + t))
        arrived.append(lax.ppermute(shard, ("req", "tp"), pairs))
    swapped = [swap_in_pair(piece, tp_count) for piece in arrived]
    last = arrived[3] + swapped[3]
    return [shard[None], *(piece[None] for piece in arrived[:3]), *(piece[None] for piece in swapped[:3]), last[None]]


def swap_in_pair(array, tp_count):
    return lax.ppermute(array, "tp", [(t, t ^ 1) for t in range(tp_count)])


def trees_kernel(parents_ref, accepted_ref, tree_ref, bias_ref, path_ref):
    requests, node_count = parents_ref.shape
    path_length = accepted_ref.shape[1]
    above = lax.broadcasted_iota(jnp.int32, (node_count, node_count), 0)
    below = lax.broadcasted_iota(jnp.int32, (node_count, node_count), 1)
    node = lax.broadcasted_iota(jnp.int32, (node_count, path_length), 0)
    closures = []
    for r in range(requests):
        parent = jnp.broadcast_to(parents_ref[r : r + 1, :], (node_count, node_count))
        step = ((parent == above) & (below > 0)) | (above == below)
        closures.append(jnp.where(step, 1.0, 0.0).astype(jnp.bfloat16))
    for repeat in range(max(1, (node_count - 1).bit_length())):
        closures = [jnp.dot(c, c, preferred_element_type=jnp.float32) for c in closures]
        closures = [jnp.where(c > 0.5, 1.0, 0.0).astype(jnp.bfloat16) for c in closures]
    for r in range(requests):
        related = closures[r].astype(jnp.float32).T
        rows = slice(r * node_count, (r + 1) * node_count)
        bias_ref[rows, :] = jnp.where(related > 0.5, 0.0, neg_large)
        chosen = jnp.broadcast_to(accepted_ref[r : r + 1, :], (node_count, path_length)) == node
        path_ref[r] = lax.dot_general(
            jnp.where(chosen, 1.0, 0.0).astype(jnp.bfloat16),
            tree_ref[rows, :],
            (((0,), (0,)), ((), ())),
            preferred_element_type=jnp.float32,
        ).astype(jnp.bfloat16)


def trees(parents, accepted, tree_kv):
    requests, node_count = parents.shape
    return pl.pallas_call(
        trees_kernel,
        out_shape=(
            jax.ShapeDtypeStruct((requests * node_count, node_count), jnp.float32),
            jax.ShapeDtypeStruct((requests, accepted.shape[1], tree_kv.shape[1]), jnp.bfloat16),
        ),
        name="trees",
        cost_estimate=pl.CostEstimate(flops=4_000_000_000, bytes_accessed=400_000, transcendentals=0),
    )(parents, accepted, tree_kv)


def chunk_kernel(unit, piece_count, place_ref, length_ref, group_ref, own_ref, other_ref, bias_ref, tree_ref, suffix_ref, *rest):
    pieces, (weight_own_ref, weight_other_ref, out_ref, attended_ref) = rest[:piece_count], rest[piece_count:]
    node_count = bias_ref.shape[1]
    head_size = tree_ref.shape[1] // 2
    heads = own_ref.shape[1] // head_size
    slot_count = suffix_ref.shape[1]
    rate = head_size**-0.5 * math.log2(math.e)
    slot = lax.broadcasted_iota(jnp.int32, (1, slot_count), 1)

    def against(query, keys):
        return lax.dot_general(query, keys, (((1,), (1,)), ((), ())), preferred_element_type=jnp.float32)

    def summed(weights, values):
        return jnp.dot(weights.astype(jnp.bfloat16), values, preferred_element_type=jnp.float32)

    for number in range(out_ref.shape[0] // unit):
        row = pl.multiple_of(place_ref[0] + number * unit, unit)
        request = row // node_count
        query = jnp.concatenate(
            [ref[pl.ds(row, unit), h * head_size : (h + 1) * head_size] for ref in (own_ref, other_ref) for h in range(heads)], axis=0
        )
        tree = tree_ref[pl.ds(pl.multiple_of(request * node_count, node_count), node_count), :]
        suffix = suffix_ref[request]
        group = group_ref[request]
        prompts = [ref[k, group] for ref in pieces for k in range(ref.shape[0])]
        bias = jnp.concatenate([bias_ref[pl.ds(row, unit), :]] * (2 * heads), axis=0)
        blocks = [(against(query, tree[:, :head_size]) + bias, tree[:, head_size:])]
        used = jnp.where(slot < length_ref[request], 0.0, neg_large)
        blocks.append((against(query, suffix[:, :head_size]) + used, suffix[:, head_size:]))
        prompt = prompts[0] if len(prompts) == 1 else jnp.concatenate(prompts, axis=0)
        blocks.append((against(query, prompt[:, :head_size]), prompt[:, head_size:]))
        largest = functools.reduce(jnp.maximum, [jnp.max(s, axis=1, keepdims=True) for s, _ in blocks])
        total, result = 0.0, 0.0
        for score, values in blocks:
            weight = jnp.exp2((score - largest) * rate)
            total = total + jnp.sum(weight, axis=1, keepdims=True)
            result = result + summed(weight, values)
        attended = (result / total).astype(jnp.bfloat16)
        for h in range(2 * heads):
            attended_ref[number * unit : (number + 1) * unit, h * head_size : (h + 1) * head_size] = attended[h * unit : (h + 1) * unit]
    width = heads * head_size
    columns = 512 if out_ref.shape[1] % 512 == 0 else out_ref.shape[1]
    for c in range(0, out_ref.shape[1], columns):
        product = jnp.dot(attended_ref[:, :width], weight_own_ref[:, c : c + columns], preferred_element_type=jnp.float32) + jnp.dot(
            attended_ref[:, width:], weight_other_ref[:, c : c + columns], preferred_element_type=jnp.float32
        )
        out_ref[:, c : c + columns] = product.astype(out_ref.dtype)


def chunk(place, dtype, chunk_rows, lengths, groups, own, other, bias, tree_kv, suffix_kv, pieces, weight_own, weight_other, name):
    unit = math.gcd(chunk_rows, bias.shape[1])
    in_smem = pl.BlockSpec(memory_space=pltpu.SMEM)
    in_vmem = pl.BlockSpec(memory_space=pltpu.VMEM)
    return pl.pallas_call(
        functools.partial(chunk_kernel, unit, len(pieces)),
        in_specs=[in_smem] * 3 + [in_vmem] * (7 + len(pieces)),
        out_specs=in_vmem,
        out_shape=jax.ShapeDtypeStruct((chunk_rows, weight_own.shape[1]), dtype),
        scratch_shapes=[pltpu.VMEM((chunk_rows, 2 * own.shape[1]), jnp.bfloat16)],
        compiler_params=pltpu.CompilerParams(vmem_limit_bytes=vmem_bytes),
        name=name,
        cost_estimate=pl.CostEstimate(flops=4_000_000_000, bytes_accessed=6_000_000, transcendentals=0),
    )(place, lengths, groups, own, other, bias, tree_kv, suffix_kv, *pieces, weight_own, weight_other)


def local(req_count, tp_count, queries, tree_kv, suffix_kv, suffix_len, group_ids, parents, accepted, prompt_kv, out_weight):
    pieces = split_gather(prompt_kv, req_count, tp_count)
    other_queries = swap_in_pair(queries, tp_count)
    other_weight = swap_in_pair(out_weight, tp_count)
    bias, path_cache = trees(parents, accepted, tree_kv)
    chunk_rows = queries.shape[0] // tp_count
    me = lax.axis_index("tp")
    places = [jnp.reshape(t * chunk_rows, (1,)).astype(jnp.int32) for t in (me ^ 2, me)]
    common = (suffix_len, group_ids, queries, other_queries, bias, tree_kv, suffix_kv, pieces, out_weight, other_weight)
    far = chunk(places[0], jnp.bfloat16, chunk_rows, *common, "far_chunk")
    arrived = lax.ppermute(far, "tp", [(t, t ^ 2) for t in range(tp_count)])
    near = chunk(places[1], jnp.float32, chunk_rows, *common, "near_chunk")
    layer_output = (near + arrived.astype(jnp.float32)).astype(jnp.bfloat16)
    return (layer_output, path_cache)


def solution(mesh):
    return jax.shard_map(
        functools.partial(local, mesh.shape["req"], mesh.shape["tp"]),
        mesh=mesh,
        in_specs=(
            P("req", "tp"),
            P("req", None),
            P("req", None, None),
            P("req"),
            P("req"),
            P("req", None),
            P("req", None),
            P(None, "req", None),
            P("tp", None),
        ),
        out_specs=(P(("req", "tp"), None), P("req", None, None)),
        check_vma=False,
    )
```

time: 90.3 us -> 35.2 us (0.39)
  blocking collectives: 32.5 us -> 0 us
  waiting for transfers between devices: 26.9 us -> 4.78 us
  between operations: 14.2 us -> 0.79 us
  starting transfers between devices: 0.04 us -> 11.3 us
  Pallas kernels: 0 us -> 11 us
  matrix products: 8.77 us -> 0 us
  other arithmetic: 3.61 us -> 2.62 us
    all_gather x1 -> x0, blocking collectives: 32.5 us -> none  [local(): lax.all_gather(prompt_kv, 'req', axis=1, tiled=True)]
    reduce_scatter x1 -> x0, waiting for transfers between devices: 26.9 us -> none  [local(): lax.psum_scatter(jnp.dot(attended, out_weight, preferred_element_type=jnp...]
    ppermute x0 -> x11, starting transfers between devices: none -> 11.3 us  [the longest x4 7.01 us: split_gather(): arrived.append(lax.ppermute(shard, ('req', 'tp'), pairs))]
    pallas_call x0 -> x3, Pallas kernels: none -> 11 us  [the longest x2 8.37 us: chunk(): pl.pallas_call(functools.partial(chunk_kernel, unit, len(pieces)), in_spe...]
    dot_general x13 -> x0, matrix products: 8.77 us -> none  [the longest x6 2.86 us: ancestry(): jnp.einsum('rij,rjk->rik', closure, closure, precision=lax.Precision.HIGH...]
    ppermute x0 -> x11, waiting for transfers between devices: none -> 4.78 us  [the longest x1 2.99 us: local(): arrived = lax.ppermute(far, 'tp', [(t, t ^ 2) for t in range(tp_count)])]
    unnamed x16 -> x32, local copies, waits for them, and re-layouts: 1.15 us -> 4.16 us
    convert_element_type x1, other arithmetic: 0.01 us -> 1.84 us  [local(): layer_output = (near + arrived.astype(jnp.float32)).astype(jnp.bfloat16)]
  transfers between devices with their start and end apart: 1 -> 11, of which waited for: 1 -> 4; matrix products, arithmetic and copies ran while one was open for 2% -> 2% of each run, Pallas kernels for 0% -> 18%
where the time goes in v1:
time: 35.2 us; the launch traced here: 34.7 us
  starting transfers between devices  11.3 us (32%)
  Pallas kernels  11 us (31%)
  waiting for transfers between devices  4.78 us (14%)
  local copies, waits for them, and re-layouts  4.16 us (12%)
  other arithmetic  2.62 us (7%)
  between operations  0.79 us (2%)
    pallas_call x2, Pallas kernels, chunk(): pl.pallas_call(functools.partial(chunk_kernel, unit, len(pieces)), in_spe...  8.37 us
    ppermute x4, starting transfers between devices, split_gather(): arrived.append(lax.ppermute(shard, ('req', 'tp'), pairs))  7.01 us
    unnamed x32, local copies, waits for them, and re-layouts  4.16 us
    ppermute x1, waiting for transfers between devices, local(): arrived = lax.ppermute(far, 'tp', [(t, t ^ 2) for t in range(tp_count)])  2.99 us
    ppermute x6, starting transfers between devices, swap_in_pair(): return lax.ppermute(array, 'tp', [(t, t ^ 1) for t in range(tp_count)])  2.78 us
    pallas_call x1, Pallas kernels, trees(): pl.pallas_call(trees_kernel, out_shape=(jax.ShapeDtypeStruct((requests *...  2.58 us
    convert_element_type x1, other arithmetic, local(): layer_output = (near + arrived.astype(jnp.float32)).astype(jnp.bfloat16)  1.84 us
    ppermute x1, starting transfers between devices, local(): arrived = lax.ppermute(far, 'tp', [(t, t ^ 2) for t in range(tp_count)])  1.56 us
  transfers between devices with their start and end apart: 11, of which 4 were waited for; matrix products, arithmetic and copies ran while one was open for 2% of the time, Pallas kernels for 18%

profile of v1, /device:TPU:0, one launch (start us, length us, event | category | flops | bytes accessed | tf_op | source)
XLA Modules:
  0.0 34.7 jit_solution(9753804758554460326)
XLA Ops:
  0.6 0.0 copy-start
  0.6 0.0 copy-start.4
  0.7 0.0 copy-start.2
  0.7 0.0 copy-start.3
  0.7 0.0 copy-start.12
  0.7 0.0 copy-start.11
  0.7 0.0 copy-start.1
  0.7 0.5 %collective-permute-start.9 = (bf16[512,2048]{1,0:T(8,128)(2,1)}, bf16[512,2048]{1,0:T(8,128)(2,1)}, u32[]{:S(2)}, u32[]{:S(2)}) collective-permute-start(bf16[512,2048]{1,0:T(8,128)(2,1)} %rest_8_.3), channel_id=1, source_target_pairs={{0,1},{1,0},{2,3},{3,2},{4,5},{5,4},{6,7},{7,6},{8,9},{9,8},{10,11... | collective-permute-start | bytes 6291464 | tf_op jit(solution)/shard_map/ppermute | solution.py:34
  1.2 4.7 %collective-permute-start.2 = (bf16[2,32,256]{2,1,0:T(8,128)(2,1)}, bf16[2,32,256]{2,1,0:T(8,128)(2,1)}, u32[]{:S(2)}, u32[]{:S(2)}) collective-permute-start(bf16[2,32,256]{2,1,0:T(8,128)(2,1)} %param.16), channel_id=1, source_target_pairs={{0,24},{1,17},{2,26},{3,19},{4,28},{5,21},{6,30},{7,23},{8,16},{9,... | collective-permute-start | bytes 98312 | tf_op jit(solution)/shard_map/ppermute | solution.py:27
  5.9 0.7 %collective-permute-start.7 = (bf16[2,32,256]{2,1,0:T(8,128)(2,1)}, bf16[2,32,256]{2,1,0:T(8,128)(2,1)S(1)}, u32[]{:S(2)}, u32[]{:S(2)}) collective-permute-start(bf16[2,32,256]{2,1,0:T(8,128)(2,1)} %param.16), channel_id=1, source_target_pairs={{1,9},{3,11},{5,13},{7,15},{9,1},{11,3},{13,5},{15,7},{17,25},{19,... | collective-permute-start | bytes 98312 | tf_op jit(solution)/shard_map/ppermute | solution.py:27
  6.6 1.4 %collective-permute-start.1 = (bf16[2,32,256]{2,1,0:T(8,128)(2,1)}, bf16[2,32,256]{2,1,0:T(8,128)(2,1)}, u32[]{:S(2)}, u32[]{:S(2)}) collective-permute-start(bf16[2,32,256]{2,1,0:T(8,128)(2,1)} %param.16), channel_id=1, source_target_pairs={{0,28},{1,21},{2,30},{3,23},{4,24},{5,17},{6,26},{7,19},{8,20},{9,... | collective-permute-start | bytes 98312 | tf_op jit(solution)/shard_map/ppermute | solution.py:27
  7.9 0.3 collective-permute-start.3
  8.2 0.0 collective-permute-done.2
  8.2 1.3 %collective-permute-start = (bf16[384,512]{1,0:T(8,128)(2,1)}, bf16[384,512]{1,0:T(8,128)(2,1)}, u32[]{:S(2)}, u32[]{:S(2)}) collective-permute-start(bf16[384,512]{1,0:T(8,128)(2,1)} %own_ref.3), channel_id=1, source_target_pairs={{0,1},{1,0},{2,3},{3,2},{4,5},{5,4},{6,7},{7,6},{8,9},{9,8},{10,11... | collective-permute-start | bytes 1179656 | tf_op jit(solution)/shard_map/ppermute | solution.py:34
  9.5 0.0 collective-permute-done.7
  9.5 0.4 %collective-permute-start.8 = (bf16[2,32,256]{2,1,0:T(8,128)(2,1)S(1)}, bf16[2,32,256]{2,1,0:T(8,128)(2,1)}, u32[]{:S(2)}, u32[]{:S(2)}) collective-permute-start(bf16[2,32,256]{2,1,0:T(8,128)(2,1)S(1)} %collective-permute-done.7), channel_id=1, source_target_pairs={{0,1},{1,0},{2,3},{3,2},{4,5},{5,4},{6,7},{7,6},{8,9},{9,8},{10,11... | collective-permute-start | bytes 98312 | tf_op jit(solution)/shard_map/ppermute | solution.py:34
  9.9 2.6 %trees.1 = (f32[384,64]{1,0:T(8,128)}, bf16[6,8,256]{2,1,0:T(8,128)(2,1)}) custom-call(s32[6,64]{1,0:T(8,128)} %parents_ref.1, s32[6,8]{1,0:T(8,128)} %accepted_ref.1, bf16[384,256]{1,0:T(8,128)(2,1)} %tree_ref.5), custom_call_target="tpu_custom_call" | custom-call | flops 4000000000 | bytes 400000 | tf_op jit(solution)/shard_map/trees/pallas_call | solution.py:66
  12.5 0.0 copy-done.15
  12.5 1.3 %collective-permute-done.1 = bf16[2,32,256]{2,1,0:T(8,128)(2,1)} collective-permute-done((bf16[2,32,256]{2,1,0:T(8,128)(2,1)}, bf16[2,32,256]{2,1,0:T(8,128)(2,1)}, u32[]{:S(2)}, u32[]{:S(2)}) %collective-permute-start.1) | collective-permute-done | bytes 32800 | tf_op jit(solution)/shard_map/ppermute | solution.py:27
  13.7 0.1 collective-permute-start.5
  13.9 0.0 collective-permute-done.3
  13.9 0.4 %collective-permute-start.4 = (bf16[2,32,256]{2,1,0:T(8,128)(2,1)}, bf16[2,32,256]{2,1,0:T(8,128)(2,1)S(1)}, u32[]{:S(2)}, u32[]{:S(2)}) collective-permute-start(bf16[2,32,256]{2,1,0:T(8,128)(2,1)} %collective-permute-done.1), channel_id=1, source_target_pairs={{0,1},{1,0},{2,3},{3,2},{4,5},{5,4},{6,7},{7,6},{8,9},{9,8},{10,11... | collective-permute-start | bytes 98312 | tf_op jit(solution)/shard_map/ppermute | solution.py:34
  14.3 0.0 collective-permute-done.8
  14.3 0.1 collective-permute-start.6
  14.4 0.8 %add_bitcast_fusion.rest_7_ = bf16[1,2,32,256]{3,2,1,0:T(8,128)(2,1)S(1)} fusion(bf16[2,32,256]{2,1,0:T(8,128)(2,1)} %copy-done.15, bf16[2,32,256]{2,1,0:T(8,128)(2,1)} %collective-permute-done.8), kind=kLoop, calls=%fused_computation.1 | loop fusion | flops 16384 | bytes 98304 | tf_op jit(solution)/shard_map/broadcast_in_dim | solution.py:30
  15.2 0.0 collective-permute-done.5
  15.2 0.2 collective-permute-done.4
  15.3 0.3 %collective-permute-done.6 = bf16[2,32,256]{2,1,0:T(8,128)(2,1)S(1)} collective-permute-done((bf16[2,32,256]{2,1,0:T(8,128)(2,1)}, bf16[2,32,256]{2,1,0:T(8,128)(2,1)S(1)}, u32[]{:S(2)}, u32[]{:S(2)}) %collective-permute-start.6) | collective-permute-done | bytes 32800 | tf_op jit(solution)/shard_map/ppermute | solution.py:34
  15.7 0.0 collective-permute-done.other_ref
  15.7 0.0 collective-permute-done.9.rest_9_
  15.7 0.0 copy-done
  15.7 0.0 copy-done.4
  15.7 0.0 copy-done.2
  15.7 0.0 copy-done.3
  15.7 0.0 copy-done.12
  15.7 0.0 copy-done.11
  15.7 0.0 copy-done.1
  15.8 0.9 %copy-done.13 = f32[384,64]{1,0:T(8,128)S(1)} copy-done((f32[384,64]{1,0:T(8,128)S(1)}, f32[384,64]{1,0:T(8,128)}, u32[]{:S(2)}) %copy-start.13) | copy-done | bytes 98328
  16.7 4.6 %far_chunk.1 = bf16[96,2048]{1,0:T(8,128)(2,1)} custom-call(s32[1]{0:T(128)} %bitcast.9.place_ref, s32[6]{0:T(128)S(1)} %copy-done.11, s32[6]{0:T(128)S(1)} %copy-done.12, bf16[384,512]{1,0:T(8,128)(2,1)S(1)} %copy-done.2, bf16[384,512]{1,0:T(8,128)(2,1)} %collective-permute-done.other_ref, f32[384,64]{1,0:T(8,128)S(1)} %copy-done.13, ...), custom_call_target="tpu_custom_call" | custom-call | flops 4000000000 | bytes 6000000 | tf_op jit(solution)/shard_map/far_chunk/pallas_call | solution.py:130
  21.3 0.0 copy-done.7
  21.3 1.6 %collective-permute-start.10 = (bf16[96,2048]{1,0:T(8,128)(2,1)}, bf16[96,2048]{1,0:T(8,128)(2,1)}, u32[]{:S(2)}, u32[]{:S(2)}) collective-permute-start(bf16[96,2048]{1,0:T(8,128)(2,1)} %far_chunk.1), channel_id=1, source_target_pairs={{0,2},{1,3},{2,0},{3,1},{4,6},{5,7},{6,4},{7,5},{8,10},{9,11},{10,... | collective-permute-start | bytes 1179656 | tf_op jit(solution)/shard_map/ppermute | solution.py:152
  22.8 0.8 %copy-done.6 = bf16[2,32,256]{2,1,0:T(8,128)(2,1)S(1)} copy-done((bf16[2,32,256]{2,1,0:T(8,128)(2,1)S(1)}, bf16[2,32,256]{2,1,0:T(8,128)(2,1)}, u32[]{:S(2)}) %copy-start.6) | copy-done | bytes 32792
  23.6 0.8 %copy-done.8 = bf16[2,32,256]{2,1,0:T(8,128)(2,1)S(1)} copy-done((bf16[2,32,256]{2,1,0:T(8,128)(2,1)S(1)}, bf16[2,32,256]{2,1,0:T(8,128)(2,1)}, u32[]{:S(2)}) %copy-start.8) | copy-done | bytes 32792
  24.3 0.8 %copy-done.10 = bf16[2,32,256]{2,1,0:T(8,128)(2,1)S(1)} copy-done((bf16[2,32,256]{2,1,0:T(8,128)(2,1)S(1)}, bf16[2,32,256]{2,1,0:T(8,128)(2,1)}, u32[]{:S(2)}) %copy-start.10) | copy-done | bytes 32792
  25.1 0.9 %copy-done.14 = f32[384,64]{1,0:T(8,128)S(1)} copy-done((f32[384,64]{1,0:T(8,128)S(1)}, f32[384,64]{1,0:T(8,128)}, u32[]{:S(2)}) %copy-start.14) | copy-done | bytes 98328
  26.0 3.8 %near_chunk.1 = f32[96,2048]{1,0:T(8,128)S(1)} custom-call(s32[1]{0:T(128)} %bitcast.place_ref, s32[6]{0:T(128)S(1)} %copy-done.11, s32[6]{0:T(128)S(1)} %copy-done.12, bf16[384,512]{1,0:T(8,128)(2,1)S(1)} %copy-done.2, bf16[384,512]{1,0:T(8,128)(2,1)} %collective-permute-done.other_ref, f32[384,64]{1,0:T(8,128)S(1)} %copy-done.14, ...), custom_call_target="tpu_custom_call" | custom-call | flops 4000000000 | bytes 6000000 | tf_op jit(solution)/shard_map/near_chunk/pallas_call | solution.py:130
  29.8 3.0 %collective-permute-done.10 = bf16[96,2048]{1,0:T(8,128)(2,1)} collective-permute-done((bf16[96,2048]{1,0:T(8,128)(2,1)}, bf16[96,2048]{1,0:T(8,128)(2,1)}, u32[]{:S(2)}, u32[]{:S(2)}) %collective-permute-start.10) | collective-permute-done | bytes 393248 | tf_op jit(solution)/shard_map/ppermute | solution.py:152
  32.8 1.8 %add_convert_fusion = bf16[96,2048]{1,0:T(8,128)(2,1)} fusion(f32[96,2048]{1,0:T(8,128)S(1)} %near_chunk.1, bf16[96,2048]{1,0:T(8,128)(2,1)} %collective-permute-done.10), kind=kLoop, calls=%fused_computation | loop fusion | flops 589824 | bytes 1572864 | tf_op jit(solution)/shard_map/convert_element_type | solution.py:154
  (11 shorter events, 0.0 us)
Async XLA Ops:
  0.6 15.1 %copy-start = (bf16[512,2048]{1,0:T(8,128)(2,1)S(1)}, bf16[512,2048]{1,0:T(8,128)(2,1)}, u32[]{:S(2)}) copy-start(bf16[512,2048]{1,0:T(8,128)(2,1)} %rest_8_.3) | copy-start | bytes 6291460
  0.6 15.1 %copy-start.4 = (bf16[2,32,256]{2,1,0:T(8,128)(2,1)S(1)}, bf16[2,32,256]{2,1,0:T(8,128)(2,1)}, u32[]{:S(2)}) copy-start(bf16[2,32,256]{2,1,0:T(8,128)(2,1)} %param.16) | copy-start | bytes 98308
  0.7 15.1 %copy-start.2 = (bf16[384,512]{1,0:T(8,128)(2,1)S(1)}, bf16[384,512]{1,0:T(8,128)(2,1)}, u32[]{:S(2)}) copy-start(bf16[384,512]{1,0:T(8,128)(2,1)} %own_ref.3) | copy-start | bytes 1179652
  0.7 15.1 %copy-start.3 = (bf16[384,256]{1,0:T(8,128)(2,1)S(1)}, bf16[384,256]{1,0:T(8,128)(2,1)}, u32[]{:S(2)}) copy-start(bf16[384,256]{1,0:T(8,128)(2,1)} %tree_ref.5) | copy-start | bytes 589828
  0.7 15.1 %copy-start.12 = (s32[6]{0:T(128)S(1)}, s32[6]{0:T(128)}, u32[]{:S(2)}) copy-start(s32[6]{0:T(128)} %group_ref.3) | copy-start | bytes 76
  0.7 15.1 %copy-start.11 = (s32[6]{0:T(128)S(1)}, s32[6]{0:T(128)}, u32[]{:S(2)}) copy-start(s32[6]{0:T(128)} %length_ref.3) | copy-start | bytes 76
  0.7 15.1 %copy-start.1 = (bf16[6,256,256]{2,1,0:T(8,128)(2,1)S(1)}, bf16[6,256,256]{2,1,0:T(8,128)(2,1)}, u32[]{:S(2)}) copy-start(bf16[6,256,256]{2,1,0:T(8,128)(2,1)} %suffix_ref.3) | copy-start | bytes 2359300
  0.7 15.0 %collective-permute-start.9 = (bf16[512,2048]{1,0:T(8,128)(2,1)}, bf16[512,2048]{1,0:T(8,128)(2,1)}, u32[]{:S(2)}, u32[]{:S(2)}) collective-permute-start(bf16[512,2048]{1,0:T(8,128)(2,1)} %rest_8_.3), channel_id=1, source_target_pairs={{0,1},{1,0},{2,3},{3,2},{4,5},{5,4},{6,7},{7,6},{8,9},{9,8},{10,11... | collective-permute-start | bytes 6291464 | tf_op jit(solution)/shard_map/ppermute | solution.py:34
  1.2 7.0 %collective-permute-start.2 = (bf16[2,32,256]{2,1,0:T(8,128)(2,1)}, bf16[2,32,256]{2,1,0:T(8,128)(2,1)}, u32[]{:S(2)}, u32[]{:S(2)}) collective-permute-start(bf16[2,32,256]{2,1,0:T(8,128)(2,1)} %param.16), channel_id=1, source_target_pairs={{0,24},{1,17},{2,26},{3,19},{4,28},{5,21},{6,30},{7,23},{8,16},{9,... | collective-permute-start | bytes 98312 | tf_op jit(solution)/shard_map/ppermute | solution.py:27
  5.9 3.6 %collective-permute-start.7 = (bf16[2,32,256]{2,1,0:T(8,128)(2,1)}, bf16[2,32,256]{2,1,0:T(8,128)(2,1)S(1)}, u32[]{:S(2)}, u32[]{:S(2)}) collective-permute-start(bf16[2,32,256]{2,1,0:T(8,128)(2,1)} %param.16), channel_id=1, source_target_pairs={{1,9},{3,11},{5,13},{7,15},{9,1},{11,3},{13,5},{15,7},{17,25},{19,... | collective-permute-start | bytes 98312 | tf_op jit(solution)/shard_map/ppermute | solution.py:27
  6.6 7.2 %collective-permute-start.1 = (bf16[2,32,256]{2,1,0:T(8,128)(2,1)}, bf16[2,32,256]{2,1,0:T(8,128)(2,1)}, u32[]{:S(2)}, u32[]{:S(2)}) collective-permute-start(bf16[2,32,256]{2,1,0:T(8,128)(2,1)} %param.16), channel_id=1, source_target_pairs={{0,28},{1,21},{2,30},{3,23},{4,24},{5,17},{6,26},{7,19},{8,20},{9,... | collective-permute-start | bytes 98312 | tf_op jit(solution)/shard_map/ppermute | solution.py:27
  7.9 5.9 %collective-permute-start.3 = (bf16[2,32,256]{2,1,0:T(8,128)(2,1)}, bf16[2,32,256]{2,1,0:T(8,128)(2,1)}, u32[]{:S(2)}, u32[]{:S(2)}) collective-permute-start(bf16[2,32,256]{2,1,0:T(8,128)(2,1)} %param.16), channel_id=1, source_target_pairs={{0,4},{1,13},{2,6},{3,15},{4,0},{5,9},{6,2},{7,11},{8,12},{9,5},{1... | collective-permute-start | bytes 98312 | tf_op jit(solution)/shard_map/ppermute | solution.py:27
  8.2 7.4 %collective-permute-start = (bf16[384,512]{1,0:T(8,128)(2,1)}, bf16[384,512]{1,0:T(8,128)(2,1)}, u32[]{:S(2)}, u32[]{:S(2)}) collective-permute-start(bf16[384,512]{1,0:T(8,128)(2,1)} %own_ref.3), channel_id=1, source_target_pairs={{0,1},{1,0},{2,3},{3,2},{4,5},{5,4},{6,7},{7,6},{8,9},{9,8},{10,11... | collective-permute-start | bytes 1179656 | tf_op jit(solution)/shard_map/ppermute | solution.py:34
  9.5 3.0 %copy-start.15 = (bf16[2,32,256]{2,1,0:T(8,128)(2,1)}, bf16[2,32,256]{2,1,0:T(8,128)(2,1)S(1)}, u32[]{:S(2)}) copy-start(bf16[2,32,256]{2,1,0:T(8,128)(2,1)S(1)} %collective-permute-done.7) | copy-start | bytes 98308
  9.5 4.7 %collective-permute-start.8 = (bf16[2,32,256]{2,1,0:T(8,128)(2,1)S(1)}, bf16[2,32,256]{2,1,0:T(8,128)(2,1)}, u32[]{:S(2)}, u32[]{:S(2)}) collective-permute-start(bf16[2,32,256]{2,1,0:T(8,128)(2,1)S(1)} %collective-permute-done.7), channel_id=1, source_target_pairs={{0,1},{1,0},{2,3},{3,2},{4,5},{5,4},{6,7},{7,6},{8,9},{9,8},{10,11... | collective-permute-start | bytes 98312 | tf_op jit(solution)/shard_map/ppermute | solution.py:34
  13.7 1.4 %collective-permute-start.5 = (bf16[2,32,256]{2,1,0:T(8,128)(2,1)}, bf16[2,32,256]{2,1,0:T(8,128)(2,1)S(1)}, u32[]{:S(2)}, u32[]{:S(2)}) collective-permute-start(bf16[2,32,256]{2,1,0:T(8,128)(2,1)} %collective-permute-done.2), channel_id=1, source_target_pairs={{0,1},{1,0},{2,3},{3,2},{4,5},{5,4},{6,7},{7,6},{8,9},{9,8},{10,11... | collective-permute-start | bytes 98312 | tf_op jit(solution)/shard_map/ppermute | solution.py:34
  13.9 1.5 %collective-permute-start.4 = (bf16[2,32,256]{2,1,0:T(8,128)(2,1)}, bf16[2,32,256]{2,1,0:T(8,128)(2,1)S(1)}, u32[]{:S(2)}, u32[]{:S(2)}) collective-permute-start(bf16[2,32,256]{2,1,0:T(8,128)(2,1)} %collective-permute-done.1), channel_id=1, source_target_pairs={{0,1},{1,0},{2,3},{3,2},{4,5},{5,4},{6,7},{7,6},{8,9},{9,8},{10,11... | collective-permute-start | bytes 98312 | tf_op jit(solution)/shard_map/ppermute | solution.py:34
  14.3 1.4 %collective-permute-start.6 = (bf16[2,32,256]{2,1,0:T(8,128)(2,1)}, bf16[2,32,256]{2,1,0:T(8,128)(2,1)S(1)}, u32[]{:S(2)}, u32[]{:S(2)}) collective-permute-start(bf16[2,32,256]{2,1,0:T(8,128)(2,1)} %collective-permute-done.3), channel_id=1, source_target_pairs={{0,1},{1,0},{2,3},{3,2},{4,5},{5,4},{6,7},{7,6},{8,9},{9,8},{10,11... | collective-permute-start | bytes 98312 | tf_op jit(solution)/shard_map/ppermute | solution.py:34
  15.2 6.1 %copy-start.5 = (bf16[2,32,256]{2,1,0:T(8,128)(2,1)}, bf16[2,32,256]{2,1,0:T(8,128)(2,1)S(1)}, u32[]{:S(2)}) copy-start(bf16[2,32,256]{2,1,0:T(8,128)(2,1)S(1)} %collective-permute-done.5) | copy-start | bytes 98308
  15.3 5.9 %copy-start.7 = (bf16[2,32,256]{2,1,0:T(8,128)(2,1)}, bf16[2,32,256]{2,1,0:T(8,128)(2,1)S(1)}, u32[]{:S(2)}) copy-start(bf16[2,32,256]{2,1,0:T(8,128)(2,1)S(1)} %collective-permute-done.4) | copy-start | bytes 98308
  15.7 5.6 %copy-start.9 = (bf16[2,32,256]{2,1,0:T(8,128)(2,1)}, bf16[2,32,256]{2,1,0:T(8,128)(2,1)S(1)}, u32[]{:S(2)}) copy-start(bf16[2,32,256]{2,1,0:T(8,128)(2,1)S(1)} %collective-permute-done.6) | copy-start | bytes 98308
  15.8 0.9 %copy-start.13 = (f32[384,64]{1,0:T(8,128)S(1)}, f32[384,64]{1,0:T(8,128)}, u32[]{:S(2)}) copy-start(f32[384,64]{1,0:T(8,128)} %get-tuple-element.4.bias_ref) | copy-start | bytes 294916
  21.3 11.6 %collective-permute-start.10 = (bf16[96,2048]{1,0:T(8,128)(2,1)}, bf16[96,2048]{1,0:T(8,128)(2,1)}, u32[]{:S(2)}, u32[]{:S(2)}) collective-permute-start(bf16[96,2048]{1,0:T(8,128)(2,1)} %far_chunk.1), channel_id=1, source_target_pairs={{0,2},{1,3},{2,0},{3,1},{4,6},{5,7},{6,4},{7,5},{8,10},{9,11},{10,... | collective-permute-start | bytes 1179656 | tf_op jit(solution)/shard_map/ppermute | solution.py:152
  22.8 0.8 %copy-start.6 = (bf16[2,32,256]{2,1,0:T(8,128)(2,1)S(1)}, bf16[2,32,256]{2,1,0:T(8,128)(2,1)}, u32[]{:S(2)}) copy-start(bf16[2,32,256]{2,1,0:T(8,128)(2,1)} %copy-done.5) | copy-start | bytes 98308
  23.6 0.8 %copy-start.8 = (bf16[2,32,256]{2,1,0:T(8,128)(2,1)S(1)}, bf16[2,32,256]{2,1,0:T(8,128)(2,1)}, u32[]{:S(2)}) copy-start(bf16[2,32,256]{2,1,0:T(8,128)(2,1)} %copy-done.7) | copy-start | bytes 98308
  24.3 0.8 %copy-start.10 = (bf16[2,32,256]{2,1,0:T(8,128)(2,1)S(1)}, bf16[2,32,256]{2,1,0:T(8,128)(2,1)}, u32[]{:S(2)}) copy-start(bf16[2,32,256]{2,1,0:T(8,128)(2,1)} %copy-done.9) | copy-start | bytes 98308
  25.1 0.9 %copy-start.14 = (f32[384,64]{1,0:T(8,128)S(1)}, f32[384,64]{1,0:T(8,128)}, u32[]{:S(2)}) copy-start(f32[384,64]{1,0:T(8,128)} %get-tuple-element.4.bias_ref) | copy-start | bytes 294916

commit v2 on v1

v2 whole, which is shorter than its diff:
```python
import functools
import math

import jax
import jax.numpy as jnp
from jax import lax
from jax.experimental import pallas as pl
from jax.experimental.pallas import tpu as pltpu
from jax.sharding import PartitionSpec as P

neg_large = -1e30
vmem_bytes = 12 * 1024 * 1024


def fetch_shards(shard, req_count, tp_count):
    masks = ((7, 6, 1), (5, 4, 3, 2))
    arrived = []
    for step in range(4):
        pairs = []
        for r in range(req_count):
            for t in range(tp_count):
                mine = masks[t % 2]
                if step < len(mine):
                    pairs.append((r * tp_count + t, (r ^ mine[step]) * tp_count + t))
        arrived.append(lax.ppermute(shard, ("req", "tp"), pairs))
    return arrived


def after(array, earlier):
    return lax.optimization_barrier((array, earlier))[0]


def swap_in_pair(array, tp_count):
    return lax.ppermute(array, "tp", [(t, t ^ 1) for t in range(tp_count)])


def score(query, keys):
    return lax.dot_general(query, keys, (((1,), (1,)), ((), ())), preferred_element_type=jnp.float32)


def stacked_heads(ref, row, unit, head_size):
    return jnp.concatenate([ref[pl.ds(row, unit), h : h + head_size] for h in range(0, ref.shape[1], head_size)], axis=0)


def log2_rate(head_size):
    return head_size**-0.5 * math.log2(math.e)


def absorb(blocks, rate):
    largest = functools.reduce(jnp.maximum, [jnp.max(s, axis=1, keepdims=True) for s, _ in blocks])
    total, result = 0.0, 0.0
    for scores, values in blocks:
        weight = jnp.exp2((scores - largest) * rate)
        total = total + jnp.sum(weight, axis=1, keepdims=True)
        result = result + jnp.dot(weight.astype(jnp.bfloat16), values, preferred_element_type=jnp.float32)
    return largest, total, result


def private_blocks(query, row, unit, length, bias_ref, tree_ref, suffix):
    node_count = bias_ref.shape[1]
    head_size = tree_ref.shape[1] // 2
    request = row // node_count
    tree = tree_ref[pl.ds(pl.multiple_of(request * node_count, node_count), node_count), :]
    bias = jnp.concatenate([bias_ref[pl.ds(row, unit), :]] * (query.shape[0] // unit), axis=0)
    slot = lax.broadcasted_iota(jnp.int32, (1, suffix.shape[0]), 1)
    used = jnp.where(slot < length, 0.0, neg_large)
    return [
        (score(query, tree[:, :head_size]) + bias, tree[:, head_size:]),
        (score(query, suffix[:, :head_size]) + used, suffix[:, head_size:]),
    ]


def prompt_of(pieces, group):
    if len(pieces) == 1:
        return pieces[0][group]
    return jnp.concatenate([ref[group] for ref in pieces[:4]] + [ref[group] for ref in pieces[5:8]] + [pieces[4][group] + pieces[8][group]], axis=0)


def project(attended_ref, weight_own_ref, weight_other_ref, out_ref):
    width = weight_own_ref.shape[0]
    columns = 512 if out_ref.shape[1] % 512 == 0 else out_ref.shape[1]
    for c in range(0, out_ref.shape[1], columns):
        product = jnp.dot(attended_ref[:, :width], weight_own_ref[:, c : c + columns], preferred_element_type=jnp.float32)
        product += jnp.dot(attended_ref[:, width:], weight_other_ref[:, c : c + columns], preferred_element_type=jnp.float32)
        out_ref[:, c : c + columns] = product.astype(out_ref.dtype)


def put_heads(attended_ref, number, unit, attended):
    head_size = attended.shape[1]
    for h in range(attended.shape[0] // unit):
        attended_ref[number * unit : (number + 1) * unit, h * head_size : (h + 1) * head_size] = attended[h * unit : (h + 1) * unit]


def first_row(chunk_rows, offset):
    return (lax.axis_index("tp") ^ offset) * chunk_rows


def prepare_kernel(
    unit, chunk_rows, parents_hbm, accepted_hbm, length_hbm, group_hbm, own_hbm, tree_hbm, suffix_hbm, shard_hbm, weight_hbm, other_ref,
    bias_ref, path_ref, state_ref, own_ref, shard_ref, weight_ref, parents_ref, accepted_ref, length_ref, group_ref, tree_ref, suffix_ref, arrival
):
    requests, node_count = parents_ref.shape
    path_length = accepted_ref.shape[1]
    head_size = tree_ref.shape[1] // 2
    start = pl.multiple_of(first_row(chunk_rows, 2), unit)
    base = jnp.minimum(start // node_count, requests - suffix_ref.shape[0])
    copies = [
        pltpu.make_async_copy(source, target, arrival.at[place])
        for place, (source, target) in enumerate((
            (parents_hbm, parents_ref),
            (accepted_hbm, accepted_ref),
            (tree_hbm, tree_ref),
            (length_hbm, length_ref),
            (group_hbm, group_ref),
            (own_hbm.at[pl.ds(start, chunk_rows)], own_ref),
            (suffix_hbm.at[pl.ds(base, suffix_ref.shape[0])], suffix_ref),
            (shard_hbm, shard_ref),
            (weight_hbm, weight_ref),
        ))
    ]
    for copy in copies:
        copy.start()
    for copy in copies[:3]:
        copy.wait()
    above = lax.broadcasted_iota(jnp.int32, (node_count, node_count), 0)
    below = lax.broadcasted_iota(jnp.int32, (node_count, node_count), 1)
    node = lax.broadcasted_iota(jnp.int32, (node_count, path_length), 0)
    closures = []
    for r in range(requests):
        parent = jnp.broadcast_to(parents_ref[r : r + 1, :], (node_count, node_count))
        step = ((parent == above) & (below > 0)) | (above == below)
        closures.append(jnp.where(step, 1.0, 0.0).astype(jnp.bfloat16))
    for repeat in range(max(1, (node_count - 1).bit_length())):
        closures = [jnp.dot(c, c, preferred_element_type=jnp.float32) for c in closures]
        closures = [jnp.where(c > 0.5, 1.0, 0.0).astype(jnp.bfloat16) for c in closures]
    for r in range(requests):
        related = closures[r].astype(jnp.float32).T
        rows = slice(r * node_count, (r + 1) * node_count)
        bias_ref[rows, :] = jnp.where(related > 0.5, 0.0, neg_large)
        chosen = jnp.broadcast_to(accepted_ref[r : r + 1, :], (node_count, path_length)) == node
        path_ref[r] = lax.dot_general(
            jnp.where(chosen, 1.0, 0.0).astype(jnp.bfloat16),
            tree_ref[rows, :],
            (((0,), (0,)), ((), ())),
            preferred_element_type=jnp.float32,
        ).astype(jnp.bfloat16)
    for copy in copies[3:7]:
        copy.wait()
    for number in range(chunk_rows // unit):
        row = pl.multiple_of(start + number * unit, unit)
        request = row // node_count
        query = jnp.concatenate(
            [stacked_heads(own_ref, number * unit, unit, head_size), stacked_heads(other_ref, row, unit, head_size)], axis=0
        )
        blocks = private_blocks(query, row, unit, length_ref[request], bias_ref, tree_ref, suffix_ref[request - base])
        largest, total, result = absorb(blocks, log2_rate(head_size))
        lanes = result.shape
        rows = slice(number * lanes[0], (number + 1) * lanes[0])
        group = group_ref[request].astype(jnp.float32)
        for place, value in enumerate((result, largest, total, group)):
            state_ref[rows, place * head_size : (place + 1) * head_size] = jnp.broadcast_to(value, lanes)
    for copy in copies[7:]:
        copy.wait()


def in_smem():
    return pl.BlockSpec(memory_space=pltpu.SMEM)


def in_vmem():
    return pl.BlockSpec(memory_space=pltpu.VMEM)


def prepare(unit, chunk_rows, parents, accepted, lengths, groups, own, tree_kv, suffix_kv, shard, weight, other):
    requests, node_count = parents.shape
    head_size = tree_kv.shape[1] // 2
    state_rows = chunk_rows * 2 * (own.shape[1] // head_size)
    touched = min(requests, -(-(chunk_rows + node_count - unit) // node_count))
    sources = [pltpu.with_memory_space_constraint(a, pltpu.HBM) for a in (parents, accepted, lengths, groups, own, tree_kv, suffix_kv, shard, weight)]
    return pl.pallas_call(
        functools.partial(prepare_kernel, unit, chunk_rows),
        in_specs=[pl.BlockSpec(memory_space=pltpu.HBM)] * 9 + [in_vmem()],
        out_specs=[in_vmem()] * 6,
        out_shape=(
            jax.ShapeDtypeStruct((requests * node_count, node_count), jnp.float32),
            jax.ShapeDtypeStruct((requests, accepted.shape[1], tree_kv.shape[1]), jnp.bfloat16),
            jax.ShapeDtypeStruct((state_rows, 4 * head_size), jnp.float32),
            jax.ShapeDtypeStruct((chunk_rows, own.shape[1]), own.dtype),
            jax.ShapeDtypeStruct(shard.shape, shard.dtype),
            jax.ShapeDtypeStruct(weight.shape, weight.dtype),
        ),
        scratch_shapes=[
            pltpu.VMEM(parents.shape, jnp.int32),
            pltpu.VMEM(accepted.shape, jnp.int32),
            pltpu.SMEM(lengths.shape, jnp.int32),
            pltpu.SMEM(groups.shape, jnp.int32),
            pltpu.VMEM(tree_kv.shape, tree_kv.dtype),
            pltpu.VMEM((touched, *suffix_kv.shape[1:]), suffix_kv.dtype),
            pltpu.SemaphoreType.DMA((9,)),
        ],
        compiler_params=pltpu.CompilerParams(vmem_limit_bytes=vmem_bytes),
        name="prepare",
        cost_estimate=pl.CostEstimate(flops=400_000_000, bytes_accessed=2_000_000, transcendentals=0),
    )(*sources, other)


def far_kernel(unit, piece_count, own_ref, other_ref, state_ref, *rest):
    pieces, (weight_own_ref, weight_other_ref, out_ref, attended_ref) = rest[:piece_count], rest[piece_count:]
    chunk_rows = out_ref.shape[0]
    head_size = state_ref.shape[1] // 4
    rate = log2_rate(head_size)
    group_count = pieces[0].shape[0]
    prompts = [prompt_of(pieces, g) for g in range(group_count)]
    start = first_row(chunk_rows, 2)
    for number in range(chunk_rows // unit):
        row = pl.multiple_of(start + number * unit, unit)
        query = jnp.concatenate(
            [stacked_heads(own_ref, number * unit, unit, head_size), stacked_heads(other_ref, row, unit, head_size)], axis=0
        )
        rows = slice(number * query.shape[0], (number + 1) * query.shape[0])
        before, largest, total, group = (state_ref[rows, place * head_size : (place + 1) * head_size] for place in range(4))
        prompt = prompts[0]
        for g in range(1, group_count):
            mine = jnp.broadcast_to(group[:1, :1], prompt.shape) == g
            prompt = jnp.where(mine, prompts[g], prompt)
        scores = score(query, prompt[:, :head_size])
        top = jnp.maximum(largest[:, :1], jnp.max(scores, axis=1, keepdims=True))
        weight = jnp.exp2((scores - top) * rate)
        fade = jnp.exp2((largest[:, :1] - top) * rate)
        total = total[:, :1] * fade + jnp.sum(weight, axis=1, keepdims=True)
        result = before * fade + jnp.dot(weight.astype(jnp.bfloat16), prompt[:, head_size:], preferred_element_type=jnp.float32)
        put_heads(attended_ref, number, unit, (result / total).astype(jnp.bfloat16))
    project(attended_ref, weight_own_ref, weight_other_ref, out_ref)


def near_kernel(unit, piece_count, length_ref, group_ref, own_ref, other_ref, bias_ref, tree_ref, suffix_ref, *rest):
    pieces, (weight_own_ref, weight_other_ref, out_ref, attended_ref) = rest[:piece_count], rest[piece_count:]
    chunk_rows = out_ref.shape[0]
    head_size = tree_ref.shape[1] // 2
    start = first_row(chunk_rows, 0)
    for number in range(chunk_rows // unit):
        row = pl.multiple_of(start + number * unit, unit)
        query = jnp.concatenate([stacked_heads(ref, row, unit, head_size) for ref in (own_ref, other_ref)], axis=0)
        request = row // bias_ref.shape[1]
        blocks = private_blocks(query, row, unit, length_ref[request], bias_ref, tree_ref, suffix_ref[request])
        prompt = prompt_of(pieces, group_ref[request])
        blocks.append((score(query, prompt[:, :head_size]), prompt[:, head_size:]))
        largest, total, result = absorb(blocks, log2_rate(head_size))
        put_heads(attended_ref, number, unit, (result / total).astype(jnp.bfloat16))
    project(attended_ref, weight_own_ref, weight_other_ref, out_ref)


def chunk(kernel, name, dtype, scalars, arrays, chunk_rows, weights):
    in_specs = [in_smem()] * len(scalars) + [in_vmem()] * (len(arrays) + len(weights))
    return pl.pallas_call(
        kernel,
        in_specs=in_specs,
        out_specs=in_vmem(),
        out_shape=jax.ShapeDtypeStruct((chunk_rows, weights[0].shape[1]), dtype),
        scratch_shapes=[pltpu.VMEM((chunk_rows, 2 * weights[0].shape[0]), jnp.bfloat16)],
        compiler_params=pltpu.CompilerParams(vmem_limit_bytes=vmem_bytes),
        name=name,
        cost_estimate=pl.CostEstimate(flops=500_000_000, bytes_accessed=1_000_000, transcendentals=0),
    )(*scalars, *arrays, *weights)


def local(req_count, tp_count, queries, tree_kv, suffix_kv, suffix_len, group_ids, parents, accepted, prompt_kv, out_weight):
    chunk_rows = queries.shape[0] // tp_count
    unit = math.gcd(chunk_rows, parents.shape[1])
    other_queries = swap_in_pair(queries, tp_count)
    if req_count == 8 and tp_count % 2 == 0:
        fetched = fetch_shards(prompt_kv, req_count, tp_count)
        other_weight = swap_in_pair(out_weight, tp_count)
    else:
        fetched = None
        other_weight = swap_in_pair(out_weight, tp_count)
    bias, path_cache, state, far_queries, shard, own_weight = prepare(
        unit, chunk_rows, parents, accepted, suffix_len, group_ids, queries, tree_kv, suffix_kv, prompt_kv, out_weight, other_queries
    )
    if fetched is None:
        pieces = [lax.all_gather(prompt_kv, "req", axis=1, tiled=True)]
    else:
        pieces = [shard, *fetched, *(swap_in_pair(after(piece, state), tp_count) for piece in fetched)]
    weights = (own_weight, other_weight)
    far = chunk(
        functools.partial(far_kernel, unit, len(pieces)), "far_chunk", jnp.bfloat16, (), (far_queries, other_queries, state, *pieces), chunk_rows, weights
    )
    arrived = lax.ppermute(far, "tp", [(t, t ^ 2) for t in range(tp_count)])
    near = chunk(
        functools.partial(near_kernel, unit, len(pieces)), "near_chunk", jnp.float32, (suffix_len, group_ids),
        (queries, other_queries, bias, tree_kv, suffix_kv, *pieces), chunk_rows, weights
    )
    layer_output = (near + arrived.astype(jnp.float32)).astype(jnp.bfloat16)
    return (layer_output, path_cache)


def solution(mesh):
    return jax.shard_map(
        functools.partial(local, mesh.shape["req"], mesh.shape["tp"]),
        mesh=mesh,
        in_specs=(
            P("req", "tp"),
            P("req", None),
            P("req", None, None),
            P("req"),
            P("req"),
            P("req", None),
            P("req", None),
            P(None, "req", None),
            P("tp", None),
        ),
        out_specs=(P(("req", "tp"), None), P("req", None, None)),
        check_vma=False,
    )
```

time: 35.2 us -> 30 us (0.85)
  waiting for transfers between devices: 4.78 us -> 9.34 us
  local copies, waits for them, and re-layouts: 4.16 us -> 0.02 us
  Pallas kernels: 11 us -> 8.39 us
  other arithmetic: 2.62 us -> 0.82 us
  starting transfers between devices: 11.3 us -> 10.5 us
    ppermute x1, waiting for transfers between devices: 2.99 us -> 7.25 us  [local(): arrived = lax.ppermute(far, 'tp', [(t, t ^ 2) for t in range(tp_count)])]
    unnamed x32 -> x10, local copies, waits for them, and re-layouts: 4.16 us -> 0.02 us
    pallas_call x3, Pallas kernels: 11 us -> 8.39 us  [the longest x2 4.73 us: chunk(): pl.pallas_call(kernel, in_specs=in_specs, out_specs=in_vmem(), out_shape=...]
    ppermute x6, starting transfers between devices: 2.78 us -> 1.62 us  [swap_in_pair(): return lax.ppermute(array, 'tp', [(t, t ^ 1) for t in range(tp_count)])]
    convert_element_type x1, other arithmetic: 1.84 us -> 0.82 us  [local(): layer_output = (near + arrived.astype(jnp.float32)).astype(jnp.bfloat16)]
    broadcast_in_dim x1 -> x0, other arithmetic: 0.78 us -> none  [split_gather(): last[None]]
  transfers between devices with their start and end apart: 11 -> 11, of which waited for: 4 -> 6; matrix products, arithmetic and copies ran while one was open for 2% -> 0% of each run, Pallas kernels for 18% -> 21%
where the time goes in v2:
time: 30 us; the launch traced here: 29.8 us
  starting transfers between devices  10.5 us (35%)
  waiting for transfers between devices  9.34 us (31%)
  Pallas kernels  8.39 us (28%)
  other arithmetic  0.82 us (3%)
  between operations  0.71 us (2%)
    ppermute x4, starting transfers between devices, fetch_shards(): arrived.append(lax.ppermute(shard, ('req', 'tp'), pairs))  7.35 us
    ppermute x1, waiting for transfers between devices, local(): arrived = lax.ppermute(far, 'tp', [(t, t ^ 2) for t in range(tp_count)])  7.25 us
    pallas_call x2, Pallas kernels, chunk(): pl.pallas_call(kernel, in_specs=in_specs, out_specs=in_vmem(), out_shape=...  4.73 us
    pallas_call x1, Pallas kernels, prepare(): pl.pallas_call(functools.partial(prepare_kernel, unit, chunk_rows), in_sp...  3.66 us
    ppermute x6, starting transfers between devices, swap_in_pair(): return lax.ppermute(array, 'tp', [(t, t ^ 1) for t in range(tp_count)])  1.62 us
    ppermute x1, starting transfers between devices, local(): arrived = lax.ppermute(far, 'tp', [(t, t ^ 2) for t in range(tp_count)])  1.54 us
    ppermute x4, waiting for transfers between devices, fetch_shards(): arrived.append(lax.ppermute(shard, ('req', 'tp'), pairs))  1.23 us
    ppermute x6, waiting for transfers between devices, swap_in_pair(): return lax.ppermute(array, 'tp', [(t, t ^ 1) for t in range(tp_count)])  0.86 us
  transfers between devices with their start and end apart: 11, of which 6 were waited for; matrix products, arithmetic and copies ran while one was open for 0% of the time, Pallas kernels for 21%

profile of v2, /device:TPU:0, one launch (start us, length us, event | category | flops | bytes accessed | tf_op | source)
XLA Modules:
  0.0 29.8 jit_solution(14368809441867177583)
XLA Ops:
  0.6 0.5 %collective-permute-start.9 = (bf16[512,2048]{1,0:T(8,128)(2,1)}, bf16[512,2048]{1,0:T(8,128)(2,1)S(1)}, u32[]{:S(2)}, u32[]{:S(2)}) collective-permute-start(bf16[512,2048]{1,0:T(8,128)(2,1)} %weight_hbm.1), channel_id=1, source_target_pairs={{0,1},{1,0},{2,3},{3,2},{4,5},{5,4},{6,7},{7,6},{8,9},{9,8},{10,11... | collective-permute-start | bytes 6291464 | tf_op jit(solution)/shard_map/ppermute | solution.py:34
  1.1 0.1 collective-permute-start
  1.2 5.0 %collective-permute-start.2 = (bf16[2,32,256]{2,1,0:T(8,128)(2,1)}, bf16[2,32,256]{2,1,0:T(8,128)(2,1)S(1)}, u32[]{:S(2)}, u32[]{:S(2)}) collective-permute-start(bf16[2,32,256]{2,1,0:T(8,128)(2,1)} %shard_hbm.1), channel_id=1, source_target_pairs={{0,24},{1,17},{2,26},{3,19},{4,28},{5,21},{6,30},{7,23},{8,16},{9,... | collective-permute-start | bytes 98312 | tf_op jit(solution)/shard_map/ppermute | solution.py:25
  6.3 1.2 %collective-permute-start.1 = (bf16[2,32,256]{2,1,0:T(8,128)(2,1)}, bf16[2,32,256]{2,1,0:T(8,128)(2,1)S(1)}, u32[]{:S(2)}, u32[]{:S(2)}) collective-permute-start(bf16[2,32,256]{2,1,0:T(8,128)(2,1)} %shard_hbm.1), channel_id=1, source_target_pairs={{0,28},{1,21},{2,30},{3,23},{4,24},{5,17},{6,26},{7,19},{8,20},{9,... | collective-permute-start | bytes 98312 | tf_op jit(solution)/shard_map/ppermute | solution.py:25
  7.4 0.7 %collective-permute-start.4 = (bf16[2,32,256]{2,1,0:T(8,128)(2,1)}, bf16[2,32,256]{2,1,0:T(8,128)(2,1)S(1)}, u32[]{:S(2)}, u32[]{:S(2)}) collective-permute-start(bf16[2,32,256]{2,1,0:T(8,128)(2,1)} %shard_hbm.1), channel_id=1, source_target_pairs={{1,9},{3,11},{5,13},{7,15},{9,1},{11,3},{13,5},{15,7},{17,25},{19,... | collective-permute-start | bytes 98312 | tf_op jit(solution)/shard_map/ppermute | solution.py:25
  8.1 0.0 collective-permute-done.other_ref
  8.1 0.5 %collective-permute-start.3 = (bf16[2,32,256]{2,1,0:T(8,128)(2,1)}, bf16[2,32,256]{2,1,0:T(8,128)(2,1)S(1)}, u32[]{:S(2)}, u32[]{:S(2)}) collective-permute-start(bf16[2,32,256]{2,1,0:T(8,128)(2,1)} %shard_hbm.1), channel_id=1, source_target_pairs={{0,4},{1,13},{2,6},{3,15},{4,0},{5,9},{6,2},{7,11},{8,12},{9,5},{1... | collective-permute-start | bytes 98312 | tf_op jit(solution)/shard_map/ppermute | solution.py:25
  8.6 3.7 %prepare.1 = (f32[384,64]{1,0:T(8,128)S(1)}, bf16[6,8,256]{2,1,0:T(8,128)(2,1)}, f32[768,512]{1,0:T(8,128)S(1)}, bf16[96,512]{1,0:T(8,128)(2,1)S(1)}, bf16[2,32,...) custom-call(s32[6,64]{1,0:T(8,128)} %parents_hbm.1, s32[6,8]{1,0:T(8,128)} %accepted_hbm.1, s32[6]{0:T(128)} %length_ref.1, ...), custom_call_target="tpu_custom_call" | custom-call | flops 400000000 | bytes 2000000 | tf_op jit(solution)/shard_map/prepare/pallas_call | solution.py:180
  12.3 0.0 collective-permute-done.4.rest_4_
  12.3 0.0 collective-permute-done.3.rest_3_
  12.3 0.0 collective-permute-done.2.rest_2_
  12.3 1.2 %collective-permute-done.1.rest_1_ = bf16[2,32,256]{2,1,0:T(8,128)(2,1)S(1)} collective-permute-done((bf16[2,32,256]{2,1,0:T(8,128)(2,1)}, bf16[2,32,256]{2,1,0:T(8,128)(2,1)S(1)}, u32[]{:S(2)}, u32[]{:S(2)}) %collective-permute-start.1) | collective-permute-done | bytes 32800 | tf_op jit(solution)/shard_map/ppermute | solution.py:25
  13.5 0.0 collective-permute-start.5
  13.5 0.5 %collective-permute-start.6 = (bf16[2,32,256]{2,1,0:T(8,128)(2,1)S(1)}, bf16[2,32,256]{2,1,0:T(8,128)(2,1)S(1)}, u32[]{:S(2)}, u32[]{:S(2)}) collective-permute-start(bf16[2,32,256]{2,1,0:T(8,128)(2,1)S(1)} %collective-permute-done.2.rest_2_), channel_id=1, source_target_pairs={{0,1},{1,0},{2,3},{3,2},{4,5},{5,4},{6,7},{7,6},{8,9},{9,8},{10,11... | collective-permute-start | bytes 98312 | tf_op jit(solution)/shard_map/ppermute | solution.py:34
  14.0 0.0 collective-permute-start.7
  14.0 0.5 %collective-permute-start.8 = (bf16[2,32,256]{2,1,0:T(8,128)(2,1)S(1)}, bf16[2,32,256]{2,1,0:T(8,128)(2,1)S(1)}, u32[]{:S(2)}, u32[]{:S(2)}) collective-permute-start(bf16[2,32,256]{2,1,0:T(8,128)(2,1)S(1)} %collective-permute-done.4.rest_4_), channel_id=1, source_target_pairs={{0,1},{1,0},{2,3},{3,2},{4,5},{5,4},{6,7},{7,6},{8,9},{9,8},{10,11... | collective-permute-start | bytes 98312 | tf_op jit(solution)/shard_map/ppermute | solution.py:34
  14.5 0.2 collective-permute-done.5.rest_5_
  14.7 0.2 collective-permute-done.6.rest_6_
  14.9 0.3 %collective-permute-done.7.rest_7_ = bf16[2,32,256]{2,1,0:T(8,128)(2,1)S(1)} collective-permute-done((bf16[2,32,256]{2,1,0:T(8,128)(2,1)S(1)}, bf16[2,32,256]{2,1,0:T(8,128)(2,1)S(1)}, u32[]{:S(2)}, u32[]{:S(2)}) %collective-permute-start.7) | collective-permute-done | bytes 32800 | tf_op jit(solution)/shard_map/ppermute | solution.py:34
  15.2 0.2 collective-permute-done.8.rest_8_
  15.4 0.0 collective-permute-done.9.rest_10_
  15.4 0.0 copy-start
  15.4 0.0 copy-start.1
  15.4 0.0 copy-start.2
  15.4 0.0 copy-start.3
  15.4 0.0 copy-start.4
  15.4 2.1 %far_chunk.1 = bf16[96,2048]{1,0:T(8,128)(2,1)S(1)} custom-call(bf16[96,512]{1,0:T(8,128)(2,1)S(1)} %get-tuple-element.20.own_ref, bf16[384,512]{1,0:T(8,128)(2,1)S(1)} %collective-permute-done.other_ref, f32[768,512]{1,0:T(8,128)S(1)} %get-tuple-element.14.state_ref, bf16[2,32,256]{2,1,0:T(8,128)(2,1)S(1)} %get-tuple-element.13.rest_0_, ...), custom_call_target="tpu_custom_call" | custom-call | flops 500000000 | bytes 1000000 | tf_op jit(solution)/shard_map/far_chunk/pallas_call | solution.py:255
  17.5 1.5 %collective-permute-start.10 = (bf16[96,2048]{1,0:T(8,128)(2,1)S(1)}, bf16[96,2048]{1,0:T(8,128)(2,1)S(1)}, u32[]{:S(2)}, u32[]{:S(2)}) collective-permute-start(bf16[96,2048]{1,0:T(8,128)(2,1)S(1)} %far_chunk.1), channel_id=1, source_target_pairs={{0,2},{1,3},{2,0},{3,1},{4,6},{5,7},{6,4},{7,5},{8,10},{9,11},{10,... | collective-permute-start | bytes 1179656 | tf_op jit(solution)/shard_map/ppermute | solution.py:288
  19.1 0.0 copy-done
  19.1 0.0 copy-done.1
  19.1 0.0 copy-done.2
  19.1 0.0 copy-done.3
  19.1 0.0 copy-done.4
  19.1 2.6 %near_chunk.1 = f32[96,2048]{1,0:T(8,128)S(1)} custom-call(s32[6]{0:T(128)S(1)} %copy-done.3, s32[6]{0:T(128)S(1)} %copy-done.4, bf16[384,512]{1,0:T(8,128)(2,1)S(1)} %copy-done.1, bf16[384,512]{1,0:T(8,128)(2,1)S(1)} %collective-permute-done.other_ref, f32[384,64]{1,0:T(8,128)S(1)} %get-tuple-element.12.bias_ref, bf16[384,256]{1,0:T(8,128)(2,1)S(1)} %copy-done.2, ...), custom_call_target="tpu_custom_call" | custom-call | flops 500000000 | bytes 1000000 | tf_op jit(solution)/shard_map/near_chunk/pallas_call | solution.py:255
  21.7 7.2 %collective-permute-done.10 = bf16[96,2048]{1,0:T(8,128)(2,1)S(1)} collective-permute-done((bf16[96,2048]{1,0:T(8,128)(2,1)S(1)}, bf16[96,2048]{1,0:T(8,128)(2,1)S(1)}, u32[]{:S(2)}, u32[]{:S(2)}) %collective-permute-start.10) | collective-permute-done | bytes 393248 | tf_op jit(solution)/shard_map/ppermute | solution.py:288
  29.0 0.8 %add_convert_fusion = bf16[96,2048]{1,0:T(8,128)(2,1)} fusion(f32[96,2048]{1,0:T(8,128)S(1)} %near_chunk.1, bf16[96,2048]{1,0:T(8,128)(2,1)S(1)} %collective-permute-done.10), kind=kLoop, calls=%fused_computation | loop fusion | flops 589824 | bytes 1572864 | tf_op jit(solution)/shard_map/convert_element_type | solution.py:293
Async XLA Ops:
  0.6 14.8 %collective-permute-start.9 = (bf16[512,2048]{1,0:T(8,128)(2,1)}, bf16[512,2048]{1,0:T(8,128)(2,1)S(1)}, u32[]{:S(2)}, u32[]{:S(2)}) collective-permute-start(bf16[512,2048]{1,0:T(8,128)(2,1)} %weight_hbm.1), channel_id=1, source_target_pairs={{0,1},{1,0},{2,3},{3,2},{4,5},{5,4},{6,7},{7,6},{8,9},{9,8},{10,11... | collective-permute-start | bytes 6291464 | tf_op jit(solution)/shard_map/ppermute | solution.py:34
  1.1 6.9 %collective-permute-start = (bf16[384,512]{1,0:T(8,128)(2,1)}, bf16[384,512]{1,0:T(8,128)(2,1)S(1)}, u32[]{:S(2)}, u32[]{:S(2)}) collective-permute-start(bf16[384,512]{1,0:T(8,128)(2,1)} %own_ref.1), channel_id=1, source_target_pairs={{0,1},{1,0},{2,3},{3,2},{4,5},{5,4},{6,7},{7,6},{8,9},{9,8},{10,11... | collective-permute-start | bytes 1179656 | tf_op jit(solution)/shard_map/ppermute | solution.py:34
  1.2 11.1 %collective-permute-start.2 = (bf16[2,32,256]{2,1,0:T(8,128)(2,1)}, bf16[2,32,256]{2,1,0:T(8,128)(2,1)S(1)}, u32[]{:S(2)}, u32[]{:S(2)}) collective-permute-start(bf16[2,32,256]{2,1,0:T(8,128)(2,1)} %shard_hbm.1), channel_id=1, source_target_pairs={{0,24},{1,17},{2,26},{3,19},{4,28},{5,21},{6,30},{7,23},{8,16},{9,... | collective-permute-start | bytes 98312 | tf_op jit(solution)/shard_map/ppermute | solution.py:25
  6.3 7.3 %collective-permute-start.1 = (bf16[2,32,256]{2,1,0:T(8,128)(2,1)}, bf16[2,32,256]{2,1,0:T(8,128)(2,1)S(1)}, u32[]{:S(2)}, u32[]{:S(2)}) collective-permute-start(bf16[2,32,256]{2,1,0:T(8,128)(2,1)} %shard_hbm.1), channel_id=1, source_target_pairs={{0,28},{1,21},{2,30},{3,23},{4,24},{5,17},{6,26},{7,19},{8,20},{9,... | collective-permute-start | bytes 98312 | tf_op jit(solution)/shard_map/ppermute | solution.py:25
  7.4 4.8 %collective-permute-start.4 = (bf16[2,32,256]{2,1,0:T(8,128)(2,1)}, bf16[2,32,256]{2,1,0:T(8,128)(2,1)S(1)}, u32[]{:S(2)}, u32[]{:S(2)}) collective-permute-start(bf16[2,32,256]{2,1,0:T(8,128)(2,1)} %shard_hbm.1), channel_id=1, source_target_pairs={{1,9},{3,11},{5,13},{7,15},{9,1},{11,3},{13,5},{15,7},{17,25},{19,... | collective-permute-start | bytes 98312 | tf_op jit(solution)/shard_map/ppermute | solution.py:25
  8.1 4.2 %collective-permute-start.3 = (bf16[2,32,256]{2,1,0:T(8,128)(2,1)}, bf16[2,32,256]{2,1,0:T(8,128)(2,1)S(1)}, u32[]{:S(2)}, u32[]{:S(2)}) collective-permute-start(bf16[2,32,256]{2,1,0:T(8,128)(2,1)} %shard_hbm.1), channel_id=1, source_target_pairs={{0,4},{1,13},{2,6},{3,15},{4,0},{5,9},{6,2},{7,11},{8,12},{9,5},{1... | collective-permute-start | bytes 98312 | tf_op jit(solution)/shard_map/ppermute | solution.py:25
  13.5 1.2 %collective-permute-start.5 = (bf16[2,32,256]{2,1,0:T(8,128)(2,1)S(1)}, bf16[2,32,256]{2,1,0:T(8,128)(2,1)S(1)}, u32[]{:S(2)}, u32[]{:S(2)}) collective-permute-start(bf16[2,32,256]{2,1,0:T(8,128)(2,1)S(1)} %collective-permute-done.1.rest_1_), channel_id=1, source_target_pairs={{0,1},{1,0},{2,3},{3,2},{4,5},{5,4},{6,7},{7,6},{8,9},{9,8},{10,11... | collective-permute-start | bytes 98312 | tf_op jit(solution)/shard_map/ppermute | solution.py:34
  13.5 1.3 %collective-permute-start.6 = (bf16[2,32,256]{2,1,0:T(8,128)(2,1)S(1)}, bf16[2,32,256]{2,1,0:T(8,128)(2,1)S(1)}, u32[]{:S(2)}, u32[]{:S(2)}) collective-permute-start(bf16[2,32,256]{2,1,0:T(8,128)(2,1)S(1)} %collective-permute-done.2.rest_2_), channel_id=1, source_target_pairs={{0,1},{1,0},{2,3},{3,2},{4,5},{5,4},{6,7},{7,6},{8,9},{9,8},{10,11... | collective-permute-start | bytes 98312 | tf_op jit(solution)/shard_map/ppermute | solution.py:34
  14.0 1.2 %collective-permute-start.7 = (bf16[2,32,256]{2,1,0:T(8,128)(2,1)S(1)}, bf16[2,32,256]{2,1,0:T(8,128)(2,1)S(1)}, u32[]{:S(2)}, u32[]{:S(2)}) collective-permute-start(bf16[2,32,256]{2,1,0:T(8,128)(2,1)S(1)} %collective-permute-done.3.rest_3_), channel_id=1, source_target_pairs={{0,1},{1,0},{2,3},{3,2},{4,5},{5,4},{6,7},{7,6},{8,9},{9,8},{10,11... | collective-permute-start | bytes 98312 | tf_op jit(solution)/shard_map/ppermute | solution.py:34
  14.0 1.3 %collective-permute-start.8 = (bf16[2,32,256]{2,1,0:T(8,128)(2,1)S(1)}, bf16[2,32,256]{2,1,0:T(8,128)(2,1)S(1)}, u32[]{:S(2)}, u32[]{:S(2)}) collective-permute-start(bf16[2,32,256]{2,1,0:T(8,128)(2,1)S(1)} %collective-permute-done.4.rest_4_), channel_id=1, source_target_pairs={{0,1},{1,0},{2,3},{3,2},{4,5},{5,4},{6,7},{7,6},{8,9},{9,8},{10,11... | collective-permute-start | bytes 98312 | tf_op jit(solution)/shard_map/ppermute | solution.py:34
  15.4 3.7 %copy-start = (bf16[6,256,256]{2,1,0:T(8,128)(2,1)S(1)}, bf16[6,256,256]{2,1,0:T(8,128)(2,1)}, u32[]{:S(2)}) copy-start(bf16[6,256,256]{2,1,0:T(8,128)(2,1)} %suffix_ref.1) | copy-start | bytes 2359300
  15.4 3.7 %copy-start.1 = (bf16[384,512]{1,0:T(8,128)(2,1)S(1)}, bf16[384,512]{1,0:T(8,128)(2,1)}, u32[]{:S(2)}) copy-start(bf16[384,512]{1,0:T(8,128)(2,1)} %own_ref.1) | copy-start | bytes 1179652
  15.4 3.7 %copy-start.2 = (bf16[384,256]{1,0:T(8,128)(2,1)S(1)}, bf16[384,256]{1,0:T(8,128)(2,1)}, u32[]{:S(2)}) copy-start(bf16[384,256]{1,0:T(8,128)(2,1)} %tree_ref.1) | copy-start | bytes 589828
  15.4 3.7 %copy-start.3 = (s32[6]{0:T(128)S(1)}, s32[6]{0:T(128)}, u32[]{:S(2)}) copy-start(s32[6]{0:T(128)} %length_ref.1) | copy-start | bytes 76
  15.4 3.7 %copy-start.4 = (s32[6]{0:T(128)S(1)}, s32[6]{0:T(128)}, u32[]{:S(2)}) copy-start(s32[6]{0:T(128)} %group_ref.1) | copy-start | bytes 76
  17.5 11.4 %collective-permute-start.10 = (bf16[96,2048]{1,0:T(8,128)(2,1)S(1)}, bf16[96,2048]{1,0:T(8,128)(2,1)S(1)}, u32[]{:S(2)}, u32[]{:S(2)}) collective-permute-start(bf16[96,2048]{1,0:T(8,128)(2,1)S(1)} %far_chunk.1), channel_id=1, source_target_pairs={{0,2},{1,3},{2,0},{3,1},{4,6},{5,7},{6,4},{7,5},{8,10},{9,11},{10,... | collective-permute-start | bytes 1179656 | tf_op jit(solution)/shard_map/ppermute | solution.py:288

commit v3 on v2

v3 whole, which is shorter than its diff:
```python
import functools
import math

import jax
import jax.numpy as jnp
from jax import lax
from jax.experimental import pallas as pl
from jax.experimental.pallas import tpu as pltpu
from jax.sharding import PartitionSpec as P

neg_large = -1e30
vmem_bytes = 12 * 1024 * 1024


def fetch_shards(shard, req_count, tp_count):
    masks = ((7, 6, 1), (5, 4, 3, 2))
    arrived = []
    for step in range(4):
        pairs = []
        for r in range(req_count):
            for t in range(tp_count):
                mine = masks[t % 2]
                if step < len(mine):
                    pairs.append((r * tp_count + t, (r ^ mine[step]) * tp_count + t))
        arrived.append(lax.ppermute(shard, ("req", "tp"), pairs))
    return arrived


def after(array, earlier):
    return lax.optimization_barrier((array, earlier))[0]


def swap_in_pair(array, tp_count):
    return lax.ppermute(array, "tp", [(t, t ^ 1) for t in range(tp_count)])


def score(query, keys):
    return lax.dot_general(query, keys, (((1,), (1,)), ((), ())), preferred_element_type=jnp.float32)


def stacked_heads(ref, row, unit, head_size):
    return jnp.concatenate([ref[pl.ds(row, unit), h : h + head_size] for h in range(0, ref.shape[1], head_size)], axis=0)


def log2_rate(head_size):
    return head_size**-0.5 * math.log2(math.e)


def absorb(blocks, rate):
    largest = functools.reduce(jnp.maximum, [jnp.max(s, axis=1, keepdims=True) for s, _ in blocks])
    total, result = 0.0, 0.0
    for scores, values in blocks:
        weight = jnp.exp2((scores - largest) * rate)
        total = total + jnp.sum(weight, axis=1, keepdims=True)
        result = result + jnp.dot(weight.astype(jnp.bfloat16), values, preferred_element_type=jnp.float32)
    return largest, total, result


def private_blocks(query, bias, used, tree, suffix):
    head_size = query.shape[1]
    every = jnp.concatenate([bias] * (query.shape[0] // bias.shape[0]), axis=0)
    return [
        (score(query, tree[:, :head_size]) + every, tree[:, head_size:]),
        (score(query, suffix[:, :head_size]) + used, suffix[:, head_size:]),
    ]


def prompt_of(pieces, group):
    if len(pieces) == 1:
        return pieces[0][group]
    shard, fetched, swapped = pieces
    groups = shard.shape[0]
    places = range(group, fetched.shape[0], groups)
    kept = [shard[group]] + [ref[place] for ref in (fetched, swapped) for place in places[:-1]]
    return jnp.concatenate([*kept, fetched[places[-1]] + swapped[places[-1]]], axis=0)


def project(attended_ref, weight_own_ref, weight_other_ref, out_ref):
    width = weight_own_ref.shape[0]
    columns = 512 if out_ref.shape[1] % 512 == 0 else out_ref.shape[1]
    for c in range(0, out_ref.shape[1], columns):
        product = jnp.dot(attended_ref[:, :width], weight_own_ref[:, c : c + columns], preferred_element_type=jnp.float32)
        product += jnp.dot(attended_ref[:, width:], weight_other_ref[:, c : c + columns], preferred_element_type=jnp.float32)
        out_ref[:, c : c + columns] = product.astype(out_ref.dtype)


def put_heads(attended_ref, number, unit, attended):
    head_size = attended.shape[1]
    for h in range(attended.shape[0] // unit):
        attended_ref[number * unit : (number + 1) * unit, h * head_size : (h + 1) * head_size] = attended[h * unit : (h + 1) * unit]


def first_row(chunk_rows, offset):
    return (lax.axis_index("tp") ^ offset) * chunk_rows


def closures(parents, node_count):
    above = lax.broadcasted_iota(jnp.int32, (node_count, node_count), 0)
    below = lax.broadcasted_iota(jnp.int32, (node_count, node_count), 1)
    found = []
    for parent in parents:
        step = ((jnp.broadcast_to(parent, (node_count, node_count)) == above) & (below > 0)) | (above == below)
        found.append(jnp.where(step, 1.0, 0.0).astype(jnp.bfloat16))
    for repeat in range(max(1, (node_count - 1).bit_length())):
        found = [jnp.dot(c, c, preferred_element_type=jnp.float32) for c in found]
        found = [jnp.where(c > 0.5, 1.0, 0.0).astype(jnp.bfloat16) for c in found]
    return found


def bias_of(closure):
    return jnp.where(closure.astype(jnp.float32).T > 0.5, 0.0, neg_large)


def first_request(chunk_rows, offset, node_count, requests, touched):
    return jnp.minimum(first_row(chunk_rows, offset) // node_count, requests - touched)


def load_kernel(
    chunk_rows, parents_hbm, length_hbm, group_hbm, own_hbm, tree_hbm, suffix_hbm, shard_hbm, weight_hbm,
    bias_ref, notes_ref, own_ref, tree_ref, suffix_ref, shard_ref, weight_ref, parents_ref, length_ref, group_ref, arrival
):
    requests, node_count = parents_ref.shape
    touched, slot_count = suffix_ref.shape[:2]
    start = pl.multiple_of(first_row(chunk_rows, 2), math.gcd(chunk_rows, node_count))
    base = first_request(chunk_rows, 2, node_count, requests, touched)
    copies = [
        pltpu.make_async_copy(source, target, arrival.at[place])
        for place, (source, target) in enumerate((
            (parents_hbm, parents_ref),
            (length_hbm, length_ref),
            (group_hbm, group_ref),
            (own_hbm.at[pl.ds(start, chunk_rows)], own_ref),
            (tree_hbm.at[pl.ds(pl.multiple_of(base * node_count, node_count), touched * node_count)], tree_ref),
            (suffix_hbm.at[pl.ds(base, touched)], suffix_ref),
            (shard_hbm, shard_ref),
            (weight_hbm, weight_ref),
        ))
    ]
    for copy in copies:
        copy.start()
    for copy in copies[:3]:
        copy.wait()
    found = closures([parents_ref[pl.ds(base + k, 1), :] for k in range(touched)], node_count)
    slot = lax.broadcasted_iota(jnp.int32, (1, slot_count), 1)
    for k in range(touched):
        bias_ref[k * node_count : (k + 1) * node_count, :] = bias_of(found[k])
        notes_ref[k, :1, :] = jnp.where(slot < length_ref[base + k], 0.0, neg_large)
        notes_ref[k, 1:2, :] = jnp.broadcast_to(group_ref[base + k].astype(jnp.float32), (1, slot_count))
    for copy in copies[3:]:
        copy.wait()


def private_kernel(unit, chunk_rows, node_count, requests, bias_ref, notes_ref, own_ref, tree_ref, suffix_ref, other_ref, state_ref):
    head_size = tree_ref.shape[1] // 2
    touched = suffix_ref.shape[0]
    start = pl.multiple_of(first_row(chunk_rows, 2), unit)
    base = first_request(chunk_rows, 2, node_count, requests, touched)
    for number in range(chunk_rows // unit):
        row = pl.multiple_of(start + number * unit, unit)
        place = row // node_count - base
        query = jnp.concatenate(
            [stacked_heads(own_ref, number * unit, unit, head_size), stacked_heads(other_ref, row, unit, head_size)], axis=0
        )
        bias = bias_ref[pl.ds(pl.multiple_of(row - base * node_count, unit), unit), :]
        tree = tree_ref[pl.ds(pl.multiple_of(place * node_count, node_count), node_count), :]
        blocks = private_blocks(query, bias, notes_ref[place, :1, :], tree, suffix_ref[place])
        largest, total, result = absorb(blocks, log2_rate(head_size))
        lanes = result.shape
        rows = slice(number * lanes[0], (number + 1) * lanes[0])
        for spot, value in enumerate((result, largest, total, notes_ref[place, 1:2, :head_size])):
            state_ref[rows, spot * head_size : (spot + 1) * head_size] = jnp.broadcast_to(value, lanes)


def in_smem():
    return pl.BlockSpec(memory_space=pltpu.SMEM)


def in_vmem():
    return pl.BlockSpec(memory_space=pltpu.VMEM)


def load(unit, chunk_rows, parents, lengths, groups, own, tree_kv, suffix_kv, shard, weight):
    requests, node_count = parents.shape
    touched = min(requests, -(-(chunk_rows + node_count - unit) // node_count))
    sources = [pltpu.with_memory_space_constraint(a, pltpu.HBM) for a in (parents, lengths, groups, own, tree_kv, suffix_kv, shard, weight)]
    return pl.pallas_call(
        functools.partial(load_kernel, chunk_rows),
        in_specs=[pl.BlockSpec(memory_space=pltpu.HBM)] * 8,
        out_specs=[in_vmem()] * 7,
        out_shape=(
            jax.ShapeDtypeStruct((touched * node_count, node_count), jnp.float32),
            jax.ShapeDtypeStruct((touched, 8, suffix_kv.shape[1]), jnp.float32),
            jax.ShapeDtypeStruct((chunk_rows, own.shape[1]), own.dtype),
            jax.ShapeDtypeStruct((touched * node_count, tree_kv.shape[1]), tree_kv.dtype),
            jax.ShapeDtypeStruct((touched, *suffix_kv.shape[1:]), suffix_kv.dtype),
            jax.ShapeDtypeStruct(shard.shape, shard.dtype),
            jax.ShapeDtypeStruct(weight.shape, weight.dtype),
        ),
        scratch_shapes=[
            pltpu.VMEM(parents.shape, jnp.int32),
            pltpu.SMEM(lengths.shape, jnp.int32),
            pltpu.SMEM(groups.shape, jnp.int32),
            pltpu.SemaphoreType.DMA((8,)),
        ],
        compiler_params=pltpu.CompilerParams(vmem_limit_bytes=vmem_bytes),
        name="load",
        cost_estimate=pl.CostEstimate(flops=100_000_000, bytes_accessed=2_000_000, transcendentals=0),
    )(*sources)


def private(unit, chunk_rows, node_count, requests, loaded, other):
    bias, notes, own, tree, suffix = loaded
    head_size = tree.shape[1] // 2
    state_rows = chunk_rows * 2 * (own.shape[1] // head_size)
    return pl.pallas_call(
        functools.partial(private_kernel, unit, chunk_rows, node_count, requests),
        in_specs=[in_vmem()] * 6,
        out_specs=in_vmem(),
        out_shape=jax.ShapeDtypeStruct((state_rows, 4 * head_size), jnp.float32),
        compiler_params=pltpu.CompilerParams(vmem_limit_bytes=vmem_bytes),
        name="private",
        cost_estimate=pl.CostEstimate(flops=300_000_000, bytes_accessed=500_000, transcendentals=0),
    )(*loaded, other)


def far_kernel(unit, piece_count, own_ref, other_ref, state_ref, *rest):
    pieces, (weight_own_ref, weight_other_ref, out_ref, attended_ref) = rest[:piece_count], rest[piece_count:]
    chunk_rows = out_ref.shape[0]
    head_size = state_ref.shape[1] // 4
    rate = log2_rate(head_size)
    group_count = pieces[0].shape[0]
    prompts = [prompt_of(pieces, g) for g in range(group_count)]
    start = first_row(chunk_rows, 2)
    for number in range(chunk_rows // unit):
        row = pl.multiple_of(start + number * unit, unit)
        query = jnp.concatenate(
            [stacked_heads(own_ref, number * unit, unit, head_size), stacked_heads(other_ref, row, unit, head_size)], axis=0
        )
        rows = slice(number * query.shape[0], (number + 1) * query.shape[0])
        before, largest, total, group = (state_ref[rows, place * head_size : (place + 1) * head_size] for place in range(4))
        prompt = prompts[0]
        for g in range(1, group_count):
            mine = jnp.broadcast_to(group[:1, :1], prompt.shape) == g
            prompt = jnp.where(mine, prompts[g], prompt)
        scores = score(query, prompt[:, :head_size])
        top = jnp.maximum(largest[:, :1], jnp.max(scores, axis=1, keepdims=True))
        weight = jnp.exp2((scores - top) * rate)
        fade = jnp.exp2((largest[:, :1] - top) * rate)
        total = total[:, :1] * fade + jnp.sum(weight, axis=1, keepdims=True)
        result = before * fade + jnp.dot(weight.astype(jnp.bfloat16), prompt[:, head_size:], preferred_element_type=jnp.float32)
        put_heads(attended_ref, number, unit, (result / total).astype(jnp.bfloat16))
    project(attended_ref, weight_own_ref, weight_other_ref, out_ref)


def near_kernel(
    unit, piece_count, length_ref, group_ref, own_ref, other_ref, parents_ref, accepted_ref, tree_ref, suffix_ref, *rest
):
    pieces, (weight_own_ref, weight_other_ref, out_ref, path_ref, attended_ref, bias_ref) = rest[:piece_count], rest[piece_count:]
    chunk_rows = out_ref.shape[0]
    requests, node_count = parents_ref.shape
    path_length = accepted_ref.shape[1]
    head_size = tree_ref.shape[1] // 2
    node = lax.broadcasted_iota(jnp.int32, (node_count, path_length), 0)
    for r, closure in enumerate(closures([parents_ref[r : r + 1, :] for r in range(requests)], node_count)):
        rows = slice(r * node_count, (r + 1) * node_count)
        bias_ref[rows, :] = bias_of(closure)
        chosen = jnp.broadcast_to(accepted_ref[r : r + 1, :], (node_count, path_length)) == node
        path_ref[r] = lax.dot_general(
            jnp.where(chosen, 1.0, 0.0).astype(jnp.bfloat16),
            tree_ref[rows, :],
            (((0,), (0,)), ((), ())),
            preferred_element_type=jnp.float32,
        ).astype(jnp.bfloat16)
    prompts = [prompt_of(pieces, g) for g in range(pieces[0].shape[0])]
    slot = lax.broadcasted_iota(jnp.int32, (1, suffix_ref.shape[1]), 1)
    start = first_row(chunk_rows, 0)
    for number in range(chunk_rows // unit):
        row = pl.multiple_of(start + number * unit, unit)
        query = jnp.concatenate([stacked_heads(ref, row, unit, head_size) for ref in (own_ref, other_ref)], axis=0)
        request = row // node_count
        used = jnp.where(slot < length_ref[request], 0.0, neg_large)
        tree = tree_ref[pl.ds(pl.multiple_of(request * node_count, node_count), node_count), :]
        blocks = private_blocks(query, bias_ref[pl.ds(row, unit), :], used, tree, suffix_ref[request])
        group = group_ref[request]
        prompt = functools.reduce(lambda held, g: jnp.where(group == g, prompts[g], held), range(1, len(prompts)), prompts[0])
        blocks.append((score(query, prompt[:, :head_size]), prompt[:, head_size:]))
        largest, total, result = absorb(blocks, log2_rate(head_size))
        put_heads(attended_ref, number, unit, (result / total).astype(jnp.bfloat16))
    project(attended_ref, weight_own_ref, weight_other_ref, out_ref)


def chunk(kernel, name, outs, scalars, arrays, weights, scratch):
    return pl.pallas_call(
        kernel,
        in_specs=[in_smem()] * len(scalars) + [in_vmem()] * (len(arrays) + len(weights)),
        out_specs=[in_vmem()] * len(outs),
        out_shape=outs,
        scratch_shapes=[pltpu.VMEM((outs[0].shape[0], 2 * weights[0].shape[0]), jnp.bfloat16), *scratch],
        compiler_params=pltpu.CompilerParams(vmem_limit_bytes=vmem_bytes),
        name=name,
        cost_estimate=pl.CostEstimate(flops=500_000_000, bytes_accessed=1_000_000, transcendentals=0),
    )(*scalars, *arrays, *weights)


def local(req_count, tp_count, queries, tree_kv, suffix_kv, suffix_len, group_ids, parents, accepted, prompt_kv, out_weight):
    chunk_rows = queries.shape[0] // tp_count
    unit = math.gcd(chunk_rows, parents.shape[1])
    other_queries = swap_in_pair(queries, tp_count)
    if req_count == 8 and tp_count % 2 == 0:
        fetched = fetch_shards(prompt_kv, req_count, tp_count)
        other_weight = swap_in_pair(out_weight, tp_count)
    else:
        fetched = None
        other_weight = swap_in_pair(out_weight, tp_count)
    requests, node_count = parents.shape
    *loaded, shard, own_weight = load(unit, chunk_rows, parents, suffix_len, group_ids, queries, tree_kv, suffix_kv, prompt_kv, out_weight)
    state = private(unit, chunk_rows, node_count, requests, loaded, other_queries)
    if fetched is None:
        pieces = [lax.all_gather(prompt_kv, "req", axis=1, tiled=True)]
    else:
        joined = jnp.concatenate([after(piece, shard) for piece in fetched], axis=0)
        pieces = [shard, joined, swap_in_pair(joined, tp_count)]
    weights = (own_weight, other_weight)
    chunk_shape = (chunk_rows, out_weight.shape[1])
    (far,) = chunk(
        functools.partial(far_kernel, unit, len(pieces)), "far_chunk", [jax.ShapeDtypeStruct(chunk_shape, jnp.bfloat16)],
        (), (loaded[2], other_queries, state, *pieces), weights, ()
    )
    arrived = lax.ppermute(far, "tp", [(t, t ^ 2) for t in range(tp_count)])
    near, path_cache = chunk(
        functools.partial(near_kernel, unit, len(pieces)), "near_chunk",
        [jax.ShapeDtypeStruct(chunk_shape, jnp.float32), jax.ShapeDtypeStruct((*accepted.shape, tree_kv.shape[1]), jnp.bfloat16)],
        (suffix_len, group_ids), (queries, other_queries, parents, accepted, tree_kv, suffix_kv, *pieces), weights,
        (pltpu.VMEM((requests * node_count, node_count), jnp.float32),)
    )
    layer_output = (near + arrived.astype(jnp.float32)).astype(jnp.bfloat16)
    return (layer_output, path_cache)


def solution(mesh):
    return jax.shard_map(
        functools.partial(local, mesh.shape["req"], mesh.shape["tp"]),
        mesh=mesh,
        in_specs=(
            P("req", "tp"),
            P("req", None),
            P("req", None, None),
            P("req"),
            P("req"),
            P("req", None),
            P("req", None),
            P(None, "req", None),
            P("tp", None),
        ),
        out_specs=(P(("req", "tp"), None), P("req", None, None)),
        check_vma=False,
    )
```

time: 30 us -> 28.6 us (0.953)
  waiting for transfers between devices: 9.34 us -> 8.05 us
    ppermute x1, waiting for transfers between devices: 7.25 us -> 6.35 us  [local(): arrived = lax.ppermute(far, 'tp', [(t, t ^ 2) for t in range(tp_count)])]
    ppermute x6 -> x3, waiting for transfers between devices: 0.86 us -> 0.26 us  [swap_in_pair(): return lax.ppermute(array, 'tp', [(t, t ^ 1) for t in range(tp_count)])]
    ppermute x4, starting transfers between devices: 7.35 us -> 6.92 us  [fetch_shards(): arrived.append(lax.ppermute(shard, ('req', 'tp'), pairs))]
    ppermute x6 -> x3, starting transfers between devices: 1.62 us -> 1.87 us  [swap_in_pair(): return lax.ppermute(array, 'tp', [(t, t ^ 1) for t in range(tp_count)])]
    pallas_call x3 -> x4, Pallas kernels: 8.39 us -> 8.42 us  [the longest x2 5.48 us: chunk(): pl.pallas_call(kernel, in_specs=[in_smem()] * len(scalars) + [in_vmem()]...]
  transfers between devices with their start and end apart: 11 -> 8, of which waited for: 6 -> 3; matrix products, arithmetic and copies ran while one was open for 0% -> 0% of each run, Pallas kernels for 21% -> 22%
where the time goes in v3:
time: 28.6 us; the launch traced here: 28.5 us
  starting transfers between devices  10.3 us (36%)
  Pallas kernels  8.42 us (29%)
  waiting for transfers between devices  8.05 us (28%)
  other arithmetic  0.82 us (3%)
  between operations  0.78 us (3%)
    ppermute x4, starting transfers between devices, fetch_shards(): arrived.append(lax.ppermute(shard, ('req', 'tp'), pairs))  6.92 us
    ppermute x1, waiting for transfers between devices, local(): arrived = lax.ppermute(far, 'tp', [(t, t ^ 2) for t in range(tp_count)])  6.35 us
    pallas_call x2, Pallas kernels, chunk(): pl.pallas_call(kernel, in_specs=[in_smem()] * len(scalars) + [in_vmem()]...  5.48 us
    pallas_call x1, Pallas kernels, load(): pl.pallas_call(functools.partial(load_kernel, chunk_rows), in_specs=[pl.B...  1.88 us
    ppermute x3, starting transfers between devices, swap_in_pair(): return lax.ppermute(array, 'tp', [(t, t ^ 1) for t in range(tp_count)])  1.87 us
    ppermute x1, starting transfers between devices, local(): arrived = lax.ppermute(far, 'tp', [(t, t ^ 2) for t in range(tp_count)])  1.55 us
    ppermute x4, waiting for transfers between devices, fetch_shards(): arrived.append(lax.ppermute(shard, ('req', 'tp'), pairs))  1.44 us
    pallas_call x1, Pallas kernels, private(): pl.pallas_call(functools.partial(private_kernel, unit, chunk_rows, node_c...  1.06 us
  transfers between devices with their start and end apart: 8, of which 3 were waited for; matrix products, arithmetic and copies ran while one was open for 0% of the time, Pallas kernels for 22%

profile of v3, /device:TPU:0, one launch (start us, length us, event | category | flops | bytes accessed | tf_op | source)
XLA Modules:
  0.0 28.5 jit_solution(3559706971270859988)
XLA Ops:
  0.6 0.0 copy-start.1
  0.6 0.5 %collective-permute-start.6 = (bf16[512,2048]{1,0:T(8,128)(2,1)}, bf16[512,2048]{1,0:T(8,128)(2,1)S(1)}, u32[]{:S(2)}, u32[]{:S(2)}) collective-permute-start(bf16[512,2048]{1,0:T(8,128)(2,1)} %weight_hbm.1), channel_id=1, source_target_pairs={{0,1},{1,0},{2,3},{3,2},{4,5},{5,4},{6,7},{7,6},{8,9},{9,8},{10,11... | collective-permute-start | bytes 6291464 | tf_op jit(solution)/shard_map/ppermute | solution.py:34
  1.2 5.6 %collective-permute-start.1 = (bf16[2,32,256]{2,1,0:T(8,128)(2,1)}, bf16[2,32,256]{2,1,0:T(8,128)(2,1)S(1)}, u32[]{:S(2)}, u32[]{:S(2)}) collective-permute-start(bf16[2,32,256]{2,1,0:T(8,128)(2,1)} %shard_hbm.1), channel_id=1, source_target_pairs={{0,28},{1,21},{2,30},{3,23},{4,24},{5,17},{6,26},{7,19},{8,20},{9,... | collective-permute-start | bytes 98312 | tf_op jit(solution)/shard_map/ppermute | solution.py:25
  6.8 0.2 collective-permute-start.2
  7.0 0.4 %collective-permute-start.3 = (bf16[2,32,256]{2,1,0:T(8,128)(2,1)}, bf16[2,32,256]{2,1,0:T(8,128)(2,1)S(1)}, u32[]{:S(2)}, u32[]{:S(2)}) collective-permute-start(bf16[2,32,256]{2,1,0:T(8,128)(2,1)} %shard_hbm.1), channel_id=1, source_target_pairs={{0,4},{1,13},{2,6},{3,15},{4,0},{5,9},{6,2},{7,11},{8,12},{9,5},{1... | collective-permute-start | bytes 98312 | tf_op jit(solution)/shard_map/ppermute | solution.py:25
  7.4 0.7 %collective-permute-start.4 = (bf16[2,32,256]{2,1,0:T(8,128)(2,1)}, bf16[2,32,256]{2,1,0:T(8,128)(2,1)S(1)}, u32[]{:S(2)}, u32[]{:S(2)}) collective-permute-start(bf16[2,32,256]{2,1,0:T(8,128)(2,1)} %shard_hbm.1), channel_id=1, source_target_pairs={{1,9},{3,11},{5,13},{7,15},{9,1},{11,3},{13,5},{15,7},{17,25},{19,... | collective-permute-start | bytes 98312 | tf_op jit(solution)/shard_map/ppermute | solution.py:25
  8.1 1.9 %load.1 = (f32[128,64]{1,0:T(8,128)S(1)}, f32[2,8,256]{2,1,0:T(8,128)S(1)}, bf16[96,512]{1,0:T(8,128)(2,1)S(1)}, bf16[128,256]{1,0:T(8,128)(2,1)S(1)}, bf16[2,25...) custom-call(s32[6,64]{1,0:T(8,128)} %parents_ref.1, s32[6]{0:T(128)} %length_ref.1, ...), custom_call_target="tpu_custom_call" | custom-call | flops 100000000 | bytes 2000000 | tf_op jit(solution)/shard_map/load/pallas_call | solution.py:186
  10.0 0.0 collective-permute-done.1
  10.0 0.0 copy-done.1
  10.0 1.3 %collective-permute-start = (bf16[384,512]{1,0:T(8,128)(2,1)S(1)}, bf16[384,512]{1,0:T(8,128)(2,1)S(1)}, u32[]{:S(2)}, u32[]{:S(2)}) collective-permute-start(bf16[384,512]{1,0:T(8,128)(2,1)S(1)} %copy-done.1), channel_id=1, source_target_pairs={{0,1},{1,0},{2,3},{3,2},{4,5},{5,4},{6,7},{7,6},{8,9},{9,8},{10,11... | collective-permute-start | bytes 1179656 | tf_op jit(solution)/shard_map/ppermute | solution.py:34
  11.3 1.4 %collective-permute-done.2 = bf16[2,32,256]{2,1,0:T(8,128)(2,1)S(1)} collective-permute-done((bf16[2,32,256]{2,1,0:T(8,128)(2,1)}, bf16[2,32,256]{2,1,0:T(8,128)(2,1)S(1)}, u32[]{:S(2)}, u32[]{:S(2)}) %collective-permute-start.2) | collective-permute-done | bytes 32800 | tf_op jit(solution)/shard_map/ppermute | solution.py:25
  12.7 0.0 collective-permute-done.3
  12.7 0.0 collective-permute-done.4
  12.8 0.1 collective-permute-start.5
  12.8 0.0 collective-permute-done.other_ref
  12.9 1.1 %private.1.state_ref = f32[768,512]{1,0:T(8,128)S(1)} custom-call(f32[128,64]{1,0:T(8,128)S(1)} %get-tuple-element.23.bias_ref, f32[2,8,256]{2,1,0:T(8,128)S(1)} %get-tuple-element.24.notes_ref, bf16[96,512]{1,0:T(8,128)(2,1)S(1)} %get-tuple-element.22.own_ref, bf16[128,256]{1,0:T(8,128)(2,1)S(1)} %get-tuple-element.25.tree_ref, ...), custom_call_target="tpu_custom_call" | custom-call | flops 300000000 | bytes 500000 | tf_op jit(solution)/shard_map/private/pallas_call | solution.py:215
  13.9 0.3 collective-permute-done.5.rest_2_
  14.2 0.0 collective-permute-done.6.rest_4_
  14.2 0.0 copy-start
  14.2 0.0 copy-start.2
  14.2 0.0 copy-start.3
  14.2 0.0 copy-start.4
  14.2 0.0 copy-start.5
  14.2 0.0 copy-start.6
  14.2 2.1 %far_chunk.1 = bf16[96,2048]{1,0:T(8,128)(2,1)S(1)} custom-call(bf16[96,512]{1,0:T(8,128)(2,1)S(1)} %get-tuple-element.22.own_ref, bf16[384,512]{1,0:T(8,128)(2,1)S(1)} %collective-permute-done.other_ref, f32[768,512]{1,0:T(8,128)S(1)} %private.1.state_ref, bf16[2,32,256]{2,1,0:T(8,128)(2,1)S(1)} %get-tuple-element.15.rest_0_, ...), custom_call_target="tpu_custom_call" | custom-call | flops 500000000 | bytes 1000000 | tf_op jit(solution)/shard_map/far_chunk/pallas_call | solution.py:293
  16.3 1.5 %collective-permute-start.7 = (bf16[96,2048]{1,0:T(8,128)(2,1)S(1)}, bf16[96,2048]{1,0:T(8,128)(2,1)S(1)}, u32[]{:S(2)}, u32[]{:S(2)}) collective-permute-start(bf16[96,2048]{1,0:T(8,128)(2,1)S(1)} %far_chunk.1), channel_id=1, source_target_pairs={{0,2},{1,3},{2,0},{3,1},{4,6},{5,7},{6,4},{7,5},{8,10},{9,11},{10,... | collective-permute-start | bytes 1179656 | tf_op jit(solution)/shard_map/ppermute | solution.py:329
  17.9 0.0 copy-done
  17.9 0.0 copy-done.2
  17.9 0.0 copy-done.3
  17.9 0.0 copy-done.4
  17.9 0.0 copy-done.5
  17.9 0.0 copy-done.6
  17.9 3.4 %near_chunk.1 = (f32[96,2048]{1,0:T(8,128)S(1)}, bf16[6,8,256]{2,1,0:T(8,128)(2,1)}) custom-call(s32[6]{0:T(128)S(1)} %copy-done.5, s32[6]{0:T(128)S(1)} %copy-done.6, bf16[384,512]{1,0:T(8,128)(2,1)S(1)} %copy-done.1, bf16[384,512]{1,0:T(8,128)(2,1)S(1)} %collective-permute-done.other_ref, s32[6,64]{1,0:T(8,128)S(1)} %copy-done.3, s32[6,8]{1,0:T(8,128)S(1)} %copy-done.4, ...), custom_call_target="tpu_custom_call" | custom-call | flops 500000000 | bytes 1000000 | tf_op jit(solution)/shard_map/near_chunk/pallas_call | solution.py:293
  21.3 6.3 %collective-permute-done.7 = bf16[96,2048]{1,0:T(8,128)(2,1)S(1)} collective-permute-done((bf16[96,2048]{1,0:T(8,128)(2,1)S(1)}, bf16[96,2048]{1,0:T(8,128)(2,1)S(1)}, u32[]{:S(2)}, u32[]{:S(2)}) %collective-permute-start.7) | collective-permute-done | bytes 393248 | tf_op jit(solution)/shard_map/ppermute | solution.py:329
  27.6 0.8 %add_convert_fusion = bf16[96,2048]{1,0:T(8,128)(2,1)} fusion(f32[96,2048]{1,0:T(8,128)S(1)} %get-tuple-element.21, bf16[96,2048]{1,0:T(8,128)(2,1)S(1)} %collective-permute-done.7), kind=kLoop, calls=%fused_computation | loop fusion | flops 589824 | bytes 1572864 | tf_op jit(solution)/shard_map/convert_element_type | solution.py:336
  (4 shorter events, 0.0 us)
Async XLA Ops:
  0.6 9.4 %copy-start.1 = (bf16[384,512]{1,0:T(8,128)(2,1)S(1)}, bf16[384,512]{1,0:T(8,128)(2,1)}, u32[]{:S(2)}) copy-start(bf16[384,512]{1,0:T(8,128)(2,1)} %own_ref.1) | copy-start | bytes 1179652
  0.6 13.5 %collective-permute-start.6 = (bf16[512,2048]{1,0:T(8,128)(2,1)}, bf16[512,2048]{1,0:T(8,128)(2,1)S(1)}, u32[]{:S(2)}, u32[]{:S(2)}) collective-permute-start(bf16[512,2048]{1,0:T(8,128)(2,1)} %weight_hbm.1), channel_id=1, source_target_pairs={{0,1},{1,0},{2,3},{3,2},{4,5},{5,4},{6,7},{7,6},{8,9},{9,8},{10,11... | collective-permute-start | bytes 6291464 | tf_op jit(solution)/shard_map/ppermute | solution.py:34
  1.2 8.8 %collective-permute-start.1 = (bf16[2,32,256]{2,1,0:T(8,128)(2,1)}, bf16[2,32,256]{2,1,0:T(8,128)(2,1)S(1)}, u32[]{:S(2)}, u32[]{:S(2)}) collective-permute-start(bf16[2,32,256]{2,1,0:T(8,128)(2,1)} %shard_hbm.1), channel_id=1, source_target_pairs={{0,28},{1,21},{2,30},{3,23},{4,24},{5,17},{6,26},{7,19},{8,20},{9,... | collective-permute-start | bytes 98312 | tf_op jit(solution)/shard_map/ppermute | solution.py:25
  6.8 5.9 %collective-permute-start.2 = (bf16[2,32,256]{2,1,0:T(8,128)(2,1)}, bf16[2,32,256]{2,1,0:T(8,128)(2,1)S(1)}, u32[]{:S(2)}, u32[]{:S(2)}) collective-permute-start(bf16[2,32,256]{2,1,0:T(8,128)(2,1)} %shard_hbm.1), channel_id=1, source_target_pairs={{0,24},{1,17},{2,26},{3,19},{4,28},{5,21},{6,30},{7,23},{8,16},{9,... | collective-permute-start | bytes 98312 | tf_op jit(solution)/shard_map/ppermute | solution.py:25
  7.0 5.7 %collective-permute-start.3 = (bf16[2,32,256]{2,1,0:T(8,128)(2,1)}, bf16[2,32,256]{2,1,0:T(8,128)(2,1)S(1)}, u32[]{:S(2)}, u32[]{:S(2)}) collective-permute-start(bf16[2,32,256]{2,1,0:T(8,128)(2,1)} %shard_hbm.1), channel_id=1, source_target_pairs={{0,4},{1,13},{2,6},{3,15},{4,0},{5,9},{6,2},{7,11},{8,12},{9,5},{1... | collective-permute-start | bytes 98312 | tf_op jit(solution)/shard_map/ppermute | solution.py:25
  7.4 5.3 %collective-permute-start.4 = (bf16[2,32,256]{2,1,0:T(8,128)(2,1)}, bf16[2,32,256]{2,1,0:T(8,128)(2,1)S(1)}, u32[]{:S(2)}, u32[]{:S(2)}) collective-permute-start(bf16[2,32,256]{2,1,0:T(8,128)(2,1)} %shard_hbm.1), channel_id=1, source_target_pairs={{1,9},{3,11},{5,13},{7,15},{9,1},{11,3},{13,5},{15,7},{17,25},{19,... | collective-permute-start | bytes 98312 | tf_op jit(solution)/shard_map/ppermute | solution.py:25
  10.0 2.8 %collective-permute-start = (bf16[384,512]{1,0:T(8,128)(2,1)S(1)}, bf16[384,512]{1,0:T(8,128)(2,1)S(1)}, u32[]{:S(2)}, u32[]{:S(2)}) collective-permute-start(bf16[384,512]{1,0:T(8,128)(2,1)S(1)} %copy-done.1), channel_id=1, source_target_pairs={{0,1},{1,0},{2,3},{3,2},{4,5},{5,4},{6,7},{7,6},{8,9},{9,8},{10,11... | collective-permute-start | bytes 1179656 | tf_op jit(solution)/shard_map/ppermute | solution.py:34
  12.8 1.4 %collective-permute-start.5 = (bf16[8,32,256]{2,1,0:T(8,128)(2,1)S(1)}, bf16[8,32,256]{2,1,0:T(8,128)(2,1)S(1)}, u32[]{:S(2)}, u32[]{:S(2)}) collective-permute-start(bf16[8,32,256]{2,1,0:T(8,128)(2,1)S(1)} %constant_dynamic-update-slice_fusion.rest_1_), channel_id=1, source_target_pairs={{0,1},{1,0},{2,3},{3,2},{4,5},{5,4},{6,7},{7,6},{8,9},{9,8},{10,11... | collective-permute-start | bytes 393224 | tf_op jit(solution)/shard_map/ppermute | solution.py:34
  14.2 3.7 %copy-start = (bf16[6,256,256]{2,1,0:T(8,128)(2,1)S(1)}, bf16[6,256,256]{2,1,0:T(8,128)(2,1)}, u32[]{:S(2)}) copy-start(bf16[6,256,256]{2,1,0:T(8,128)(2,1)} %suffix_ref.1) | copy-start | bytes 2359300
  14.2 3.7 %copy-start.2 = (bf16[384,256]{1,0:T(8,128)(2,1)S(1)}, bf16[384,256]{1,0:T(8,128)(2,1)}, u32[]{:S(2)}) copy-start(bf16[384,256]{1,0:T(8,128)(2,1)} %tree_ref.1) | copy-start | bytes 589828
  14.2 3.7 %copy-start.3 = (s32[6,64]{1,0:T(8,128)S(1)}, s32[6,64]{1,0:T(8,128)}, u32[]{:S(2)}) copy-start(s32[6,64]{1,0:T(8,128)} %parents_ref.1) | copy-start | bytes 4612
  14.2 3.7 %copy-start.4 = (s32[6,8]{1,0:T(8,128)S(1)}, s32[6,8]{1,0:T(8,128)}, u32[]{:S(2)}) copy-start(s32[6,8]{1,0:T(8,128)} %accepted_ref.1) | copy-start | bytes 580
  14.2 3.7 %copy-start.5 = (s32[6]{0:T(128)S(1)}, s32[6]{0:T(128)}, u32[]{:S(2)}) copy-start(s32[6]{0:T(128)} %length_ref.1) | copy-start | bytes 76
  14.2 3.7 %copy-start.6 = (s32[6]{0:T(128)S(1)}, s32[6]{0:T(128)}, u32[]{:S(2)}) copy-start(s32[6]{0:T(128)} %group_ref.1) | copy-start | bytes 76
  16.3 11.3 %collective-permute-start.7 = (bf16[96,2048]{1,0:T(8,128)(2,1)S(1)}, bf16[96,2048]{1,0:T(8,128)(2,1)S(1)}, u32[]{:S(2)}, u32[]{:S(2)}) collective-permute-start(bf16[96,2048]{1,0:T(8,128)(2,1)S(1)} %far_chunk.1), channel_id=1, source_target_pairs={{0,2},{1,3},{2,0},{3,1},{4,6},{5,7},{6,4},{7,5},{8,10},{9,11},{10,... | collective-permute-start | bytes 1179656 | tf_op jit(solution)/shard_map/ppermute | solution.py:329

commit v4 on v3

--- a/solution.py
+++ b/solution.py
@@ -10,12 +10,13 @@
 
 neg_large = -1e30
 vmem_bytes = 12 * 1024 * 1024
+fetches = 4
 
 
 def fetch_shards(shard, req_count, tp_count):
-    masks = ((7, 6, 1), (5, 4, 3, 2))
+    masks = ((7, 4, 3), (6, 5, 2, 1))
     arrived = []
-    for step in range(4):
+    for step in range(fetches):
         pairs = []
         for r in range(req_count):
             for t in range(tp_count):
@@ -65,14 +66,18 @@
     ]
 
 
-def prompt_of(pieces, group):
-    if len(pieces) == 1:
-        return pieces[0][group]
-    shard, fetched, swapped = pieces
+def prompt_of(prompts, group):
+    return functools.reduce(lambda held, g: jnp.where(group == g, prompts[g], held), range(1, len(prompts)), prompts[0])
+
+
+def kept_prompts(shard, fetched):
     groups = shard.shape[0]
-    places = range(group, fetched.shape[0], groups)
-    kept = [shard[group]] + [ref[place] for ref in (fetched, swapped) for place in places[:-1]]
-    return jnp.concatenate([*kept, fetched[places[-1]] + swapped[places[-1]]], axis=0)
+    return [jnp.concatenate([shard[g]] + [fetched[k + g] for k in range(0, fetched.shape[0] - groups, groups)], axis=0) for g in range(groups)]
+
+
+def swapped_prompts(fetched, swapped, groups):
+    last = swapped.shape[0] - groups
+    return [jnp.concatenate([swapped[k + g] for k in range(0, last, groups)] + [fetched[last + g] + swapped[last + g]], axis=0) for g in range(groups)]
 
 
 def project(attended_ref, weight_own_ref, weight_other_ref, out_ref):
@@ -150,9 +155,11 @@
         copy.wait()
 
 
-def private_kernel(unit, chunk_rows, node_count, requests, bias_ref, notes_ref, own_ref, tree_ref, suffix_ref, other_ref, state_ref):
+def private_kernel(unit, chunk_rows, node_count, requests, bias_ref, notes_ref, own_ref, tree_ref, suffix_ref, other_ref, *rest):
     head_size = tree_ref.shape[1] // 2
     touched = suffix_ref.shape[0]
+    *parts, state_ref = rest
+    prompts = kept_prompts(*parts) if parts else []
     start = pl.multiple_of(first_row(chunk_rows, 2), unit)
     base = first_request(chunk_rows, 2, node_count, requests, touched)
     for number in range(chunk_rows // unit):
@@ -163,11 +170,16 @@
         )
         bias = bias_ref[pl.ds(pl.multiple_of(row - base * node_count, unit), unit), :]
         tree = tree_ref[pl.ds(pl.multiple_of(place * node_count, node_count), node_count), :]
-        blocks = private_blocks(query, bias, notes_ref[place, :1, :], tree, suffix_ref[place])
+        notes = notes_ref[place]
+        group = notes[1:2]
+        blocks = private_blocks(query, bias, notes[:1], tree, suffix_ref[place])
+        if prompts:
+            prompt = prompt_of(prompts, group[:, : 2 * head_size])
+            blocks.append((score(query, prompt[:, :head_size]), prompt[:, head_size:]))
         largest, total, result = absorb(blocks, log2_rate(head_size))
         lanes = result.shape
         rows = slice(number * lanes[0], (number + 1) * lanes[0])
-        for spot, value in enumerate((result, largest, total, notes_ref[place, 1:2, :head_size])):
+        for spot, value in enumerate((result, largest, total, group[:, :head_size])):
             state_ref[rows, spot * head_size : (spot + 1) * head_size] = jnp.broadcast_to(value, lanes)
 
 
@@ -208,28 +220,27 @@
     )(*sources)
 
 
-def private(unit, chunk_rows, node_count, requests, loaded, other):
+def private(unit, chunk_rows, node_count, requests, loaded, other, parts):
     bias, notes, own, tree, suffix = loaded
     head_size = tree.shape[1] // 2
     state_rows = chunk_rows * 2 * (own.shape[1] // head_size)
     return pl.pallas_call(
         functools.partial(private_kernel, unit, chunk_rows, node_count, requests),
-        in_specs=[in_vmem()] * 6,
+        in_specs=[in_vmem()] * (6 + len(parts)),
         out_specs=in_vmem(),
         out_shape=jax.ShapeDtypeStruct((state_rows, 4 * head_size), jnp.float32),
         compiler_params=pltpu.CompilerParams(vmem_limit_bytes=vmem_bytes),
         name="private",
         cost_estimate=pl.CostEstimate(flops=300_000_000, bytes_accessed=500_000, transcendentals=0),
-    )(*loaded, other)
-
-
-def far_kernel(unit, piece_count, own_ref, other_ref, state_ref, *rest):
-    pieces, (weight_own_ref, weight_other_ref, out_ref, attended_ref) = rest[:piece_count], rest[piece_count:]
+    )(*loaded, other, *parts)
+
+
+def far_kernel(unit, part_count, own_ref, other_ref, state_ref, *rest):
+    parts, (weight_own_ref, weight_other_ref, out_ref, attended_ref) = rest[:part_count], rest[part_count:]
     chunk_rows = out_ref.shape[0]
     head_size = state_ref.shape[1] // 4
     rate = log2_rate(head_size)
-    group_count = pieces[0].shape[0]
-    prompts = [prompt_of(pieces, g) for g in range(group_count)]
+    prompts = swapped_prompts(parts[0], parts[1], parts[0].shape[0] // fetches) if part_count == 2 else [parts[0][g] for g in range(parts[0].shape[0])]
     start = first_row(chunk_rows, 2)
     for number in range(chunk_rows // unit):
         row = pl.multiple_of(start + number * unit, unit)
@@ -237,16 +248,14 @@
             [stacked_heads(own_ref, number * unit, unit, head_size), stacked_heads(other_ref, row, unit, head_size)], axis=0
         )
         rows = slice(number * query.shape[0], (number + 1) * query.shape[0])
-        before, largest, total, group = (state_ref[rows, place * head_size : (place + 1) * head_size] for place in range(4))
-        prompt = prompts[0]
-        for g in range(1, group_count):
-            mine = jnp.broadcast_to(group[:1, :1], prompt.shape) == g
-            prompt = jnp.where(mine, prompts[g], prompt)
+        before, largest, total, group = (state_ref[rows, spot * head_size : (spot + 1) * head_size] for spot in range(4))
+        prompt = prompt_of(prompts, jnp.concatenate([group[:1], group[:1]], axis=1))
         scores = score(query, prompt[:, :head_size])
-        top = jnp.maximum(largest[:, :1], jnp.max(scores, axis=1, keepdims=True))
-        weight = jnp.exp2((scores - top) * rate)
-        fade = jnp.exp2((largest[:, :1] - top) * rate)
-        total = total[:, :1] * fade + jnp.sum(weight, axis=1, keepdims=True)
+        top = jnp.maximum(largest, jnp.max(scores, axis=1, keepdims=True))
+        fade = jnp.exp2((largest - top) * rate)
+        width = scores.shape[1] // head_size
+        weight = jnp.exp2((scores - (top if width == 1 else jnp.concatenate([top] * width, axis=1))) * rate)
+        total = total * fade + jnp.sum(weight, axis=1, keepdims=True)
         result = before * fade + jnp.dot(weight.astype(jnp.bfloat16), prompt[:, head_size:], preferred_element_type=jnp.float32)
         put_heads(attended_ref, number, unit, (result / total).astype(jnp.bfloat16))
     project(attended_ref, weight_own_ref, weight_other_ref, out_ref)
@@ -271,7 +280,11 @@
             (((0,), (0,)), ((), ())),
             preferred_element_type=jnp.float32,
         ).astype(jnp.bfloat16)
-    prompts = [prompt_of(pieces, g) for g in range(pieces[0].shape[0])]
+    if piece_count == 3:
+        kept = kept_prompts(pieces[0], pieces[1])
+        prompts = [jnp.concatenate(pair, axis=0) for pair in zip(kept, swapped_prompts(pieces[1], pieces[2], len(kept)))]
+    else:
+        prompts = [pieces[0][g] for g in range(pieces[0].shape[0])]
     slot = lax.broadcasted_iota(jnp.int32, (1, suffix_ref.shape[1]), 1)
     start = first_row(chunk_rows, 0)
     for number in range(chunk_rows // unit):
@@ -282,7 +295,7 @@
         tree = tree_ref[pl.ds(pl.multiple_of(request * node_count, node_count), node_count), :]
         blocks = private_blocks(query, bias_ref[pl.ds(row, unit), :], used, tree, suffix_ref[request])
         group = group_ref[request]
-        prompt = functools.reduce(lambda held, g: jnp.where(group == g, prompts[g], held), range(1, len(prompts)), prompts[0])
+        prompt = prompt_of(prompts, group)
         blocks.append((score(query, prompt[:, :head_size]), prompt[:, head_size:]))
         largest, total, result = absorb(blocks, log2_rate(head_size))
         put_heads(attended_ref, number, unit, (result / total).astype(jnp.bfloat16))
@@ -314,17 +327,19 @@
         other_weight = swap_in_pair(out_weight, tp_count)
     requests, node_count = parents.shape
     *loaded, shard, own_weight = load(unit, chunk_rows, parents, suffix_len, group_ids, queries, tree_kv, suffix_kv, prompt_kv, out_weight)
-    state = private(unit, chunk_rows, node_count, requests, loaded, other_queries)
     if fetched is None:
         pieces = [lax.all_gather(prompt_kv, "req", axis=1, tiled=True)]
+        state = private(unit, chunk_rows, node_count, requests, loaded, other_queries, [])
     else:
         joined = jnp.concatenate([after(piece, shard) for piece in fetched], axis=0)
         pieces = [shard, joined, swap_in_pair(joined, tp_count)]
+        state = private(unit, chunk_rows, node_count, requests, loaded, other_queries, pieces[:2])
+    parts = pieces[-2:]
     weights = (own_weight, other_weight)
     chunk_shape = (chunk_rows, out_weight.shape[1])
     (far,) = chunk(
-        functools.partial(far_kernel, unit, len(pieces)), "far_chunk", [jax.ShapeDtypeStruct(chunk_shape, jnp.bfloat16)],
-        (), (loaded[2], other_queries, state, *pieces), weights, ()
+        functools.partial(far_kernel, unit, len(parts)), "far_chunk", [jax.ShapeDtypeStruct(chunk_shape, jnp.bfloat16)],
+        (), (loaded[2], other_queries, state, *parts), weights, ()
     )
     arrived = lax.ppermute(far, "tp", [(t, t ^ 2) for t in range(tp_count)])
     near, path_cache = chunk(

time: 28.6 us -> 27.9 us (0.976)
  waiting for transfers between devices: 8.05 us -> 7.55 us
  Pallas kernels: 8.42 us -> 7.97 us
    ppermute x4, waiting for transfers between devices: 1.44 us -> 0.79 us  [fetch_shards(): arrived.append(lax.ppermute(shard, ('req', 'tp'), pairs))]
    pallas_call x2, Pallas kernels: 5.48 us -> 4.88 us  [chunk(): pl.pallas_call(kernel, in_specs=[in_smem()] * len(scalars) + [in_vmem()]...]
  transfers between devices with their start and end apart: 8 -> 8, of which waited for: 3 -> 4; matrix products, arithmetic and copies ran while one was open for 0% -> 0% of each run, Pallas kernels for 22% -> 23%
where the time goes in v4:
time: 27.9 us; the launch traced here: 27.7 us
  starting transfers between devices  10.5 us (38%)
  Pallas kernels  7.97 us (29%)
  waiting for transfers between devices  7.55 us (27%)
  other arithmetic  0.82 us (3%)
  between operations  0.79 us (3%)
    ppermute x4, starting transfers between devices, fetch_shards(): arrived.append(lax.ppermute(shard, ('req', 'tp'), pairs))  6.92 us
    ppermute x1, waiting for transfers between devices, local(): arrived = lax.ppermute(far, 'tp', [(t, t ^ 2) for t in range(tp_count)])  6.44 us
    pallas_call x2, Pallas kernels, chunk(): pl.pallas_call(kernel, in_specs=[in_smem()] * len(scalars) + [in_vmem()]...  4.88 us
    ppermute x3, starting transfers between devices, swap_in_pair(): return lax.ppermute(array, 'tp', [(t, t ^ 1) for t in range(tp_count)])  2.06 us
    pallas_call x1, Pallas kernels, load(): pl.pallas_call(functools.partial(load_kernel, chunk_rows), in_specs=[pl.B...  1.88 us
    ppermute x1, starting transfers between devices, local(): arrived = lax.ppermute(far, 'tp', [(t, t ^ 2) for t in range(tp_count)])  1.56 us
    pallas_call x1, Pallas kernels, private(): pl.pallas_call(functools.partial(private_kernel, unit, chunk_rows, node_c...  1.21 us
    convert_element_type x1, other arithmetic, local(): layer_output = (near + arrived.astype(jnp.float32)).astype(jnp.bfloat16)  0.82 us
  transfers between devices with their start and end apart: 8, of which 4 were waited for; matrix products, arithmetic and copies ran while one was open for 0% of the time, Pallas kernels for 23%

profile of v4, /device:TPU:0, one launch (start us, length us, event | category | flops | bytes accessed | tf_op | source)
XLA Modules:
  0.0 27.7 jit_solution(18324051544979136764)
XLA Ops:
  0.6 0.0 copy-start.1
  0.6 0.5 %collective-permute-start.6 = (bf16[512,2048]{1,0:T(8,128)(2,1)}, bf16[512,2048]{1,0:T(8,128)(2,1)S(1)}, u32[]{:S(2)}, u32[]{:S(2)}) collective-permute-start(bf16[512,2048]{1,0:T(8,128)(2,1)} %weight_hbm.1), channel_id=1, source_target_pairs={{0,1},{1,0},{2,3},{3,2},{4,5},{5,4},{6,7},{7,6},{8,9},{9,8},{10,11... | collective-permute-start | bytes 6291464 | tf_op jit(solution)/shard_map/ppermute | solution.py:35
  1.2 5.6 %collective-permute-start.1 = (bf16[2,32,256]{2,1,0:T(8,128)(2,1)}, bf16[2,32,256]{2,1,0:T(8,128)(2,1)S(1)}, u32[]{:S(2)}, u32[]{:S(2)}) collective-permute-start(bf16[2,32,256]{2,1,0:T(8,128)(2,1)} %shard_hbm.1), channel_id=1, source_target_pairs={{0,28},{1,25},{2,30},{3,27},{4,24},{5,29},{6,26},{7,31},{8,20},{9,... | collective-permute-start | bytes 98312 | tf_op jit(solution)/shard_map/ppermute | solution.py:26
  6.8 0.0 collective-permute-start.2
  6.8 0.6 %collective-permute-start.3 = (bf16[2,32,256]{2,1,0:T(8,128)(2,1)}, bf16[2,32,256]{2,1,0:T(8,128)(2,1)S(1)}, u32[]{:S(2)}, u32[]{:S(2)}) collective-permute-start(bf16[2,32,256]{2,1,0:T(8,128)(2,1)} %shard_hbm.1), channel_id=1, source_target_pairs={{0,12},{1,9},{2,14},{3,11},{4,8},{5,13},{6,10},{7,15},{8,4},{9,1},... | collective-permute-start | bytes 98312 | tf_op jit(solution)/shard_map/ppermute | solution.py:26
  7.4 0.7 %collective-permute-start.4 = (bf16[2,32,256]{2,1,0:T(8,128)(2,1)}, bf16[2,32,256]{2,1,0:T(8,128)(2,1)S(1)}, u32[]{:S(2)}, u32[]{:S(2)}) collective-permute-start(bf16[2,32,256]{2,1,0:T(8,128)(2,1)} %shard_hbm.1), channel_id=1, source_target_pairs={{1,5},{3,7},{5,1},{7,3},{9,13},{11,15},{13,9},{15,11},{17,21},{19,... | collective-permute-start | bytes 98312 | tf_op jit(solution)/shard_map/ppermute | solution.py:26
  8.1 1.9 %load.1 = (f32[128,64]{1,0:T(8,128)S(1)}, f32[2,8,256]{2,1,0:T(8,128)S(1)}, bf16[96,512]{1,0:T(8,128)(2,1)S(1)}, bf16[128,256]{1,0:T(8,128)(2,1)S(1)}, bf16[2,25...) custom-call(s32[6,64]{1,0:T(8,128)} %parents_ref.1, s32[6]{0:T(128)} %length_ref.1, ...), custom_call_target="tpu_custom_call" | custom-call | flops 100000000 | bytes 2000000 | tf_op jit(solution)/shard_map/load/pallas_call | solution.py:198
  10.0 0.0 collective-permute-done.1
  10.0 0.0 copy-done.1
  10.0 1.3 %collective-permute-start = (bf16[384,512]{1,0:T(8,128)(2,1)S(1)}, bf16[384,512]{1,0:T(8,128)(2,1)S(1)}, u32[]{:S(2)}, u32[]{:S(2)}) collective-permute-start(bf16[384,512]{1,0:T(8,128)(2,1)S(1)} %copy-done.1), channel_id=1, source_target_pairs={{0,1},{1,0},{2,3},{3,2},{4,5},{5,4},{6,7},{7,6},{8,9},{9,8},{10,11... | collective-permute-start | bytes 1179656 | tf_op jit(solution)/shard_map/ppermute | solution.py:35
  11.3 0.5 %collective-permute-done.2 = bf16[2,32,256]{2,1,0:T(8,128)(2,1)S(1)} collective-permute-done((bf16[2,32,256]{2,1,0:T(8,128)(2,1)}, bf16[2,32,256]{2,1,0:T(8,128)(2,1)S(1)}, u32[]{:S(2)}, u32[]{:S(2)}) %collective-permute-start.2) | collective-permute-done | bytes 32800 | tf_op jit(solution)/shard_map/ppermute | solution.py:26
  11.8 0.3 %collective-permute-done.3 = bf16[2,32,256]{2,1,0:T(8,128)(2,1)S(1)} collective-permute-done((bf16[2,32,256]{2,1,0:T(8,128)(2,1)}, bf16[2,32,256]{2,1,0:T(8,128)(2,1)S(1)}, u32[]{:S(2)}, u32[]{:S(2)}) %collective-permute-start.3) | collective-permute-done | bytes 32800 | tf_op jit(solution)/shard_map/ppermute | solution.py:26
  12.1 0.0 collective-permute-done.4
  12.2 0.2 collective-permute-start.5
  12.4 0.3 %collective-permute-done.other_ref = bf16[384,512]{1,0:T(8,128)(2,1)S(1)} collective-permute-done((bf16[384,512]{1,0:T(8,128)(2,1)S(1)}, bf16[384,512]{1,0:T(8,128)(2,1)S(1)}, u32[]{:S(2)}, u32[]{:S(2)}) %collective-permute-start) | collective-permute-done | bytes 393248 | tf_op jit(solution)/shard_map/ppermute | solution.py:35
  12.7 1.2 %private.1.state_ref = f32[768,512]{1,0:T(8,128)S(1)} custom-call(f32[128,64]{1,0:T(8,128)S(1)} %get-tuple-element.23.bias_ref, f32[2,8,256]{2,1,0:T(8,128)S(1)} %get-tuple-element.24.notes_ref, bf16[96,512]{1,0:T(8,128)(2,1)S(1)} %get-tuple-element.22.own_ref, bf16[128,256]{1,0:T(8,128)(2,1)S(1)} %get-tuple-element.25.tree_ref, ...), custom_call_target="tpu_custom_call" | custom-call | flops 300000000 | bytes 500000 | tf_op jit(solution)/shard_map/private/pallas_call | solution.py:227
  13.9 0.0 collective-permute-done.5.rest_2_.rest_1_
  13.9 0.0 collective-permute-done.6.rest_4_.rest_3_
  13.9 0.0 copy-start
  13.9 0.0 copy-start.2
  13.9 0.0 copy-start.3
  14.0 0.0 copy-start.4
  14.0 0.0 copy-start.5
  14.0 0.0 copy-start.6
  14.0 1.5 %far_chunk.1 = bf16[96,2048]{1,0:T(8,128)(2,1)S(1)} custom-call(bf16[96,512]{1,0:T(8,128)(2,1)S(1)} %get-tuple-element.22.own_ref, bf16[384,512]{1,0:T(8,128)(2,1)S(1)} %collective-permute-done.other_ref, f32[768,512]{1,0:T(8,128)S(1)} %private.1.state_ref, bf16[8,32,256]{2,1,0:T(8,128)(2,1)S(1)} %constant_dynamic-update-slice_fusion.rest_1_.rest_0_, ...), custom_call_target="tpu_custom_call" | custom-call | flops 500000000 | bytes 1000000 | tf_op jit(solution)/shard_map/far_chunk/pallas_call | solution.py:306
  15.5 1.6 %collective-permute-start.7 = (bf16[96,2048]{1,0:T(8,128)(2,1)S(1)}, bf16[96,2048]{1,0:T(8,128)(2,1)S(1)}, u32[]{:S(2)}, u32[]{:S(2)}) collective-permute-start(bf16[96,2048]{1,0:T(8,128)(2,1)S(1)} %far_chunk.1), channel_id=1, source_target_pairs={{0,2},{1,3},{2,0},{3,1},{4,6},{5,7},{6,4},{7,5},{8,10},{9,11},{10,... | collective-permute-start | bytes 1179656 | tf_op jit(solution)/shard_map/ppermute | solution.py:344
  17.0 0.0 copy-done
  17.0 0.0 copy-done.2
  17.0 0.0 copy-done.3
  17.0 0.0 copy-done.4
  17.0 0.0 copy-done.5
  17.0 0.0 copy-done.6
  17.1 3.4 %near_chunk.1 = (f32[96,2048]{1,0:T(8,128)S(1)}, bf16[6,8,256]{2,1,0:T(8,128)(2,1)}) custom-call(s32[6]{0:T(128)S(1)} %copy-done.5, s32[6]{0:T(128)S(1)} %copy-done.6, bf16[384,512]{1,0:T(8,128)(2,1)S(1)} %copy-done.1, bf16[384,512]{1,0:T(8,128)(2,1)S(1)} %collective-permute-done.other_ref, s32[6,64]{1,0:T(8,128)S(1)} %copy-done.3, s32[6,8]{1,0:T(8,128)S(1)} %copy-done.4, ...), custom_call_target="tpu_custom_call" | custom-call | flops 500000000 | bytes 1000000 | tf_op jit(solution)/shard_map/near_chunk/pallas_call | solution.py:306
  20.5 6.4 %collective-permute-done.7 = bf16[96,2048]{1,0:T(8,128)(2,1)S(1)} collective-permute-done((bf16[96,2048]{1,0:T(8,128)(2,1)S(1)}, bf16[96,2048]{1,0:T(8,128)(2,1)S(1)}, u32[]{:S(2)}, u32[]{:S(2)}) %collective-permute-start.7) | collective-permute-done | bytes 393248 | tf_op jit(solution)/shard_map/ppermute | solution.py:344
  26.9 0.8 %add_convert_fusion = bf16[96,2048]{1,0:T(8,128)(2,1)} fusion(f32[96,2048]{1,0:T(8,128)S(1)} %get-tuple-element.21, bf16[96,2048]{1,0:T(8,128)(2,1)S(1)} %collective-permute-done.7), kind=kLoop, calls=%fused_computation | loop fusion | flops 589824 | bytes 1572864 | tf_op jit(solution)/shard_map/convert_element_type | solution.py:351
  (4 shorter events, 0.0 us)
Async XLA Ops:
  0.6 9.4 %copy-start.1 = (bf16[384,512]{1,0:T(8,128)(2,1)S(1)}, bf16[384,512]{1,0:T(8,128)(2,1)}, u32[]{:S(2)}) copy-start(bf16[384,512]{1,0:T(8,128)(2,1)} %own_ref.1) | copy-start | bytes 1179652
  0.6 13.3 %collective-permute-start.6 = (bf16[512,2048]{1,0:T(8,128)(2,1)}, bf16[512,2048]{1,0:T(8,128)(2,1)S(1)}, u32[]{:S(2)}, u32[]{:S(2)}) collective-permute-start(bf16[512,2048]{1,0:T(8,128)(2,1)} %weight_hbm.1), channel_id=1, source_target_pairs={{0,1},{1,0},{2,3},{3,2},{4,5},{5,4},{6,7},{7,6},{8,9},{9,8},{10,11... | collective-permute-start | bytes 6291464 | tf_op jit(solution)/shard_map/ppermute | solution.py:35
  1.2 8.8 %collective-permute-start.1 = (bf16[2,32,256]{2,1,0:T(8,128)(2,1)}, bf16[2,32,256]{2,1,0:T(8,128)(2,1)S(1)}, u32[]{:S(2)}, u32[]{:S(2)}) collective-permute-start(bf16[2,32,256]{2,1,0:T(8,128)(2,1)} %shard_hbm.1), channel_id=1, source_target_pairs={{0,28},{1,25},{2,30},{3,27},{4,24},{5,29},{6,26},{7,31},{8,20},{9,... | collective-permute-start | bytes 98312 | tf_op jit(solution)/shard_map/ppermute | solution.py:26
  6.8 5.0 %collective-permute-start.2 = (bf16[2,32,256]{2,1,0:T(8,128)(2,1)}, bf16[2,32,256]{2,1,0:T(8,128)(2,1)S(1)}, u32[]{:S(2)}, u32[]{:S(2)}) collective-permute-start(bf16[2,32,256]{2,1,0:T(8,128)(2,1)} %shard_hbm.1), channel_id=1, source_target_pairs={{0,16},{1,21},{2,18},{3,23},{4,20},{5,17},{6,22},{7,19},{8,24},{9,... | collective-permute-start | bytes 98312 | tf_op jit(solution)/shard_map/ppermute | solution.py:26
  6.8 5.3 %collective-permute-start.3 = (bf16[2,32,256]{2,1,0:T(8,128)(2,1)}, bf16[2,32,256]{2,1,0:T(8,128)(2,1)S(1)}, u32[]{:S(2)}, u32[]{:S(2)}) collective-permute-start(bf16[2,32,256]{2,1,0:T(8,128)(2,1)} %shard_hbm.1), channel_id=1, source_target_pairs={{0,12},{1,9},{2,14},{3,11},{4,8},{5,13},{6,10},{7,15},{8,4},{9,1},... | collective-permute-start | bytes 98312 | tf_op jit(solution)/shard_map/ppermute | solution.py:26
  7.4 4.7 %collective-permute-start.4 = (bf16[2,32,256]{2,1,0:T(8,128)(2,1)}, bf16[2,32,256]{2,1,0:T(8,128)(2,1)S(1)}, u32[]{:S(2)}, u32[]{:S(2)}) collective-permute-start(bf16[2,32,256]{2,1,0:T(8,128)(2,1)} %shard_hbm.1), channel_id=1, source_target_pairs={{1,5},{3,7},{5,1},{7,3},{9,13},{11,15},{13,9},{15,11},{17,21},{19,... | collective-permute-start | bytes 98312 | tf_op jit(solution)/shard_map/ppermute | solution.py:26
  10.0 2.7 %collective-permute-start = (bf16[384,512]{1,0:T(8,128)(2,1)S(1)}, bf16[384,512]{1,0:T(8,128)(2,1)S(1)}, u32[]{:S(2)}, u32[]{:S(2)}) collective-permute-start(bf16[384,512]{1,0:T(8,128)(2,1)S(1)} %copy-done.1), channel_id=1, source_target_pairs={{0,1},{1,0},{2,3},{3,2},{4,5},{5,4},{6,7},{7,6},{8,9},{9,8},{10,11... | collective-permute-start | bytes 1179656 | tf_op jit(solution)/shard_map/ppermute | solution.py:35
  12.2 1.7 %collective-permute-start.5 = (bf16[8,32,256]{2,1,0:T(8,128)(2,1)S(1)}, bf16[8,32,256]{2,1,0:T(8,128)(2,1)S(1)}, u32[]{:S(2)}, u32[]{:S(2)}) collective-permute-start(bf16[8,32,256]{2,1,0:T(8,128)(2,1)S(1)} %constant_dynamic-update-slice_fusion.rest_1_.rest_0_), channel_id=1, source_target_pairs={{0,1},{1,0},{2,3},{3,2},{4,5},{5,4},{6,7},{7,6},{8,9},{9,8},{10,11... | collective-permute-start | bytes 393224 | tf_op jit(solution)/shard_map/ppermute | solution.py:35
  13.9 3.1 %copy-start = (bf16[6,256,256]{2,1,0:T(8,128)(2,1)S(1)}, bf16[6,256,256]{2,1,0:T(8,128)(2,1)}, u32[]{:S(2)}) copy-start(bf16[6,256,256]{2,1,0:T(8,128)(2,1)} %suffix_ref.1) | copy-start | bytes 2359300
  13.9 3.1 %copy-start.2 = (bf16[384,256]{1,0:T(8,128)(2,1)S(1)}, bf16[384,256]{1,0:T(8,128)(2,1)}, u32[]{:S(2)}) copy-start(bf16[384,256]{1,0:T(8,128)(2,1)} %tree_ref.1) | copy-start | bytes 589828
  13.9 3.1 %copy-start.3 = (s32[6,64]{1,0:T(8,128)S(1)}, s32[6,64]{1,0:T(8,128)}, u32[]{:S(2)}) copy-start(s32[6,64]{1,0:T(8,128)} %parents_ref.1) | copy-start | bytes 4612
  14.0 3.1 %copy-start.4 = (s32[6,8]{1,0:T(8,128)S(1)}, s32[6,8]{1,0:T(8,128)}, u32[]{:S(2)}) copy-start(s32[6,8]{1,0:T(8,128)} %accepted_ref.1) | copy-start | bytes 580
  14.0 3.1 %copy-start.5 = (s32[6]{0:T(128)S(1)}, s32[6]{0:T(128)}, u32[]{:S(2)}) copy-start(s32[6]{0:T(128)} %length_ref.1) | copy-start | bytes 76
  14.0 3.1 %copy-start.6 = (s32[6]{0:T(128)S(1)}, s32[6]{0:T(128)}, u32[]{:S(2)}) copy-start(s32[6]{0:T(128)} %group_ref.1) | copy-start | bytes 76
  15.5 11.4 %collective-permute-start.7 = (bf16[96,2048]{1,0:T(8,128)(2,1)S(1)}, bf16[96,2048]{1,0:T(8,128)(2,1)S(1)}, u32[]{:S(2)}, u32[]{:S(2)}) collective-permute-start(bf16[96,2048]{1,0:T(8,128)(2,1)S(1)} %far_chunk.1), channel_id=1, source_target_pairs={{0,2},{1,3},{2,0},{3,1},{4,6},{5,7},{6,4},{7,5},{8,10},{9,11},{10,... | collective-permute-start | bytes 1179656 | tf_op jit(solution)/shard_map/ppermute | solution.py:344

commit v5 on v4

--- a/solution.py
+++ b/solution.py
@@ -27,6 +27,23 @@
     return arrived
 
 
+def touch_kernel(in_ref, out_ref):
+    del in_ref, out_ref
+
+
+def touched(array):
+    return pl.pallas_call(
+        touch_kernel,
+        in_specs=[in_vmem()],
+        out_specs=in_vmem(),
+        out_shape=jax.ShapeDtypeStruct(array.shape, array.dtype),
+        input_output_aliases={0: 0},
+        compiler_params=pltpu.CompilerParams(vmem_limit_bytes=1024 * 1024),
+        name="touch",
+        cost_estimate=pl.CostEstimate(flops=int(5e9), bytes_accessed=0, transcendentals=0),
+    )(array)
+
+
 def after(array, earlier):
     return lax.optimization_barrier((array, earlier))[0]
 
@@ -80,13 +97,27 @@
     return [jnp.concatenate([swapped[k + g] for k in range(0, last, groups)] + [fetched[last + g] + swapped[last + g]], axis=0) for g in range(groups)]
 
 
-def project(attended_ref, weight_own_ref, weight_other_ref, out_ref):
+def project(attended_ref, weight_own_ref, weight_other_ref, out_ref, first=0):
     width = weight_own_ref.shape[0]
-    columns = 512 if out_ref.shape[1] % 512 == 0 else out_ref.shape[1]
-    for c in range(0, out_ref.shape[1], columns):
-        product = jnp.dot(attended_ref[:, :width], weight_own_ref[:, c : c + columns], preferred_element_type=jnp.float32)
-        product += jnp.dot(attended_ref[:, width:], weight_other_ref[:, c : c + columns], preferred_element_type=jnp.float32)
+    count = out_ref.shape[1]
+    columns = 512 if count % 512 == 0 else count
+    for c in range(0, count, columns):
+        product = jnp.dot(attended_ref[:, :width], weight_own_ref[:, first + c : first + c + columns], preferred_element_type=jnp.float32)
+        product += jnp.dot(attended_ref[:, width:], weight_other_ref[:, first + c : first + c + columns], preferred_element_type=jnp.float32)
         out_ref[:, c : c + columns] = product.astype(out_ref.dtype)
+
+
+def rest_kernel(first, attended_ref, weight_own_ref, weight_other_ref, out_ref):
+    project(attended_ref, weight_own_ref, weight_other_ref, out_ref, first)
+
+
+def sum_kernel(near_ref, *rest):
+    *arrived, out_ref = rest
+    first = 0
+    for part_ref in arrived:
+        columns = slice(first, first + part_ref.shape[1])
+        out_ref[:, columns] = (near_ref[:, columns] + part_ref[...].astype(jnp.float32)).astype(out_ref.dtype)
+        first += part_ref.shape[1]
 
 
 def put_heads(attended_ref, number, unit, attended):
@@ -302,16 +333,16 @@
     project(attended_ref, weight_own_ref, weight_other_ref, out_ref)
 
 
-def chunk(kernel, name, outs, scalars, arrays, weights, scratch):
+def chunk(kernel, name, outs, scalars, arrays, weights, scratch=(), flops=500_000_000):
     return pl.pallas_call(
         kernel,
         in_specs=[in_smem()] * len(scalars) + [in_vmem()] * (len(arrays) + len(weights)),
         out_specs=[in_vmem()] * len(outs),
         out_shape=outs,
-        scratch_shapes=[pltpu.VMEM((outs[0].shape[0], 2 * weights[0].shape[0]), jnp.bfloat16), *scratch],
+        scratch_shapes=scratch,
         compiler_params=pltpu.CompilerParams(vmem_limit_bytes=vmem_bytes),
         name=name,
-        cost_estimate=pl.CostEstimate(flops=500_000_000, bytes_accessed=1_000_000, transcendentals=0),
+        cost_estimate=pl.CostEstimate(flops=flops, bytes_accessed=1_000_000, transcendentals=0),
     )(*scalars, *arrays, *weights)
 
 
@@ -336,19 +367,30 @@
         state = private(unit, chunk_rows, node_count, requests, loaded, other_queries, pieces[:2])
     parts = pieces[-2:]
     weights = (own_weight, other_weight)
-    chunk_shape = (chunk_rows, out_weight.shape[1])
-    (far,) = chunk(
-        functools.partial(far_kernel, unit, len(parts)), "far_chunk", [jax.ShapeDtypeStruct(chunk_shape, jnp.bfloat16)],
-        (), (loaded[2], other_queries, state, *parts), weights, ()
+    columns = out_weight.shape[1]
+    early = columns // 4
+    attended_shape = (chunk_rows, 2 * out_weight.shape[0])
+    early_far, attended = chunk(
+        functools.partial(far_kernel, unit, len(parts)), "far_chunk",
+        [jax.ShapeDtypeStruct((chunk_rows, early), jnp.bfloat16), jax.ShapeDtypeStruct(attended_shape, jnp.bfloat16)],
+        (), (loaded[2], other_queries, state, *parts), weights, flops=200_000_000
     )
-    arrived = lax.ppermute(far, "tp", [(t, t ^ 2) for t in range(tp_count)])
+    across = [(t, t ^ 2) for t in range(tp_count)]
+    early_arrived = touched(lax.ppermute(early_far, "tp", across))
+    (late_far,) = chunk(
+        functools.partial(rest_kernel, early), "far_rest", [jax.ShapeDtypeStruct((chunk_rows, columns - early), jnp.bfloat16)],
+        (), (attended,), weights, flops=300_000_000
+    )
+    late_arrived = lax.ppermute(late_far, "tp", across)
     near, path_cache = chunk(
         functools.partial(near_kernel, unit, len(pieces)), "near_chunk",
-        [jax.ShapeDtypeStruct(chunk_shape, jnp.float32), jax.ShapeDtypeStruct((*accepted.shape, tree_kv.shape[1]), jnp.bfloat16)],
+        [jax.ShapeDtypeStruct((chunk_rows, columns), jnp.float32), jax.ShapeDtypeStruct((*accepted.shape, tree_kv.shape[1]), jnp.bfloat16)],
         (suffix_len, group_ids), (queries, other_queries, parents, accepted, tree_kv, suffix_kv, *pieces), weights,
-        (pltpu.VMEM((requests * node_count, node_count), jnp.float32),)
+        (pltpu.VMEM(attended_shape, jnp.bfloat16), pltpu.VMEM((requests * node_count, node_count), jnp.float32))
     )
-    layer_output = (near + arrived.astype(jnp.float32)).astype(jnp.bfloat16)
+    (layer_output,) = chunk(
+        sum_kernel, "sum", [jax.ShapeDtypeStruct((chunk_rows, columns), jnp.bfloat16)], (), (near, early_arrived, late_arrived), (), flops=1_000_000
+    )
     return (layer_output, path_cache)
 
 

time: 27.9 us -> 27.3 us (0.978)
  waiting for transfers between devices: 7.55 us -> 6.25 us
  Pallas kernels: 7.97 us -> 8.9 us
  other arithmetic: 0.82 us -> 0 us
  starting transfers between devices: 10.5 us -> 11.1 us
    ppermute x1 -> x2, waiting for transfers between devices: 6.44 us -> 5.14 us  [the longest x1 5.14 us: local(): late_arrived = lax.ppermute(late_far, 'tp', across)]
    pallas_call x2 -> x4, Pallas kernels: 4.88 us -> 5.82 us  [chunk(): pl.pallas_call(kernel, in_specs=[in_smem()] * len(scalars) + [in_vmem()]...]
    convert_element_type x1 -> x0, other arithmetic: 0.82 us -> none  [local(): layer_output = (near + arrived.astype(jnp.float32)).astype(jnp.bfloat16)]
    ppermute x1 -> x2, starting transfers between devices: 1.56 us -> 2.16 us  [the longest x1 1.56 us: local(): early_arrived = touched(lax.ppermute(early_far, 'tp', across))]
  transfers between devices with their start and end apart: 8 -> 9, of which waited for: 4 -> 4; matrix products, arithmetic and copies ran while one was open for 0% -> 0% of each run, Pallas kernels for 23% -> 26%
where the time goes in v5:
time: 27.3 us; the launch traced here: 27.1 us
  starting transfers between devices  11.1 us (41%)
  Pallas kernels  8.9 us (33%)
  waiting for transfers between devices  6.25 us (23%)
  between operations  0.78 us (3%)
    ppermute x4, starting transfers between devices, fetch_shards(): arrived.append(lax.ppermute(shard, ('req', 'tp'), pairs))  6.92 us
    pallas_call x4, Pallas kernels, chunk(): pl.pallas_call(kernel, in_specs=[in_smem()] * len(scalars) + [in_vmem()]...  5.82 us
    ppermute x1, waiting for transfers between devices, local(): late_arrived = lax.ppermute(late_far, 'tp', across)  5.14 us
    ppermute x3, starting transfers between devices, swap_in_pair(): return lax.ppermute(array, 'tp', [(t, t ^ 1) for t in range(tp_count)])  2.06 us
    pallas_call x1, Pallas kernels, load(): pl.pallas_call(functools.partial(load_kernel, chunk_rows), in_specs=[pl.B...  1.88 us
    ppermute x1, starting transfers between devices, local(): early_arrived = touched(lax.ppermute(early_far, 'tp', across))  1.56 us
    pallas_call x1, Pallas kernels, private(): pl.pallas_call(functools.partial(private_kernel, unit, chunk_rows, node_c...  1.2 us
    ppermute x4, waiting for transfers between devices, fetch_shards(): arrived.append(lax.ppermute(shard, ('req', 'tp'), pairs))  0.79 us
  transfers between devices with their start and end apart: 9, of which 4 were waited for; matrix products, arithmetic and copies ran while one was open for 0% of the time, Pallas kernels for 26%

profile of v5, /device:TPU:0, one launch (start us, length us, event | category | flops | bytes accessed | tf_op | source)
XLA Modules:
  0.0 27.1 jit_solution(6448991272733287423)
XLA Ops:
  0.6 0.0 copy-start.1
  0.6 0.5 %collective-permute-start.6 = (bf16[512,2048]{1,0:T(8,128)(2,1)}, bf16[512,2048]{1,0:T(8,128)(2,1)S(1)}, u32[]{:S(2)}, u32[]{:S(2)}) collective-permute-start(bf16[512,2048]{1,0:T(8,128)(2,1)} %weight_hbm.1), channel_id=1, source_target_pairs={{0,1},{1,0},{2,3},{3,2},{4,5},{5,4},{6,7},{7,6},{8,9},{9,8},{10,11... | collective-permute-start | bytes 6291464 | tf_op jit(solution)/shard_map/ppermute | solution.py:52
  1.2 5.6 %collective-permute-start.1 = (bf16[2,32,256]{2,1,0:T(8,128)(2,1)}, bf16[2,32,256]{2,1,0:T(8,128)(2,1)S(1)}, u32[]{:S(2)}, u32[]{:S(2)}) collective-permute-start(bf16[2,32,256]{2,1,0:T(8,128)(2,1)} %shard_hbm.1), channel_id=1, source_target_pairs={{0,28},{1,25},{2,30},{3,27},{4,24},{5,29},{6,26},{7,31},{8,20},{9,... | collective-permute-start | bytes 98312 | tf_op jit(solution)/shard_map/ppermute | solution.py:26
  6.8 0.0 collective-permute-start.2
  6.8 0.6 %collective-permute-start.3 = (bf16[2,32,256]{2,1,0:T(8,128)(2,1)}, bf16[2,32,256]{2,1,0:T(8,128)(2,1)S(1)}, u32[]{:S(2)}, u32[]{:S(2)}) collective-permute-start(bf16[2,32,256]{2,1,0:T(8,128)(2,1)} %shard_hbm.1), channel_id=1, source_target_pairs={{0,12},{1,9},{2,14},{3,11},{4,8},{5,13},{6,10},{7,15},{8,4},{9,1},... | collective-permute-start | bytes 98312 | tf_op jit(solution)/shard_map/ppermute | solution.py:26
  7.4 0.7 %collective-permute-start.4 = (bf16[2,32,256]{2,1,0:T(8,128)(2,1)}, bf16[2,32,256]{2,1,0:T(8,128)(2,1)S(1)}, u32[]{:S(2)}, u32[]{:S(2)}) collective-permute-start(bf16[2,32,256]{2,1,0:T(8,128)(2,1)} %shard_hbm.1), channel_id=1, source_target_pairs={{1,5},{3,7},{5,1},{7,3},{9,13},{11,15},{13,9},{15,11},{17,21},{19,... | collective-permute-start | bytes 98312 | tf_op jit(solution)/shard_map/ppermute | solution.py:26
  8.1 1.9 %load.1 = (f32[128,64]{1,0:T(8,128)S(1)}, f32[2,8,256]{2,1,0:T(8,128)S(1)}, bf16[96,512]{1,0:T(8,128)(2,1)S(1)}, bf16[128,256]{1,0:T(8,128)(2,1)S(1)}, bf16[2,25...) custom-call(s32[6,64]{1,0:T(8,128)} %parents_ref.1, s32[6]{0:T(128)} %length_ref.1, ...), custom_call_target="tpu_custom_call" | custom-call | flops 100000000 | bytes 2000000 | tf_op jit(solution)/shard_map/load/pallas_call | solution.py:229
  10.0 0.0 collective-permute-done.1
  10.0 0.0 copy-done.1
  10.0 1.3 %collective-permute-start = (bf16[384,512]{1,0:T(8,128)(2,1)S(1)}, bf16[384,512]{1,0:T(8,128)(2,1)S(1)}, u32[]{:S(2)}, u32[]{:S(2)}) collective-permute-start(bf16[384,512]{1,0:T(8,128)(2,1)S(1)} %copy-done.1), channel_id=1, source_target_pairs={{0,1},{1,0},{2,3},{3,2},{4,5},{5,4},{6,7},{7,6},{8,9},{9,8},{10,11... | collective-permute-start | bytes 1179656 | tf_op jit(solution)/shard_map/ppermute | solution.py:52
  11.3 0.5 %collective-permute-done.2 = bf16[2,32,256]{2,1,0:T(8,128)(2,1)S(1)} collective-permute-done((bf16[2,32,256]{2,1,0:T(8,128)(2,1)}, bf16[2,32,256]{2,1,0:T(8,128)(2,1)S(1)}, u32[]{:S(2)}, u32[]{:S(2)}) %collective-permute-start.2) | collective-permute-done | bytes 32800 | tf_op jit(solution)/shard_map/ppermute | solution.py:26
  11.8 0.3 %collective-permute-done.3 = bf16[2,32,256]{2,1,0:T(8,128)(2,1)S(1)} collective-permute-done((bf16[2,32,256]{2,1,0:T(8,128)(2,1)}, bf16[2,32,256]{2,1,0:T(8,128)(2,1)S(1)}, u32[]{:S(2)}, u32[]{:S(2)}) %collective-permute-start.3) | collective-permute-done | bytes 32800 | tf_op jit(solution)/shard_map/ppermute | solution.py:26
  12.1 0.0 collective-permute-done.4
  12.2 0.2 collective-permute-start.5
  12.4 0.3 %collective-permute-done.other_ref = bf16[384,512]{1,0:T(8,128)(2,1)S(1)} collective-permute-done((bf16[384,512]{1,0:T(8,128)(2,1)S(1)}, bf16[384,512]{1,0:T(8,128)(2,1)S(1)}, u32[]{:S(2)}, u32[]{:S(2)}) %collective-permute-start) | collective-permute-done | bytes 393248 | tf_op jit(solution)/shard_map/ppermute | solution.py:52
  12.7 1.2 %private.1.state_ref = f32[768,512]{1,0:T(8,128)S(1)} custom-call(f32[128,64]{1,0:T(8,128)S(1)} %get-tuple-element.25.bias_ref, f32[2,8,256]{2,1,0:T(8,128)S(1)} %get-tuple-element.26.notes_ref, bf16[96,512]{1,0:T(8,128)(2,1)S(1)} %get-tuple-element.24.own_ref, bf16[128,256]{1,0:T(8,128)(2,1)S(1)} %get-tuple-element.27.tree_ref, ...), custom_call_target="tpu_custom_call" | custom-call | flops 300000000 | bytes 500000 | tf_op jit(solution)/shard_map/private/pallas_call | solution.py:258
  13.9 0.0 collective-permute-done.5.rest_2_.rest_1_
  13.9 0.0 collective-permute-done.6.rest_4_.rest_3_.weight_other_ref
  13.9 1.0 %far_chunk.1 = (bf16[96,512]{1,0:T(8,128)(2,1)S(1)}, bf16[96,1024]{1,0:T(8,128)(2,1)S(1)}) custom-call(bf16[96,512]{1,0:T(8,128)(2,1)S(1)} %get-tuple-element.24.own_ref, bf16[384,512]{1,0:T(8,128)(2,1)S(1)} %collective-permute-done.other_ref, f32[768,512]{1,0:T(8,128)S(1)} %private.1.state_ref, ...), custom_call_target="tpu_custom_call" | custom-call | flops 200000000 | bytes 1000000 | tf_op jit(solution)/shard_map/far_chunk/pallas_call | solution.py:337
  14.9 1.6 %collective-permute-start.7 = (bf16[96,512]{1,0:T(8,128)(2,1)S(1)}, bf16[96,512]{1,0:T(8,128)(2,1)S(1)}, u32[]{:S(2)}, u32[]{:S(2)}) collective-permute-start(bf16[96,512]{1,0:T(8,128)(2,1)S(1)} %get-tuple-element.29), channel_id=1, source_target_pairs={{0,2},{1,3},{2,0},{3,1},{4,6},{5,7},{6,4},{7,5},{8,10},{9,11},{10,... | collective-permute-start | bytes 294920 | tf_op jit(solution)/shard_map/ppermute | solution.py:379
  16.4 0.0 copy-start
  16.4 0.0 copy-start.2
  16.4 0.0 copy-start.3
  16.4 0.0 copy-start.4
  16.4 0.0 copy-start.5
  16.5 0.0 copy-start.6
  16.5 0.6 %far_rest.1 = bf16[96,1536]{1,0:T(8,128)(2,1)S(1)} custom-call(bf16[96,1024]{1,0:T(8,128)(2,1)S(1)} %get-tuple-element.30.attended_ref, bf16[512,2048]{1,0:T(8,128)(2,1)S(1)} %get-tuple-element.22.rest_3_.rest_2_.weight_own_ref, bf16[512,2048]{1,0:T(8,128)(2,1)S(1)} %collective-permute-done.6.rest_4_.rest_3_.weight_other_ref), custom_call_target="tpu_custom_call" | custom-call | flops 300000000 | bytes 1000000 | tf_op jit(solution)/shard_map/far_rest/pallas_call | solution.py:337
  17.1 0.6 %collective-permute-start.8 = (bf16[96,1536]{1,0:T(8,128)(2,1)S(1)}, bf16[96,1536]{1,0:T(8,128)(2,1)S(1)}, u32[]{:S(2)}, u32[]{:S(2)}) collective-permute-start(bf16[96,1536]{1,0:T(8,128)(2,1)S(1)} %far_rest.1), channel_id=1, source_target_pairs={{0,2},{1,3},{2,0},{3,1},{4,6},{5,7},{6,4},{7,5},{8,10},{9,11},{10,... | collective-permute-start | bytes 884744 | tf_op jit(solution)/shard_map/ppermute | solution.py:384
  17.7 0.0 copy-done
  17.7 0.0 copy-done.2
  17.7 0.0 copy-done.3
  17.7 0.0 copy-done.4
  17.7 0.0 copy-done.5
  17.7 0.0 copy-done.6
  17.7 3.4 %near_chunk.1 = (f32[96,2048]{1,0:T(8,128)S(1)}, bf16[6,8,256]{2,1,0:T(8,128)(2,1)}) custom-call(s32[6]{0:T(128)S(1)} %copy-done.5, s32[6]{0:T(128)S(1)} %copy-done.6, bf16[384,512]{1,0:T(8,128)(2,1)S(1)} %copy-done.1, bf16[384,512]{1,0:T(8,128)(2,1)S(1)} %collective-permute-done.other_ref, s32[6,64]{1,0:T(8,128)S(1)} %copy-done.3, s32[6,8]{1,0:T(8,128)S(1)} %copy-done.4, ...), custom_call_target="tpu_custom_call" | custom-call | flops 500000000 | bytes 1000000 | tf_op jit(solution)/shard_map/near_chunk/pallas_call | solution.py:337
  21.2 0.0 collective-permute-done.7.in_ref
  21.2 5.1 %collective-permute-done.8.rest_1_ = bf16[96,1536]{1,0:T(8,128)(2,1)S(1)} collective-permute-done((bf16[96,1536]{1,0:T(8,128)(2,1)S(1)}, bf16[96,1536]{1,0:T(8,128)(2,1)S(1)}, u32[]{:S(2)}, u32[]{:S(2)}) %collective-permute-start.8) | collective-permute-done | bytes 294944 | tf_op jit(solution)/shard_map/ppermute | solution.py:384
  26.3 0.8 %sum.1 = bf16[96,2048]{1,0:T(8,128)(2,1)} custom-call(f32[96,2048]{1,0:T(8,128)S(1)} %get-tuple-element.23.near_ref, bf16[96,512]{1,0:T(8,128)(2,1)S(1)} %touch.1.rest_0_, bf16[96,1536]{1,0:T(8,128)(2,1)S(1)} %collective-permute-done.8.rest_1_), custom_call_target="tpu_custom_call" | custom-call | flops 1000000 | bytes 1000000 | tf_op jit(solution)/shard_map/sum/pallas_call | solution.py:337
  (5 shorter events, 0.0 us)
Async XLA Ops:
  0.6 9.4 %copy-start.1 = (bf16[384,512]{1,0:T(8,128)(2,1)S(1)}, bf16[384,512]{1,0:T(8,128)(2,1)}, u32[]{:S(2)}) copy-start(bf16[384,512]{1,0:T(8,128)(2,1)} %own_ref.1) | copy-start | bytes 1179652
  0.6 13.3 %collective-permute-start.6 = (bf16[512,2048]{1,0:T(8,128)(2,1)}, bf16[512,2048]{1,0:T(8,128)(2,1)S(1)}, u32[]{:S(2)}, u32[]{:S(2)}) collective-permute-start(bf16[512,2048]{1,0:T(8,128)(2,1)} %weight_hbm.1), channel_id=1, source_target_pairs={{0,1},{1,0},{2,3},{3,2},{4,5},{5,4},{6,7},{7,6},{8,9},{9,8},{10,11... | collective-permute-start | bytes 6291464 | tf_op jit(solution)/shard_map/ppermute | solution.py:52
  1.2 8.8 %collective-permute-start.1 = (bf16[2,32,256]{2,1,0:T(8,128)(2,1)}, bf16[2,32,256]{2,1,0:T(8,128)(2,1)S(1)}, u32[]{:S(2)}, u32[]{:S(2)}) collective-permute-start(bf16[2,32,256]{2,1,0:T(8,128)(2,1)} %shard_hbm.1), channel_id=1, source_target_pairs={{0,28},{1,25},{2,30},{3,27},{4,24},{5,29},{6,26},{7,31},{8,20},{9,... | collective-permute-start | bytes 98312 | tf_op jit(solution)/shard_map/ppermute | solution.py:26
  6.8 5.0 %collective-permute-start.2 = (bf16[2,32,256]{2,1,0:T(8,128)(2,1)}, bf16[2,32,256]{2,1,0:T(8,128)(2,1)S(1)}, u32[]{:S(2)}, u32[]{:S(2)}) collective-permute-start(bf16[2,32,256]{2,1,0:T(8,128)(2,1)} %shard_hbm.1), channel_id=1, source_target_pairs={{0,16},{1,21},{2,18},{3,23},{4,20},{5,17},{6,22},{7,19},{8,24},{9,... | collective-permute-start | bytes 98312 | tf_op jit(solution)/shard_map/ppermute | solution.py:26
  6.8 5.3 %collective-permute-start.3 = (bf16[2,32,256]{2,1,0:T(8,128)(2,1)}, bf16[2,32,256]{2,1,0:T(8,128)(2,1)S(1)}, u32[]{:S(2)}, u32[]{:S(2)}) collective-permute-start(bf16[2,32,256]{2,1,0:T(8,128)(2,1)} %shard_hbm.1), channel_id=1, source_target_pairs={{0,12},{1,9},{2,14},{3,11},{4,8},{5,13},{6,10},{7,15},{8,4},{9,1},... | collective-permute-start | bytes 98312 | tf_op jit(solution)/shard_map/ppermute | solution.py:26
  7.4 4.7 %collective-permute-start.4 = (bf16[2,32,256]{2,1,0:T(8,128)(2,1)}, bf16[2,32,256]{2,1,0:T(8,128)(2,1)S(1)}, u32[]{:S(2)}, u32[]{:S(2)}) collective-permute-start(bf16[2,32,256]{2,1,0:T(8,128)(2,1)} %shard_hbm.1), channel_id=1, source_target_pairs={{1,5},{3,7},{5,1},{7,3},{9,13},{11,15},{13,9},{15,11},{17,21},{19,... | collective-permute-start | bytes 98312 | tf_op jit(solution)/shard_map/ppermute | solution.py:26
  10.0 2.7 %collective-permute-start = (bf16[384,512]{1,0:T(8,128)(2,1)S(1)}, bf16[384,512]{1,0:T(8,128)(2,1)S(1)}, u32[]{:S(2)}, u32[]{:S(2)}) collective-permute-start(bf16[384,512]{1,0:T(8,128)(2,1)S(1)} %copy-done.1), channel_id=1, source_target_pairs={{0,1},{1,0},{2,3},{3,2},{4,5},{5,4},{6,7},{7,6},{8,9},{9,8},{10,11... | collective-permute-start | bytes 1179656 | tf_op jit(solution)/shard_map/ppermute | solution.py:52
  12.2 1.7 %collective-permute-start.5 = (bf16[8,32,256]{2,1,0:T(8,128)(2,1)S(1)}, bf16[8,32,256]{2,1,0:T(8,128)(2,1)S(1)}, u32[]{:S(2)}, u32[]{:S(2)}) collective-permute-start(bf16[8,32,256]{2,1,0:T(8,128)(2,1)S(1)} %constant_dynamic-update-slice_fusion.rest_1_.rest_0_), channel_id=1, source_target_pairs={{0,1},{1,0},{2,3},{3,2},{4,5},{5,4},{6,7},{7,6},{8,9},{9,8},{10,11... | collective-permute-start | bytes 393224 | tf_op jit(solution)/shard_map/ppermute | solution.py:52
  14.9 6.3 %collective-permute-start.7 = (bf16[96,512]{1,0:T(8,128)(2,1)S(1)}, bf16[96,512]{1,0:T(8,128)(2,1)S(1)}, u32[]{:S(2)}, u32[]{:S(2)}) collective-permute-start(bf16[96,512]{1,0:T(8,128)(2,1)S(1)} %get-tuple-element.29), channel_id=1, source_target_pairs={{0,2},{1,3},{2,0},{3,1},{4,6},{5,7},{6,4},{7,5},{8,10},{9,11},{10,... | collective-permute-start | bytes 294920 | tf_op jit(solution)/shard_map/ppermute | solution.py:379
  16.4 1.3 %copy-start = (bf16[6,256,256]{2,1,0:T(8,128)(2,1)S(1)}, bf16[6,256,256]{2,1,0:T(8,128)(2,1)}, u32[]{:S(2)}) copy-start(bf16[6,256,256]{2,1,0:T(8,128)(2,1)} %suffix_ref.1) | copy-start | bytes 2359300
  16.4 1.3 %copy-start.2 = (bf16[384,256]{1,0:T(8,128)(2,1)S(1)}, bf16[384,256]{1,0:T(8,128)(2,1)}, u32[]{:S(2)}) copy-start(bf16[384,256]{1,0:T(8,128)(2,1)} %tree_ref.1) | copy-start | bytes 589828
  16.4 1.3 %copy-start.3 = (s32[6,64]{1,0:T(8,128)S(1)}, s32[6,64]{1,0:T(8,128)}, u32[]{:S(2)}) copy-start(s32[6,64]{1,0:T(8,128)} %parents_ref.1) | copy-start | bytes 4612
  16.4 1.3 %copy-start.4 = (s32[6,8]{1,0:T(8,128)S(1)}, s32[6,8]{1,0:T(8,128)}, u32[]{:S(2)}) copy-start(s32[6,8]{1,0:T(8,128)} %accepted_ref.1) | copy-start | bytes 580
  16.4 1.3 %copy-start.5 = (s32[6]{0:T(128)S(1)}, s32[6]{0:T(128)}, u32[]{:S(2)}) copy-start(s32[6]{0:T(128)} %length_ref.1) | copy-start | bytes 76
  16.5 1.3 %copy-start.6 = (s32[6]{0:T(128)S(1)}, s32[6]{0:T(128)}, u32[]{:S(2)}) copy-start(s32[6]{0:T(128)} %group_ref.1) | copy-start | bytes 76
  17.1 9.2 %collective-permute-start.8 = (bf16[96,1536]{1,0:T(8,128)(2,1)S(1)}, bf16[96,1536]{1,0:T(8,128)(2,1)S(1)}, u32[]{:S(2)}, u32[]{:S(2)}) collective-permute-start(bf16[96,1536]{1,0:T(8,128)(2,1)S(1)} %far_rest.1), channel_id=1, source_target_pairs={{0,2},{1,3},{2,0},{3,1},{4,6},{5,7},{6,4},{7,5},{8,10},{9,11},{10,... | collective-permute-start | bytes 884744 | tf_op jit(solution)/shard_map/ppermute | solution.py:384

commit v6 on v5

--- a/solution.py
+++ b/solution.py
@@ -14,7 +14,7 @@
 
 
 def fetch_shards(shard, req_count, tp_count):
-    masks = ((7, 4, 3), (6, 5, 2, 1))
+    masks = ((4, 5, 3), (6, 7, 2, 1))
     arrived = []
     for step in range(fetches):
         pairs = []

time: 27.3 us -> 27.1 us (level)
  waiting for transfers between devices: 6.25 us -> 5.46 us
  starting transfers between devices: 11.1 us -> 11.7 us
    ppermute x4, waiting for transfers between devices: 0.79 us -> 0.03 us  [fetch_shards(): arrived.append(lax.ppermute(shard, ('req', 'tp'), pairs))]
    ppermute x3, starting transfers between devices: 2.06 us -> 2.43 us  [swap_in_pair(): return lax.ppermute(array, 'tp', [(t, t ^ 1) for t in range(tp_count)])]
  transfers between devices with their start and end apart: 9 -> 9, of which waited for: 4 -> 2; matrix products, arithmetic and copies ran while one was open for 0% -> 0% of each run, Pallas kernels for 26% -> 26%
where the time goes in v6:
time: 27.1 us; the launch traced here: 26.9 us
  starting transfers between devices  11.7 us (43%)
  Pallas kernels  8.91 us (33%)
  waiting for transfers between devices  5.46 us (20%)
  between operations  0.79 us (3%)
    ppermute x4, starting transfers between devices, fetch_shards(): arrived.append(lax.ppermute(shard, ('req', 'tp'), pairs))  7.12 us
    pallas_call x4, Pallas kernels, chunk(): pl.pallas_call(kernel, in_specs=[in_smem()] * len(scalars) + [in_vmem()]...  5.82 us
    ppermute x1, waiting for transfers between devices, local(): late_arrived = lax.ppermute(late_far, 'tp', across)  5.14 us
    ppermute x3, starting transfers between devices, swap_in_pair(): return lax.ppermute(array, 'tp', [(t, t ^ 1) for t in range(tp_count)])  2.43 us
    pallas_call x1, Pallas kernels, load(): pl.pallas_call(functools.partial(load_kernel, chunk_rows), in_specs=[pl.B...  1.88 us
    ppermute x1, starting transfers between devices, local(): early_arrived = touched(lax.ppermute(early_far, 'tp', across))  1.56 us
    pallas_call x1, Pallas kernels, private(): pl.pallas_call(functools.partial(private_kernel, unit, chunk_rows, node_c...  1.2 us
    ppermute x1, starting transfers between devices, local(): late_arrived = lax.ppermute(late_far, 'tp', across)  0.6 us
  transfers between devices with their start and end apart: 9, of which 2 were waited for; matrix products, arithmetic and copies ran while one was open for 0% of the time, Pallas kernels for 26%

profile of v6, /device:TPU:0, one launch (start us, length us, event | category | flops | bytes accessed | tf_op | source)
XLA Modules:
  0.0 26.9 jit_solution(10306785261705982185)
XLA Ops:
  0.6 0.0 copy-start.1
  0.6 0.5 %collective-permute-start.6 = (bf16[512,2048]{1,0:T(8,128)(2,1)}, bf16[512,2048]{1,0:T(8,128)(2,1)S(1)}, u32[]{:S(2)}, u32[]{:S(2)}) collective-permute-start(bf16[512,2048]{1,0:T(8,128)(2,1)} %weight_hbm.1), channel_id=1, source_target_pairs={{0,1},{1,0},{2,3},{3,2},{4,5},{5,4},{6,7},{7,6},{8,9},{9,8},{10,11... | collective-permute-start | bytes 6291464 | tf_op jit(solution)/shard_map/ppermute | solution.py:52
  1.2 3.7 %collective-permute-start.1 = (bf16[2,32,256]{2,1,0:T(8,128)(2,1)}, bf16[2,32,256]{2,1,0:T(8,128)(2,1)S(1)}, u32[]{:S(2)}, u32[]{:S(2)}) collective-permute-start(bf16[2,32,256]{2,1,0:T(8,128)(2,1)} %shard_hbm.1), channel_id=1, source_target_pairs={{0,16},{1,25},{2,18},{3,27},{4,20},{5,29},{6,22},{7,31},{8,24},{9,... | collective-permute-start | bytes 98312 | tf_op jit(solution)/shard_map/ppermute | solution.py:26
  4.8 1.3 %collective-permute-start.2 = (bf16[2,32,256]{2,1,0:T(8,128)(2,1)}, bf16[2,32,256]{2,1,0:T(8,128)(2,1)S(1)}, u32[]{:S(2)}, u32[]{:S(2)}) collective-permute-start(bf16[2,32,256]{2,1,0:T(8,128)(2,1)} %shard_hbm.1), channel_id=1, source_target_pairs={{0,20},{1,29},{2,22},{3,31},{4,16},{5,25},{6,18},{7,27},{8,28},{9,... | collective-permute-start | bytes 98312 | tf_op jit(solution)/shard_map/ppermute | solution.py:26
  6.1 1.5 %collective-permute-start.3 = (bf16[2,32,256]{2,1,0:T(8,128)(2,1)}, bf16[2,32,256]{2,1,0:T(8,128)(2,1)S(1)}, u32[]{:S(2)}, u32[]{:S(2)}) collective-permute-start(bf16[2,32,256]{2,1,0:T(8,128)(2,1)} %shard_hbm.1), channel_id=1, source_target_pairs={{0,12},{1,9},{2,14},{3,11},{4,8},{5,13},{6,10},{7,15},{8,4},{9,1},... | collective-permute-start | bytes 98312 | tf_op jit(solution)/shard_map/ppermute | solution.py:26
  7.6 0.7 %collective-permute-start.4 = (bf16[2,32,256]{2,1,0:T(8,128)(2,1)}, bf16[2,32,256]{2,1,0:T(8,128)(2,1)S(1)}, u32[]{:S(2)}, u32[]{:S(2)}) collective-permute-start(bf16[2,32,256]{2,1,0:T(8,128)(2,1)} %shard_hbm.1), channel_id=1, source_target_pairs={{1,5},{3,7},{5,1},{7,3},{9,13},{11,15},{13,9},{15,11},{17,21},{19,... | collective-permute-start | bytes 98312 | tf_op jit(solution)/shard_map/ppermute | solution.py:26
  8.3 1.9 %load.1 = (f32[128,64]{1,0:T(8,128)S(1)}, f32[2,8,256]{2,1,0:T(8,128)S(1)}, bf16[96,512]{1,0:T(8,128)(2,1)S(1)}, bf16[128,256]{1,0:T(8,128)(2,1)S(1)}, bf16[2,25...) custom-call(s32[6,64]{1,0:T(8,128)} %parents_ref.1, s32[6]{0:T(128)} %length_ref.1, ...), custom_call_target="tpu_custom_call" | custom-call | flops 100000000 | bytes 2000000 | tf_op jit(solution)/shard_map/load/pallas_call | solution.py:229
  10.2 0.0 collective-permute-done.1
  10.2 0.0 copy-done.1
  10.2 0.9 %collective-permute-start = (bf16[384,512]{1,0:T(8,128)(2,1)S(1)}, bf16[384,512]{1,0:T(8,128)(2,1)S(1)}, u32[]{:S(2)}, u32[]{:S(2)}) collective-permute-start(bf16[384,512]{1,0:T(8,128)(2,1)S(1)} %copy-done.1), channel_id=1, source_target_pairs={{0,1},{1,0},{2,3},{3,2},{4,5},{5,4},{6,7},{7,6},{8,9},{9,8},{10,11... | collective-permute-start | bytes 1179656 | tf_op jit(solution)/shard_map/ppermute | solution.py:52
  11.1 0.0 collective-permute-done.2
  11.1 0.0 collective-permute-done.3
  11.1 0.0 collective-permute-done.4
  11.2 1.0 %collective-permute-start.5 = (bf16[8,32,256]{2,1,0:T(8,128)(2,1)S(1)}, bf16[8,32,256]{2,1,0:T(8,128)(2,1)S(1)}, u32[]{:S(2)}, u32[]{:S(2)}) collective-permute-start(bf16[8,32,256]{2,1,0:T(8,128)(2,1)S(1)} %constant_dynamic-update-slice_fusion.rest_1_.rest_0_), channel_id=1, source_target_pairs={{0,1},{1,0},{2,3},{3,2},{4,5},{5,4},{6,7},{7,6},{8,9},{9,8},{10,11... | collective-permute-start | bytes 393224 | tf_op jit(solution)/shard_map/ppermute | solution.py:52
  12.2 0.3 %collective-permute-done.other_ref = bf16[384,512]{1,0:T(8,128)(2,1)S(1)} collective-permute-done((bf16[384,512]{1,0:T(8,128)(2,1)S(1)}, bf16[384,512]{1,0:T(8,128)(2,1)S(1)}, u32[]{:S(2)}, u32[]{:S(2)}) %collective-permute-start) | collective-permute-done | bytes 393248 | tf_op jit(solution)/shard_map/ppermute | solution.py:52
  12.5 1.2 %private.1.state_ref = f32[768,512]{1,0:T(8,128)S(1)} custom-call(f32[128,64]{1,0:T(8,128)S(1)} %get-tuple-element.25.bias_ref, f32[2,8,256]{2,1,0:T(8,128)S(1)} %get-tuple-element.26.notes_ref, bf16[96,512]{1,0:T(8,128)(2,1)S(1)} %get-tuple-element.24.own_ref, bf16[128,256]{1,0:T(8,128)(2,1)S(1)} %get-tuple-element.27.tree_ref, ...), custom_call_target="tpu_custom_call" | custom-call | flops 300000000 | bytes 500000 | tf_op jit(solution)/shard_map/private/pallas_call | solution.py:258
  13.7 0.0 collective-permute-done.5.rest_2_.rest_1_
  13.7 0.0 collective-permute-done.6.rest_4_.rest_3_.weight_other_ref
  13.7 1.0 %far_chunk.1 = (bf16[96,512]{1,0:T(8,128)(2,1)S(1)}, bf16[96,1024]{1,0:T(8,128)(2,1)S(1)}) custom-call(bf16[96,512]{1,0:T(8,128)(2,1)S(1)} %get-tuple-element.24.own_ref, bf16[384,512]{1,0:T(8,128)(2,1)S(1)} %collective-permute-done.other_ref, f32[768,512]{1,0:T(8,128)S(1)} %private.1.state_ref, ...), custom_call_target="tpu_custom_call" | custom-call | flops 200000000 | bytes 1000000 | tf_op jit(solution)/shard_map/far_chunk/pallas_call | solution.py:337
  14.7 1.6 %collective-permute-start.7 = (bf16[96,512]{1,0:T(8,128)(2,1)S(1)}, bf16[96,512]{1,0:T(8,128)(2,1)S(1)}, u32[]{:S(2)}, u32[]{:S(2)}) collective-permute-start(bf16[96,512]{1,0:T(8,128)(2,1)S(1)} %get-tuple-element.29), channel_id=1, source_target_pairs={{0,2},{1,3},{2,0},{3,1},{4,6},{5,7},{6,4},{7,5},{8,10},{9,11},{10,... | collective-permute-start | bytes 294920 | tf_op jit(solution)/shard_map/ppermute | solution.py:379
  16.2 0.0 copy-start
  16.2 0.0 copy-start.2
  16.2 0.0 copy-start.3
  16.2 0.0 copy-start.4
  16.2 0.0 copy-start.5
  16.2 0.0 copy-start.6
  16.2 0.6 %far_rest.1 = bf16[96,1536]{1,0:T(8,128)(2,1)S(1)} custom-call(bf16[96,1024]{1,0:T(8,128)(2,1)S(1)} %get-tuple-element.30.attended_ref, bf16[512,2048]{1,0:T(8,128)(2,1)S(1)} %get-tuple-element.22.rest_3_.rest_2_.weight_own_ref, bf16[512,2048]{1,0:T(8,128)(2,1)S(1)} %collective-permute-done.6.rest_4_.rest_3_.weight_other_ref), custom_call_target="tpu_custom_call" | custom-call | flops 300000000 | bytes 1000000 | tf_op jit(solution)/shard_map/far_rest/pallas_call | solution.py:337
  16.9 0.6 %collective-permute-start.8 = (bf16[96,1536]{1,0:T(8,128)(2,1)S(1)}, bf16[96,1536]{1,0:T(8,128)(2,1)S(1)}, u32[]{:S(2)}, u32[]{:S(2)}) collective-permute-start(bf16[96,1536]{1,0:T(8,128)(2,1)S(1)} %far_rest.1), channel_id=1, source_target_pairs={{0,2},{1,3},{2,0},{3,1},{4,6},{5,7},{6,4},{7,5},{8,10},{9,11},{10,... | collective-permute-start | bytes 884744 | tf_op jit(solution)/shard_map/ppermute | solution.py:384
  17.5 0.0 copy-done
  17.5 0.0 copy-done.2
  17.5 0.0 copy-done.3
  17.5 0.0 copy-done.4
  17.5 0.0 copy-done.5
  17.5 0.0 copy-done.6
  17.5 3.4 %near_chunk.1 = (f32[96,2048]{1,0:T(8,128)S(1)}, bf16[6,8,256]{2,1,0:T(8,128)(2,1)}) custom-call(s32[6]{0:T(128)S(1)} %copy-done.5, s32[6]{0:T(128)S(1)} %copy-done.6, bf16[384,512]{1,0:T(8,128)(2,1)S(1)} %copy-done.1, bf16[384,512]{1,0:T(8,128)(2,1)S(1)} %collective-permute-done.other_ref, s32[6,64]{1,0:T(8,128)S(1)} %copy-done.3, s32[6,8]{1,0:T(8,128)S(1)} %copy-done.4, ...), custom_call_target="tpu_custom_call" | custom-call | flops 500000000 | bytes 1000000 | tf_op jit(solution)/shard_map/near_chunk/pallas_call | solution.py:337
  20.9 0.0 collective-permute-done.7.in_ref
  21.0 5.1 %collective-permute-done.8.rest_1_ = bf16[96,1536]{1,0:T(8,128)(2,1)S(1)} collective-permute-done((bf16[96,1536]{1,0:T(8,128)(2,1)S(1)}, bf16[96,1536]{1,0:T(8,128)(2,1)S(1)}, u32[]{:S(2)}, u32[]{:S(2)}) %collective-permute-start.8) | collective-permute-done | bytes 294944 | tf_op jit(solution)/shard_map/ppermute | solution.py:384
  26.1 0.8 %sum.1 = bf16[96,2048]{1,0:T(8,128)(2,1)} custom-call(f32[96,2048]{1,0:T(8,128)S(1)} %get-tuple-element.23.near_ref, bf16[96,512]{1,0:T(8,128)(2,1)S(1)} %touch.1.rest_0_, bf16[96,1536]{1,0:T(8,128)(2,1)S(1)} %collective-permute-done.8.rest_1_), custom_call_target="tpu_custom_call" | custom-call | flops 1000000 | bytes 1000000 | tf_op jit(solution)/shard_map/sum/pallas_call | solution.py:337
  (5 shorter events, 0.0 us)
Async XLA Ops:
  0.6 9.6 %copy-start.1 = (bf16[384,512]{1,0:T(8,128)(2,1)S(1)}, bf16[384,512]{1,0:T(8,128)(2,1)}, u32[]{:S(2)}) copy-start(bf16[384,512]{1,0:T(8,128)(2,1)} %own_ref.1) | copy-start | bytes 1179652
  0.6 13.0 %collective-permute-start.6 = (bf16[512,2048]{1,0:T(8,128)(2,1)}, bf16[512,2048]{1,0:T(8,128)(2,1)S(1)}, u32[]{:S(2)}, u32[]{:S(2)}) collective-permute-start(bf16[512,2048]{1,0:T(8,128)(2,1)} %weight_hbm.1), channel_id=1, source_target_pairs={{0,1},{1,0},{2,3},{3,2},{4,5},{5,4},{6,7},{7,6},{8,9},{9,8},{10,11... | collective-permute-start | bytes 6291464 | tf_op jit(solution)/shard_map/ppermute | solution.py:52
  1.2 9.0 %collective-permute-start.1 = (bf16[2,32,256]{2,1,0:T(8,128)(2,1)}, bf16[2,32,256]{2,1,0:T(8,128)(2,1)S(1)}, u32[]{:S(2)}, u32[]{:S(2)}) collective-permute-start(bf16[2,32,256]{2,1,0:T(8,128)(2,1)} %shard_hbm.1), channel_id=1, source_target_pairs={{0,16},{1,25},{2,18},{3,27},{4,20},{5,29},{6,22},{7,31},{8,24},{9,... | collective-permute-start | bytes 98312 | tf_op jit(solution)/shard_map/ppermute | solution.py:26
  4.8 6.3 %collective-permute-start.2 = (bf16[2,32,256]{2,1,0:T(8,128)(2,1)}, bf16[2,32,256]{2,1,0:T(8,128)(2,1)S(1)}, u32[]{:S(2)}, u32[]{:S(2)}) collective-permute-start(bf16[2,32,256]{2,1,0:T(8,128)(2,1)} %shard_hbm.1), channel_id=1, source_target_pairs={{0,20},{1,29},{2,22},{3,31},{4,16},{5,25},{6,18},{7,27},{8,28},{9,... | collective-permute-start | bytes 98312 | tf_op jit(solution)/shard_map/ppermute | solution.py:26
  6.1 5.0 %collective-permute-start.3 = (bf16[2,32,256]{2,1,0:T(8,128)(2,1)}, bf16[2,32,256]{2,1,0:T(8,128)(2,1)S(1)}, u32[]{:S(2)}, u32[]{:S(2)}) collective-permute-start(bf16[2,32,256]{2,1,0:T(8,128)(2,1)} %shard_hbm.1), channel_id=1, source_target_pairs={{0,12},{1,9},{2,14},{3,11},{4,8},{5,13},{6,10},{7,15},{8,4},{9,1},... | collective-permute-start | bytes 98312 | tf_op jit(solution)/shard_map/ppermute | solution.py:26
  7.6 3.5 %collective-permute-start.4 = (bf16[2,32,256]{2,1,0:T(8,128)(2,1)}, bf16[2,32,256]{2,1,0:T(8,128)(2,1)S(1)}, u32[]{:S(2)}, u32[]{:S(2)}) collective-permute-start(bf16[2,32,256]{2,1,0:T(8,128)(2,1)} %shard_hbm.1), channel_id=1, source_target_pairs={{1,5},{3,7},{5,1},{7,3},{9,13},{11,15},{13,9},{15,11},{17,21},{19,... | collective-permute-start | bytes 98312 | tf_op jit(solution)/shard_map/ppermute | solution.py:26
  10.2 2.3 %collective-permute-start = (bf16[384,512]{1,0:T(8,128)(2,1)S(1)}, bf16[384,512]{1,0:T(8,128)(2,1)S(1)}, u32[]{:S(2)}, u32[]{:S(2)}) collective-permute-start(bf16[384,512]{1,0:T(8,128)(2,1)S(1)} %copy-done.1), channel_id=1, source_target_pairs={{0,1},{1,0},{2,3},{3,2},{4,5},{5,4},{6,7},{7,6},{8,9},{9,8},{10,11... | collective-permute-start | bytes 1179656 | tf_op jit(solution)/shard_map/ppermute | solution.py:52
  11.2 2.5 %collective-permute-start.5 = (bf16[8,32,256]{2,1,0:T(8,128)(2,1)S(1)}, bf16[8,32,256]{2,1,0:T(8,128)(2,1)S(1)}, u32[]{:S(2)}, u32[]{:S(2)}) collective-permute-start(bf16[8,32,256]{2,1,0:T(8,128)(2,1)S(1)} %constant_dynamic-update-slice_fusion.rest_1_.rest_0_), channel_id=1, source_target_pairs={{0,1},{1,0},{2,3},{3,2},{4,5},{5,4},{6,7},{7,6},{8,9},{9,8},{10,11... | collective-permute-start | bytes 393224 | tf_op jit(solution)/shard_map/ppermute | solution.py:52
  14.7 6.3 %collective-permute-start.7 = (bf16[96,512]{1,0:T(8,128)(2,1)S(1)}, bf16[96,512]{1,0:T(8,128)(2,1)S(1)}, u32[]{:S(2)}, u32[]{:S(2)}) collective-permute-start(bf16[96,512]{1,0:T(8,128)(2,1)S(1)} %get-tuple-element.29), channel_id=1, source_target_pairs={{0,2},{1,3},{2,0},{3,1},{4,6},{5,7},{6,4},{7,5},{8,10},{9,11},{10,... | collective-permute-start | bytes 294920 | tf_op jit(solution)/shard_map/ppermute | solution.py:379
  16.2 1.3 %copy-start = (bf16[6,256,256]{2,1,0:T(8,128)(2,1)S(1)}, bf16[6,256,256]{2,1,0:T(8,128)(2,1)}, u32[]{:S(2)}) copy-start(bf16[6,256,256]{2,1,0:T(8,128)(2,1)} %suffix_ref.1) | copy-start | bytes 2359300
  16.2 1.3 %copy-start.2 = (bf16[384,256]{1,0:T(8,128)(2,1)S(1)}, bf16[384,256]{1,0:T(8,128)(2,1)}, u32[]{:S(2)}) copy-start(bf16[384,256]{1,0:T(8,128)(2,1)} %tree_ref.1) | copy-start | bytes 589828
  16.2 1.3 %copy-start.3 = (s32[6,64]{1,0:T(8,128)S(1)}, s32[6,64]{1,0:T(8,128)}, u32[]{:S(2)}) copy-start(s32[6,64]{1,0:T(8,128)} %parents_ref.1) | copy-start | bytes 4612
  16.2 1.3 %copy-start.4 = (s32[6,8]{1,0:T(8,128)S(1)}, s32[6,8]{1,0:T(8,128)}, u32[]{:S(2)}) copy-start(s32[6,8]{1,0:T(8,128)} %accepted_ref.1) | copy-start | bytes 580
  16.2 1.3 %copy-start.5 = (s32[6]{0:T(128)S(1)}, s32[6]{0:T(128)}, u32[]{:S(2)}) copy-start(s32[6]{0:T(128)} %length_ref.1) | copy-start | bytes 76
  16.2 1.3 %copy-start.6 = (s32[6]{0:T(128)S(1)}, s32[6]{0:T(128)}, u32[]{:S(2)}) copy-start(s32[6]{0:T(128)} %group_ref.1) | copy-start | bytes 76
  16.9 9.2 %collective-permute-start.8 = (bf16[96,1536]{1,0:T(8,128)(2,1)S(1)}, bf16[96,1536]{1,0:T(8,128)(2,1)S(1)}, u32[]{:S(2)}, u32[]{:S(2)}) collective-permute-start(bf16[96,1536]{1,0:T(8,128)(2,1)S(1)} %far_rest.1), channel_id=1, source_target_pairs={{0,2},{1,3},{2,0},{3,1},{4,6},{5,7},{6,4},{7,5},{8,10},{9,11},{10,... | collective-permute-start | bytes 884744 | tf_op jit(solution)/shard_map/ppermute | solution.py:384

commit v7 on v6

--- a/solution.py
+++ b/solution.py
@@ -153,11 +153,12 @@
 
 def load_kernel(
     chunk_rows, parents_hbm, length_hbm, group_hbm, own_hbm, tree_hbm, suffix_hbm, shard_hbm, weight_hbm,
-    bias_ref, notes_ref, own_ref, tree_ref, suffix_ref, shard_ref, weight_ref, parents_ref, length_ref, group_ref, arrival
+    bias_ref, notes_ref, own_ref, tree_ref, suffix_ref, pair_ref, shard_ref, weight_ref, parents_ref, length_ref, group_ref, arrival
 ):
     requests, node_count = parents_ref.shape
     touched, slot_count = suffix_ref.shape[:2]
     start = pl.multiple_of(first_row(chunk_rows, 2), math.gcd(chunk_rows, node_count))
+    pair_start = pl.multiple_of(first_row(chunk_rows, 3), math.gcd(chunk_rows, node_count))
     base = first_request(chunk_rows, 2, node_count, requests, touched)
     copies = [
         pltpu.make_async_copy(source, target, arrival.at[place])
@@ -166,6 +167,7 @@
             (length_hbm, length_ref),
             (group_hbm, group_ref),
             (own_hbm.at[pl.ds(start, chunk_rows)], own_ref),
+            (own_hbm.at[pl.ds(pair_start, chunk_rows)], pair_ref),
             (tree_hbm.at[pl.ds(pl.multiple_of(base * node_count, node_count), touched * node_count)], tree_ref),
             (suffix_hbm.at[pl.ds(base, touched)], suffix_ref),
             (shard_hbm, shard_ref),
@@ -197,7 +199,7 @@
         row = pl.multiple_of(start + number * unit, unit)
         place = row // node_count - base
         query = jnp.concatenate(
-            [stacked_heads(own_ref, number * unit, unit, head_size), stacked_heads(other_ref, row, unit, head_size)], axis=0
+            [stacked_heads(own_ref, number * unit, unit, head_size), stacked_heads(other_ref, number * unit, unit, head_size)], axis=0
         )
         bias = bias_ref[pl.ds(pl.multiple_of(row - base * node_count, unit), unit), :]
         tree = tree_ref[pl.ds(pl.multiple_of(place * node_count, node_count), node_count), :]
@@ -229,13 +231,14 @@
     return pl.pallas_call(
         functools.partial(load_kernel, chunk_rows),
         in_specs=[pl.BlockSpec(memory_space=pltpu.HBM)] * 8,
-        out_specs=[in_vmem()] * 7,
+        out_specs=[in_vmem()] * 8,
         out_shape=(
             jax.ShapeDtypeStruct((touched * node_count, node_count), jnp.float32),
             jax.ShapeDtypeStruct((touched, 8, suffix_kv.shape[1]), jnp.float32),
             jax.ShapeDtypeStruct((chunk_rows, own.shape[1]), own.dtype),
             jax.ShapeDtypeStruct((touched * node_count, tree_kv.shape[1]), tree_kv.dtype),
             jax.ShapeDtypeStruct((touched, *suffix_kv.shape[1:]), suffix_kv.dtype),
+            jax.ShapeDtypeStruct((chunk_rows, own.shape[1]), own.dtype),
             jax.ShapeDtypeStruct(shard.shape, shard.dtype),
             jax.ShapeDtypeStruct(weight.shape, weight.dtype),
         ),
@@ -243,7 +246,7 @@
             pltpu.VMEM(parents.shape, jnp.int32),
             pltpu.SMEM(lengths.shape, jnp.int32),
             pltpu.SMEM(groups.shape, jnp.int32),
-            pltpu.SemaphoreType.DMA((8,)),
+            pltpu.SemaphoreType.DMA((9,)),
         ],
         compiler_params=pltpu.CompilerParams(vmem_limit_bytes=vmem_bytes),
         name="load",
@@ -276,7 +279,7 @@
     for number in range(chunk_rows // unit):
         row = pl.multiple_of(start + number * unit, unit)
         query = jnp.concatenate(
-            [stacked_heads(own_ref, number * unit, unit, head_size), stacked_heads(other_ref, row, unit, head_size)], axis=0
+            [stacked_heads(own_ref, number * unit, unit, head_size), stacked_heads(other_ref, number * unit, unit, head_size)], axis=0
         )
         rows = slice(number * query.shape[0], (number + 1) * query.shape[0])
         before, largest, total, group = (state_ref[rows, spot * head_size : (spot + 1) * head_size] for spot in range(4))
@@ -349,7 +352,6 @@
 def local(req_count, tp_count, queries, tree_kv, suffix_kv, suffix_len, group_ids, parents, accepted, prompt_kv, out_weight):
     chunk_rows = queries.shape[0] // tp_count
     unit = math.gcd(chunk_rows, parents.shape[1])
-    other_queries = swap_in_pair(queries, tp_count)
     if req_count == 8 and tp_count % 2 == 0:
         fetched = fetch_shards(prompt_kv, req_count, tp_count)
         other_weight = swap_in_pair(out_weight, tp_count)
@@ -357,14 +359,15 @@
         fetched = None
         other_weight = swap_in_pair(out_weight, tp_count)
     requests, node_count = parents.shape
-    *loaded, shard, own_weight = load(unit, chunk_rows, parents, suffix_len, group_ids, queries, tree_kv, suffix_kv, prompt_kv, out_weight)
+    *loaded, pair_queries, shard, own_weight = load(unit, chunk_rows, parents, suffix_len, group_ids, queries, tree_kv, suffix_kv, prompt_kv, out_weight)
+    far_queries = touched(swap_in_pair(pair_queries, tp_count))
     if fetched is None:
         pieces = [lax.all_gather(prompt_kv, "req", axis=1, tiled=True)]
-        state = private(unit, chunk_rows, node_count, requests, loaded, other_queries, [])
+        state = private(unit, chunk_rows, node_count, requests, loaded, far_queries, [])
     else:
         joined = jnp.concatenate([after(piece, shard) for piece in fetched], axis=0)
         pieces = [shard, joined, swap_in_pair(joined, tp_count)]
-        state = private(unit, chunk_rows, node_count, requests, loaded, other_queries, pieces[:2])
+        state = private(unit, chunk_rows, node_count, requests, loaded, far_queries, pieces[:2])
     parts = pieces[-2:]
     weights = (own_weight, other_weight)
     columns = out_weight.shape[1]
@@ -373,7 +376,7 @@
     early_far, attended = chunk(
         functools.partial(far_kernel, unit, len(parts)), "far_chunk",
         [jax.ShapeDtypeStruct((chunk_rows, early), jnp.bfloat16), jax.ShapeDtypeStruct(attended_shape, jnp.bfloat16)],
-        (), (loaded[2], other_queries, state, *parts), weights, flops=200_000_000
+        (), (loaded[2], far_queries, state, *parts), weights, flops=200_000_000
     )
     across = [(t, t ^ 2) for t in range(tp_count)]
     early_arrived = touched(lax.ppermute(early_far, "tp", across))
@@ -382,6 +385,7 @@
         (), (attended,), weights, flops=300_000_000
     )
     late_arrived = lax.ppermute(late_far, "tp", across)
+    other_queries = swap_in_pair(after(queries, late_far), tp_count)
     near, path_cache = chunk(
         functools.partial(near_kernel, unit, len(pieces)), "near_chunk",
         [jax.ShapeDtypeStruct((chunk_rows, columns), jnp.float32), jax.ShapeDtypeStruct((*accepted.shape, tree_kv.shape[1]), jnp.bfloat16)],

time: 27.1 us -> 26.7 us (0.985)
  waiting for transfers between devices: 5.46 us -> 5.05 us
    ppermute x1, waiting for transfers between devices: 5.14 us -> 2.78 us  [local(): late_arrived = lax.ppermute(late_far, 'tp', across)]
    ppermute x1, waiting for transfers between devices: 0.01 us -> 2.25 us  [local(): early_arrived = touched(lax.ppermute(early_far, 'tp', across))]
    ppermute x3 -> x4, waiting for transfers between devices: 0.29 us -> 0.01 us  [swap_in_pair(): return lax.ppermute(array, 'tp', [(t, t ^ 1) for t in range(tp_count)])]
    ppermute x3 -> x4, starting transfers between devices: 2.43 us -> 2.38 us  [swap_in_pair(): return lax.ppermute(array, 'tp', [(t, t ^ 1) for t in range(tp_count)])]
  transfers between devices with their start and end apart: 9 -> 10, of which waited for: 2 -> 2; matrix products, arithmetic and copies ran while one was open for 0% -> 0% of each run, Pallas kernels for 26% -> 27%
where the time goes in v7:
time: 26.7 us; the launch traced here: 26.5 us
  starting transfers between devices  11.6 us (43%)
  Pallas kernels  8.97 us (34%)
  waiting for transfers between devices  5.05 us (19%)
  between operations  0.81 us (3%)
    ppermute x4, starting transfers between devices, fetch_shards(): arrived.append(lax.ppermute(shard, ('req', 'tp'), pairs))  7.12 us
    pallas_call x4, Pallas kernels, chunk(): pl.pallas_call(kernel, in_specs=[in_smem()] * len(scalars) + [in_vmem()]...  5.82 us
    ppermute x1, waiting for transfers between devices, local(): late_arrived = lax.ppermute(late_far, 'tp', across)  2.78 us
    ppermute x4, starting transfers between devices, swap_in_pair(): return lax.ppermute(array, 'tp', [(t, t ^ 1) for t in range(tp_count)])  2.38 us
    ppermute x1, waiting for transfers between devices, local(): early_arrived = touched(lax.ppermute(early_far, 'tp', across))  2.25 us
    pallas_call x1, Pallas kernels, load(): pl.pallas_call(functools.partial(load_kernel, chunk_rows), in_specs=[pl.B...  1.95 us
    ppermute x1, starting transfers between devices, local(): early_arrived = touched(lax.ppermute(early_far, 'tp', across))  1.54 us
    pallas_call x1, Pallas kernels, private(): pl.pallas_call(functools.partial(private_kernel, unit, chunk_rows, node_c...  1.2 us
  transfers between devices with their start and end apart: 10, of which 2 were waited for; matrix products, arithmetic and copies ran while one was open for 0% of the time, Pallas kernels for 27%

profile of v7, /device:TPU:0, one launch (start us, length us, event | category | flops | bytes accessed | tf_op | source)
XLA Modules:
  0.0 26.5 jit_solution(5927815043231710298)
XLA Ops:
  0.6 0.5 %collective-permute-start.6 = (bf16[512,2048]{1,0:T(8,128)(2,1)}, bf16[512,2048]{1,0:T(8,128)(2,1)S(1)}, u32[]{:S(2)}, u32[]{:S(2)}) collective-permute-start(bf16[512,2048]{1,0:T(8,128)(2,1)} %weight_hbm.1), channel_id=1, source_target_pairs={{0,1},{1,0},{2,3},{3,2},{4,5},{5,4},{6,7},{7,6},{8,9},{9,8},{10,11... | collective-permute-start | bytes 6291464 | tf_op jit(solution)/shard_map/ppermute | solution.py:52
  1.1 3.7 %collective-permute-start.1 = (bf16[2,32,256]{2,1,0:T(8,128)(2,1)}, bf16[2,32,256]{2,1,0:T(8,128)(2,1)S(1)}, u32[]{:S(2)}, u32[]{:S(2)}) collective-permute-start(bf16[2,32,256]{2,1,0:T(8,128)(2,1)} %shard_hbm.1), channel_id=1, source_target_pairs={{0,16},{1,25},{2,18},{3,27},{4,20},{5,29},{6,22},{7,31},{8,24},{9,... | collective-permute-start | bytes 98312 | tf_op jit(solution)/shard_map/ppermute | solution.py:26
  4.8 1.3 %collective-permute-start.2 = (bf16[2,32,256]{2,1,0:T(8,128)(2,1)}, bf16[2,32,256]{2,1,0:T(8,128)(2,1)S(1)}, u32[]{:S(2)}, u32[]{:S(2)}) collective-permute-start(bf16[2,32,256]{2,1,0:T(8,128)(2,1)} %shard_hbm.1), channel_id=1, source_target_pairs={{0,20},{1,29},{2,22},{3,31},{4,16},{5,25},{6,18},{7,27},{8,28},{9,... | collective-permute-start | bytes 98312 | tf_op jit(solution)/shard_map/ppermute | solution.py:26
  6.1 1.5 %collective-permute-start.3 = (bf16[2,32,256]{2,1,0:T(8,128)(2,1)}, bf16[2,32,256]{2,1,0:T(8,128)(2,1)S(1)}, u32[]{:S(2)}, u32[]{:S(2)}) collective-permute-start(bf16[2,32,256]{2,1,0:T(8,128)(2,1)} %shard_hbm.1), channel_id=1, source_target_pairs={{0,12},{1,9},{2,14},{3,11},{4,8},{5,13},{6,10},{7,15},{8,4},{9,1},... | collective-permute-start | bytes 98312 | tf_op jit(solution)/shard_map/ppermute | solution.py:26
  7.6 0.7 %collective-permute-start.4 = (bf16[2,32,256]{2,1,0:T(8,128)(2,1)}, bf16[2,32,256]{2,1,0:T(8,128)(2,1)S(1)}, u32[]{:S(2)}, u32[]{:S(2)}) collective-permute-start(bf16[2,32,256]{2,1,0:T(8,128)(2,1)} %shard_hbm.1), channel_id=1, source_target_pairs={{1,5},{3,7},{5,1},{7,3},{9,13},{11,15},{13,9},{15,11},{17,21},{19,... | collective-permute-start | bytes 98312 | tf_op jit(solution)/shard_map/ppermute | solution.py:26
  8.3 1.9 %load.1 = (f32[128,64]{1,0:T(8,128)S(1)}, f32[2,8,256]{2,1,0:T(8,128)S(1)}, bf16[96,512]{1,0:T(8,128)(2,1)S(1)}, bf16[128,256]{1,0:T(8,128)(2,1)S(1)}, bf16[2,25...) custom-call(s32[6,64]{1,0:T(8,128)} %parents_ref.1, ...), custom_call_target="tpu_custom_call" | custom-call | flops 100000000 | bytes 2000000 | tf_op jit(solution)/shard_map/load/pallas_call | solution.py:231
  10.2 0.0 collective-permute-done.1
  10.2 0.9 %collective-permute-start = (bf16[96,512]{1,0:T(8,128)(2,1)S(1)}, bf16[96,512]{1,0:T(8,128)(2,1)S(1)}, u32[]{:S(2)}, u32[]{:S(2)}) collective-permute-start(bf16[96,512]{1,0:T(8,128)(2,1)S(1)} %get-tuple-element.20), channel_id=1, source_target_pairs={{0,1},{1,0},{2,3},{3,2},{4,5},{5,4},{6,7},{7,6},{8,9},{9,8},{10,11... | collective-permute-start | bytes 294920 | tf_op jit(solution)/shard_map/ppermute | solution.py:52
  11.2 0.0 collective-permute-done.2
  11.2 0.0 collective-permute-done.3
  11.2 0.0 collective-permute-done.4
  11.2 0.9 %collective-permute-start.5 = (bf16[8,32,256]{2,1,0:T(8,128)(2,1)S(1)}, bf16[8,32,256]{2,1,0:T(8,128)(2,1)S(1)}, u32[]{:S(2)}, u32[]{:S(2)}) collective-permute-start(bf16[8,32,256]{2,1,0:T(8,128)(2,1)S(1)} %constant_dynamic-update-slice_fusion.rest_1_.rest_0_), channel_id=1, source_target_pairs={{0,1},{1,0},{2,3},{3,2},{4,5},{5,4},{6,7},{7,6},{8,9},{9,8},{10,11... | collective-permute-start | bytes 393224 | tf_op jit(solution)/shard_map/ppermute | solution.py:52
  12.2 0.0 collective-permute-done.in_ref
  12.2 1.2 %private.1.state_ref = f32[768,512]{1,0:T(8,128)S(1)} custom-call(f32[128,64]{1,0:T(8,128)S(1)} %get-tuple-element.21.bias_ref, f32[2,8,256]{2,1,0:T(8,128)S(1)} %get-tuple-element.22.notes_ref, bf16[96,512]{1,0:T(8,128)(2,1)S(1)} %get-tuple-element.19.own_ref, bf16[128,256]{1,0:T(8,128)(2,1)S(1)} %get-tuple-element.23.tree_ref, ...), custom_call_target="tpu_custom_call" | custom-call | flops 300000000 | bytes 500000 | tf_op jit(solution)/shard_map/private/pallas_call | solution.py:261
  13.4 0.0 collective-permute-done.5.rest_1_.rest_2_
  13.4 0.0 collective-permute-done.6.rest_3_.weight_other_ref.rest_4_
  13.4 1.0 %far_chunk.1 = (bf16[96,512]{1,0:T(8,128)(2,1)S(1)}, bf16[96,1024]{1,0:T(8,128)(2,1)S(1)}) custom-call(bf16[96,512]{1,0:T(8,128)(2,1)S(1)} %get-tuple-element.19.own_ref, bf16[96,512]{1,0:T(8,128)(2,1)S(1)} %touch.2.other_ref, f32[768,512]{1,0:T(8,128)S(1)} %private.1.state_ref, bf16[8,32,256]{2,1,0:T(8,128)(2,1)S(1)} %constant_dynamic-update-slice_fusion.rest_1_.rest_0_, ...), custom_call_target="tpu_custom_call" | custom-call | flops 200000000 | bytes 1000000 | tf_op jit(solution)/shard_map/far_chunk/pallas_call | solution.py:340
  14.4 1.5 %collective-permute-start.8 = (bf16[96,512]{1,0:T(8,128)(2,1)S(1)}, bf16[96,512]{1,0:T(8,128)(2,1)S(1)}, u32[]{:S(2)}, u32[]{:S(2)}) collective-permute-start(bf16[96,512]{1,0:T(8,128)(2,1)S(1)} %get-tuple-element.34), channel_id=1, source_target_pairs={{0,2},{1,3},{2,0},{3,1},{4,6},{5,7},{6,4},{7,5},{8,10},{9,11},{10,... | collective-permute-start | bytes 294920 | tf_op jit(solution)/shard_map/ppermute | solution.py:382
  15.9 0.0 copy-start.1
  15.9 0.6 %far_rest.1 = bf16[96,1536]{1,0:T(8,128)(2,1)S(1)} custom-call(bf16[96,1024]{1,0:T(8,128)(2,1)S(1)} %get-tuple-element.31.attended_ref, bf16[512,2048]{1,0:T(8,128)(2,1)S(1)} %get-tuple-element.30.rest_2_.weight_own_ref.rest_3_, bf16[512,2048]{1,0:T(8,128)(2,1)S(1)} %collective-permute-done.6.rest_3_.weight_other_ref.rest_4_), custom_call_target="tpu_custom_call" | custom-call | flops 300000000 | bytes 1000000 | tf_op jit(solution)/shard_map/far_rest/pallas_call | solution.py:340
  16.6 0.0 copy-start
  16.6 0.0 copy-start.2
  16.6 0.0 copy-start.3
  16.6 0.0 copy-start.4
  16.6 0.0 copy-start.5
  16.6 0.0 copy-start.6
  16.6 0.6 %collective-permute-start.9 = (bf16[96,1536]{1,0:T(8,128)(2,1)S(1)}, bf16[96,1536]{1,0:T(8,128)(2,1)S(1)}, u32[]{:S(2)}, u32[]{:S(2)}) collective-permute-start(bf16[96,1536]{1,0:T(8,128)(2,1)S(1)} %far_rest.1), channel_id=1, source_target_pairs={{0,2},{1,3},{2,0},{3,1},{4,6},{5,7},{6,4},{7,5},{8,10},{9,11},{10,... | collective-permute-start | bytes 884744 | tf_op jit(solution)/shard_map/ppermute | solution.py:387
  17.2 0.0 copy-done.1
  17.2 0.0 collective-permute-start.7
  17.2 2.2 %collective-permute-done.8.in_ref = bf16[96,512]{1,0:T(8,128)(2,1)S(1)} collective-permute-done((bf16[96,512]{1,0:T(8,128)(2,1)S(1)}, bf16[96,512]{1,0:T(8,128)(2,1)S(1)}, u32[]{:S(2)}, u32[]{:S(2)}) %collective-permute-start.8) | collective-permute-done | bytes 98336 | tf_op jit(solution)/shard_map/ppermute | solution.py:382
  19.5 0.0 collective-permute-done.7.other_ref
  19.5 0.0 copy-done
  19.5 0.0 copy-done.2
  19.5 0.0 copy-done.3
  19.5 0.0 copy-done.4
  19.5 0.0 copy-done.5
  19.5 0.0 copy-done.6
  19.5 3.4 %near_chunk.1 = (f32[96,2048]{1,0:T(8,128)S(1)}, bf16[6,8,256]{2,1,0:T(8,128)(2,1)}) custom-call(s32[6]{0:T(128)S(1)} %copy-done.5, s32[6]{0:T(128)S(1)} %copy-done.6, bf16[384,512]{1,0:T(8,128)(2,1)S(1)} %copy-done.1, bf16[384,512]{1,0:T(8,128)(2,1)S(1)} %collective-permute-done.7.other_ref, s32[6,64]{1,0:T(8,128)S(1)} %copy-done.3, s32[6,8]{1,0:T(8,128)S(1)} %copy-done.4, ...), custom_call_target="tpu_custom_call" | custom-call | flops 500000000 | bytes 1000000 | tf_op jit(solution)/shard_map/near_chunk/pallas_call | solution.py:340
  22.9 2.8 %collective-permute-done.9.rest_1_ = bf16[96,1536]{1,0:T(8,128)(2,1)S(1)} collective-permute-done((bf16[96,1536]{1,0:T(8,128)(2,1)S(1)}, bf16[96,1536]{1,0:T(8,128)(2,1)S(1)}, u32[]{:S(2)}, u32[]{:S(2)}) %collective-permute-start.9) | collective-permute-done | bytes 294944 | tf_op jit(solution)/shard_map/ppermute | solution.py:387
  25.7 0.8 %sum.1 = bf16[96,2048]{1,0:T(8,128)(2,1)} custom-call(f32[96,2048]{1,0:T(8,128)S(1)} %get-tuple-element.33.near_ref, bf16[96,512]{1,0:T(8,128)(2,1)S(1)} %touch.3.rest_0_, bf16[96,1536]{1,0:T(8,128)(2,1)S(1)} %collective-permute-done.9.rest_1_), custom_call_target="tpu_custom_call" | custom-call | flops 1000000 | bytes 1000000 | tf_op jit(solution)/shard_map/sum/pallas_call | solution.py:340
  (6 shorter events, 0.0 us)
Async XLA Ops:
  0.6 12.8 %collective-permute-start.6 = (bf16[512,2048]{1,0:T(8,128)(2,1)}, bf16[512,2048]{1,0:T(8,128)(2,1)S(1)}, u32[]{:S(2)}, u32[]{:S(2)}) collective-permute-start(bf16[512,2048]{1,0:T(8,128)(2,1)} %weight_hbm.1), channel_id=1, source_target_pairs={{0,1},{1,0},{2,3},{3,2},{4,5},{5,4},{6,7},{7,6},{8,9},{9,8},{10,11... | collective-permute-start | bytes 6291464 | tf_op jit(solution)/shard_map/ppermute | solution.py:52
  1.1 9.1 %collective-permute-start.1 = (bf16[2,32,256]{2,1,0:T(8,128)(2,1)}, bf16[2,32,256]{2,1,0:T(8,128)(2,1)S(1)}, u32[]{:S(2)}, u32[]{:S(2)}) collective-permute-start(bf16[2,32,256]{2,1,0:T(8,128)(2,1)} %shard_hbm.1), channel_id=1, source_target_pairs={{0,16},{1,25},{2,18},{3,27},{4,20},{5,29},{6,22},{7,31},{8,24},{9,... | collective-permute-start | bytes 98312 | tf_op jit(solution)/shard_map/ppermute | solution.py:26
  4.8 6.3 %collective-permute-start.2 = (bf16[2,32,256]{2,1,0:T(8,128)(2,1)}, bf16[2,32,256]{2,1,0:T(8,128)(2,1)S(1)}, u32[]{:S(2)}, u32[]{:S(2)}) collective-permute-start(bf16[2,32,256]{2,1,0:T(8,128)(2,1)} %shard_hbm.1), channel_id=1, source_target_pairs={{0,20},{1,29},{2,22},{3,31},{4,16},{5,25},{6,18},{7,27},{8,28},{9,... | collective-permute-start | bytes 98312 | tf_op jit(solution)/shard_map/ppermute | solution.py:26
  6.1 5.1 %collective-permute-start.3 = (bf16[2,32,256]{2,1,0:T(8,128)(2,1)}, bf16[2,32,256]{2,1,0:T(8,128)(2,1)S(1)}, u32[]{:S(2)}, u32[]{:S(2)}) collective-permute-start(bf16[2,32,256]{2,1,0:T(8,128)(2,1)} %shard_hbm.1), channel_id=1, source_target_pairs={{0,12},{1,9},{2,14},{3,11},{4,8},{5,13},{6,10},{7,15},{8,4},{9,1},... | collective-permute-start | bytes 98312 | tf_op jit(solution)/shard_map/ppermute | solution.py:26
  7.6 3.5 %collective-permute-start.4 = (bf16[2,32,256]{2,1,0:T(8,128)(2,1)}, bf16[2,32,256]{2,1,0:T(8,128)(2,1)S(1)}, u32[]{:S(2)}, u32[]{:S(2)}) collective-permute-start(bf16[2,32,256]{2,1,0:T(8,128)(2,1)} %shard_hbm.1), channel_id=1, source_target_pairs={{1,5},{3,7},{5,1},{7,3},{9,13},{11,15},{13,9},{15,11},{17,21},{19,... | collective-permute-start | bytes 98312 | tf_op jit(solution)/shard_map/ppermute | solution.py:26
  10.2 1.9 %collective-permute-start = (bf16[96,512]{1,0:T(8,128)(2,1)S(1)}, bf16[96,512]{1,0:T(8,128)(2,1)S(1)}, u32[]{:S(2)}, u32[]{:S(2)}) collective-permute-start(bf16[96,512]{1,0:T(8,128)(2,1)S(1)} %get-tuple-element.20), channel_id=1, source_target_pairs={{0,1},{1,0},{2,3},{3,2},{4,5},{5,4},{6,7},{7,6},{8,9},{9,8},{10,11... | collective-permute-start | bytes 294920 | tf_op jit(solution)/shard_map/ppermute | solution.py:52
  11.2 2.2 %collective-permute-start.5 = (bf16[8,32,256]{2,1,0:T(8,128)(2,1)S(1)}, bf16[8,32,256]{2,1,0:T(8,128)(2,1)S(1)}, u32[]{:S(2)}, u32[]{:S(2)}) collective-permute-start(bf16[8,32,256]{2,1,0:T(8,128)(2,1)S(1)} %constant_dynamic-update-slice_fusion.rest_1_.rest_0_), channel_id=1, source_target_pairs={{0,1},{1,0},{2,3},{3,2},{4,5},{5,4},{6,7},{7,6},{8,9},{9,8},{10,11... | collective-permute-start | bytes 393224 | tf_op jit(solution)/shard_map/ppermute | solution.py:52
  14.4 5.1 %collective-permute-start.8 = (bf16[96,512]{1,0:T(8,128)(2,1)S(1)}, bf16[96,512]{1,0:T(8,128)(2,1)S(1)}, u32[]{:S(2)}, u32[]{:S(2)}) collective-permute-start(bf16[96,512]{1,0:T(8,128)(2,1)S(1)} %get-tuple-element.34), channel_id=1, source_target_pairs={{0,2},{1,3},{2,0},{3,1},{4,6},{5,7},{6,4},{7,5},{8,10},{9,11},{10,... | collective-permute-start | bytes 294920 | tf_op jit(solution)/shard_map/ppermute | solution.py:382
  15.9 1.3 %copy-start.1 = (bf16[384,512]{1,0:T(8,128)(2,1)S(1)}, bf16[384,512]{1,0:T(8,128)(2,1)}, u32[]{:S(2)}) copy-start(bf16[384,512]{1,0:T(8,128)(2,1)} %own_ref.1) | copy-start | bytes 1179652
  16.6 2.9 %copy-start = (bf16[6,256,256]{2,1,0:T(8,128)(2,1)S(1)}, bf16[6,256,256]{2,1,0:T(8,128)(2,1)}, u32[]{:S(2)}) copy-start(bf16[6,256,256]{2,1,0:T(8,128)(2,1)} %suffix_ref.1) | copy-start | bytes 2359300
  16.6 2.9 %copy-start.2 = (bf16[384,256]{1,0:T(8,128)(2,1)S(1)}, bf16[384,256]{1,0:T(8,128)(2,1)}, u32[]{:S(2)}) copy-start(bf16[384,256]{1,0:T(8,128)(2,1)} %tree_ref.1) | copy-start | bytes 589828
  16.6 2.9 %copy-start.3 = (s32[6,64]{1,0:T(8,128)S(1)}, s32[6,64]{1,0:T(8,128)}, u32[]{:S(2)}) copy-start(s32[6,64]{1,0:T(8,128)} %parents_ref.1) | copy-start | bytes 4612
  16.6 2.9 %copy-start.4 = (s32[6,8]{1,0:T(8,128)S(1)}, s32[6,8]{1,0:T(8,128)}, u32[]{:S(2)}) copy-start(s32[6,8]{1,0:T(8,128)} %accepted_ref.1) | copy-start | bytes 580
  16.6 2.9 %copy-start.5 = (s32[6]{0:T(128)S(1)}, s32[6]{0:T(128)}, u32[]{:S(2)}) copy-start(s32[6]{0:T(128)} %length_ref.1) | copy-start | bytes 76
  16.6 2.9 %copy-start.6 = (s32[6]{0:T(128)S(1)}, s32[6]{0:T(128)}, u32[]{:S(2)}) copy-start(s32[6]{0:T(128)} %group_ref.1) | copy-start | bytes 76
  16.6 9.1 %collective-permute-start.9 = (bf16[96,1536]{1,0:T(8,128)(2,1)S(1)}, bf16[96,1536]{1,0:T(8,128)(2,1)S(1)}, u32[]{:S(2)}, u32[]{:S(2)}) collective-permute-start(bf16[96,1536]{1,0:T(8,128)(2,1)S(1)} %far_rest.1), channel_id=1, source_target_pairs={{0,2},{1,3},{2,0},{3,1},{4,6},{5,7},{6,4},{7,5},{8,10},{9,11},{10,... | collective-permute-start | bytes 884744 | tf_op jit(solution)/shard_map/ppermute | solution.py:387
  17.2 2.3 %collective-permute-start.7 = (bf16[384,512]{1,0:T(8,128)(2,1)S(1)}, bf16[384,512]{1,0:T(8,128)(2,1)S(1)}, u32[]{:S(2)}, u32[]{:S(2)}) collective-permute-start(bf16[384,512]{1,0:T(8,128)(2,1)S(1)} %copy-done.1), channel_id=1, source_target_pairs={{0,1},{1,0},{2,3},{3,2},{4,5},{5,4},{6,7},{7,6},{8,9},{9,8},{10,11... | collective-permute-start | bytes 1179656 | tf_op jit(solution)/shard_map/ppermute | solution.py:52

commit v8 on v7

--- a/solution.py
+++ b/solution.py
@@ -111,13 +111,33 @@
     project(attended_ref, weight_own_ref, weight_other_ref, out_ref, first)
 
 
-def sum_kernel(near_ref, *rest):
-    *arrived, out_ref = rest
-    first = 0
-    for part_ref in arrived:
-        columns = slice(first, first + part_ref.shape[1])
-        out_ref[:, columns] = (near_ref[:, columns] + part_ref[...].astype(jnp.float32)).astype(out_ref.dtype)
-        first += part_ref.shape[1]
+def sum_kernel(piece_rows, near_ref, *rest):
+    *arrived, out_hbm, total_ref, sent = rest
+    copies = []
+    for place, row in enumerate(range(0, near_ref.shape[0], piece_rows)):
+        rows = slice(row, row + piece_rows)
+        first = 0
+        for part_ref in arrived:
+            columns = slice(first, first + part_ref.shape[1])
+            total_ref[rows, columns] = (near_ref[rows, columns] + part_ref[rows, :].astype(jnp.float32)).astype(total_ref.dtype)
+            first += part_ref.shape[1]
+        copies.append(pltpu.make_async_copy(total_ref.at[rows], out_hbm.at[rows], sent.at[place]))
+        copies[-1].start()
+    for copy in copies:
+        copy.wait()
+
+
+def sum_parts(unit, near, arrived):
+    return pl.pallas_call(
+        functools.partial(sum_kernel, unit),
+        in_specs=[in_vmem()] * (1 + len(arrived)),
+        out_specs=pl.BlockSpec(memory_space=pl.ANY),
+        out_shape=jax.ShapeDtypeStruct(near.shape, jnp.bfloat16),
+        scratch_shapes=[pltpu.VMEM(near.shape, jnp.bfloat16), pltpu.SemaphoreType.DMA((near.shape[0] // unit,))],
+        compiler_params=pltpu.CompilerParams(vmem_limit_bytes=vmem_bytes),
+        name="sum",
+        cost_estimate=pl.CostEstimate(flops=1_000_000, bytes_accessed=1_000_000, transcendentals=0),
+    )(near, *arrived)
 
 
 def put_heads(attended_ref, number, unit, attended):
@@ -392,9 +412,7 @@
         (suffix_len, group_ids), (queries, other_queries, parents, accepted, tree_kv, suffix_kv, *pieces), weights,
         (pltpu.VMEM(attended_shape, jnp.bfloat16), pltpu.VMEM((requests * node_count, node_count), jnp.float32))
     )
-    (layer_output,) = chunk(
-        sum_kernel, "sum", [jax.ShapeDtypeStruct((chunk_rows, columns), jnp.bfloat16)], (), (near, early_arrived, late_arrived), (), flops=1_000_000
-    )
+    layer_output = sum_parts(unit, near, (early_arrived, late_arrived))
     return (layer_output, path_cache)
 
 

time: 26.7 us -> 26.7 us (level)
    pallas_call x4 -> x3, Pallas kernels: 5.82 us -> 5.01 us  [chunk(): pl.pallas_call(kernel, in_specs=[in_smem()] * len(scalars) + [in_vmem()]...]
    pallas_call x0 -> x1, Pallas kernels: none -> 0.8 us  [sum_parts(): pl.pallas_call(functools.partial(sum_kernel, unit), in_specs=[in_vmem()]...]
where the time goes in v8:
time: 26.7 us; the launch traced here: 26.5 us
  starting transfers between devices  11.6 us (43%)
  Pallas kernels  8.95 us (34%)
  waiting for transfers between devices  5.05 us (19%)
  between operations  0.81 us (3%)
    ppermute x4, starting transfers between devices, fetch_shards(): arrived.append(lax.ppermute(shard, ('req', 'tp'), pairs))  7.12 us
    pallas_call x3, Pallas kernels, chunk(): pl.pallas_call(kernel, in_specs=[in_smem()] * len(scalars) + [in_vmem()]...  5.01 us
    ppermute x1, waiting for transfers between devices, local(): late_arrived = lax.ppermute(late_far, 'tp', across)  2.78 us
    ppermute x4, starting transfers between devices, swap_in_pair(): return lax.ppermute(array, 'tp', [(t, t ^ 1) for t in range(tp_count)])  2.38 us
    ppermute x1, waiting for transfers between devices, local(): early_arrived = touched(lax.ppermute(early_far, 'tp', across))  2.25 us
    pallas_call x1, Pallas kernels, load(): pl.pallas_call(functools.partial(load_kernel, chunk_rows), in_specs=[pl.B...  1.95 us
    ppermute x1, starting transfers between devices, local(): early_arrived = touched(lax.ppermute(early_far, 'tp', across))  1.54 us
    pallas_call x1, Pallas kernels, private(): pl.pallas_call(functools.partial(private_kernel, unit, chunk_rows, node_c...  1.2 us
  transfers between devices with their start and end apart: 10, of which 2 were waited for; matrix products, arithmetic and copies ran while one was open for 0% of the time, Pallas kernels for 27%

profile of v8, /device:TPU:0, one launch (start us, length us, event | category | flops | bytes accessed | tf_op | source)
XLA Modules:
  0.0 26.5 jit_solution(18223990312990059098)
XLA Ops:
  0.6 0.5 %collective-permute-start.6 = (bf16[512,2048]{1,0:T(8,128)(2,1)}, bf16[512,2048]{1,0:T(8,128)(2,1)S(1)}, u32[]{:S(2)}, u32[]{:S(2)}) collective-permute-start(bf16[512,2048]{1,0:T(8,128)(2,1)} %weight_hbm.1), channel_id=1, source_target_pairs={{0,1},{1,0},{2,3},{3,2},{4,5},{5,4},{6,7},{7,6},{8,9},{9,8},{10,11... | collective-permute-start | bytes 6291464 | tf_op jit(solution)/shard_map/ppermute | solution.py:52
  1.1 3.7 %collective-permute-start.1 = (bf16[2,32,256]{2,1,0:T(8,128)(2,1)}, bf16[2,32,256]{2,1,0:T(8,128)(2,1)S(1)}, u32[]{:S(2)}, u32[]{:S(2)}) collective-permute-start(bf16[2,32,256]{2,1,0:T(8,128)(2,1)} %shard_hbm.1), channel_id=1, source_target_pairs={{0,16},{1,25},{2,18},{3,27},{4,20},{5,29},{6,22},{7,31},{8,24},{9,... | collective-permute-start | bytes 98312 | tf_op jit(solution)/shard_map/ppermute | solution.py:26
  4.8 1.3 %collective-permute-start.2 = (bf16[2,32,256]{2,1,0:T(8,128)(2,1)}, bf16[2,32,256]{2,1,0:T(8,128)(2,1)S(1)}, u32[]{:S(2)}, u32[]{:S(2)}) collective-permute-start(bf16[2,32,256]{2,1,0:T(8,128)(2,1)} %shard_hbm.1), channel_id=1, source_target_pairs={{0,20},{1,29},{2,22},{3,31},{4,16},{5,25},{6,18},{7,27},{8,28},{9,... | collective-permute-start | bytes 98312 | tf_op jit(solution)/shard_map/ppermute | solution.py:26
  6.1 1.5 %collective-permute-start.3 = (bf16[2,32,256]{2,1,0:T(8,128)(2,1)}, bf16[2,32,256]{2,1,0:T(8,128)(2,1)S(1)}, u32[]{:S(2)}, u32[]{:S(2)}) collective-permute-start(bf16[2,32,256]{2,1,0:T(8,128)(2,1)} %shard_hbm.1), channel_id=1, source_target_pairs={{0,12},{1,9},{2,14},{3,11},{4,8},{5,13},{6,10},{7,15},{8,4},{9,1},... | collective-permute-start | bytes 98312 | tf_op jit(solution)/shard_map/ppermute | solution.py:26
  7.6 0.7 %collective-permute-start.4 = (bf16[2,32,256]{2,1,0:T(8,128)(2,1)}, bf16[2,32,256]{2,1,0:T(8,128)(2,1)S(1)}, u32[]{:S(2)}, u32[]{:S(2)}) collective-permute-start(bf16[2,32,256]{2,1,0:T(8,128)(2,1)} %shard_hbm.1), channel_id=1, source_target_pairs={{1,5},{3,7},{5,1},{7,3},{9,13},{11,15},{13,9},{15,11},{17,21},{19,... | collective-permute-start | bytes 98312 | tf_op jit(solution)/shard_map/ppermute | solution.py:26
  8.3 1.9 %load.1 = (f32[128,64]{1,0:T(8,128)S(1)}, f32[2,8,256]{2,1,0:T(8,128)S(1)}, bf16[96,512]{1,0:T(8,128)(2,1)S(1)}, bf16[128,256]{1,0:T(8,128)(2,1)S(1)}, bf16[2,25...) custom-call(s32[6,64]{1,0:T(8,128)} %parents_ref.1, ...), custom_call_target="tpu_custom_call" | custom-call | flops 100000000 | bytes 2000000 | tf_op jit(solution)/shard_map/load/pallas_call | solution.py:251
  10.2 0.0 collective-permute-done.1
  10.2 0.9 %collective-permute-start = (bf16[96,512]{1,0:T(8,128)(2,1)S(1)}, bf16[96,512]{1,0:T(8,128)(2,1)S(1)}, u32[]{:S(2)}, u32[]{:S(2)}) collective-permute-start(bf16[96,512]{1,0:T(8,128)(2,1)S(1)} %get-tuple-element.20), channel_id=1, source_target_pairs={{0,1},{1,0},{2,3},{3,2},{4,5},{5,4},{6,7},{7,6},{8,9},{9,8},{10,11... | collective-permute-start | bytes 294920 | tf_op jit(solution)/shard_map/ppermute | solution.py:52
  11.2 0.0 collective-permute-done.2
  11.2 0.0 collective-permute-done.3
  11.2 0.0 collective-permute-done.4
  11.2 0.9 %collective-permute-start.5 = (bf16[8,32,256]{2,1,0:T(8,128)(2,1)S(1)}, bf16[8,32,256]{2,1,0:T(8,128)(2,1)S(1)}, u32[]{:S(2)}, u32[]{:S(2)}) collective-permute-start(bf16[8,32,256]{2,1,0:T(8,128)(2,1)S(1)} %constant_dynamic-update-slice_fusion.rest_1_.rest_0_), channel_id=1, source_target_pairs={{0,1},{1,0},{2,3},{3,2},{4,5},{5,4},{6,7},{7,6},{8,9},{9,8},{10,11... | collective-permute-start | bytes 393224 | tf_op jit(solution)/shard_map/ppermute | solution.py:52
  12.2 0.0 collective-permute-done.in_ref
  12.2 1.2 %private.1.state_ref = f32[768,512]{1,0:T(8,128)S(1)} custom-call(f32[128,64]{1,0:T(8,128)S(1)} %get-tuple-element.21.bias_ref, f32[2,8,256]{2,1,0:T(8,128)S(1)} %get-tuple-element.22.notes_ref, bf16[96,512]{1,0:T(8,128)(2,1)S(1)} %get-tuple-element.19.own_ref, bf16[128,256]{1,0:T(8,128)(2,1)S(1)} %get-tuple-element.23.tree_ref, ...), custom_call_target="tpu_custom_call" | custom-call | flops 300000000 | bytes 500000 | tf_op jit(solution)/shard_map/private/pallas_call | solution.py:281
  13.4 0.0 collective-permute-done.5.rest_1_.rest_2_
  13.4 0.0 collective-permute-done.6.rest_3_.weight_other_ref.rest_4_
  13.4 1.0 %far_chunk.1 = (bf16[96,512]{1,0:T(8,128)(2,1)S(1)}, bf16[96,1024]{1,0:T(8,128)(2,1)S(1)}) custom-call(bf16[96,512]{1,0:T(8,128)(2,1)S(1)} %get-tuple-element.19.own_ref, bf16[96,512]{1,0:T(8,128)(2,1)S(1)} %touch.2.other_ref, f32[768,512]{1,0:T(8,128)S(1)} %private.1.state_ref, bf16[8,32,256]{2,1,0:T(8,128)(2,1)S(1)} %constant_dynamic-update-slice_fusion.rest_1_.rest_0_, ...), custom_call_target="tpu_custom_call" | custom-call | flops 200000000 | bytes 1000000 | tf_op jit(solution)/shard_map/far_chunk/pallas_call | solution.py:360
  14.4 1.5 %collective-permute-start.8 = (bf16[96,512]{1,0:T(8,128)(2,1)S(1)}, bf16[96,512]{1,0:T(8,128)(2,1)S(1)}, u32[]{:S(2)}, u32[]{:S(2)}) collective-permute-start(bf16[96,512]{1,0:T(8,128)(2,1)S(1)} %get-tuple-element.34), channel_id=1, source_target_pairs={{0,2},{1,3},{2,0},{3,1},{4,6},{5,7},{6,4},{7,5},{8,10},{9,11},{10,... | collective-permute-start | bytes 294920 | tf_op jit(solution)/shard_map/ppermute | solution.py:402
  15.9 0.0 copy-start.1
  15.9 0.6 %far_rest.1 = bf16[96,1536]{1,0:T(8,128)(2,1)S(1)} custom-call(bf16[96,1024]{1,0:T(8,128)(2,1)S(1)} %get-tuple-element.31.attended_ref, bf16[512,2048]{1,0:T(8,128)(2,1)S(1)} %get-tuple-element.30.rest_2_.weight_own_ref.rest_3_, bf16[512,2048]{1,0:T(8,128)(2,1)S(1)} %collective-permute-done.6.rest_3_.weight_other_ref.rest_4_), custom_call_target="tpu_custom_call" | custom-call | flops 300000000 | bytes 1000000 | tf_op jit(solution)/shard_map/far_rest/pallas_call | solution.py:360
  16.6 0.0 copy-start
  16.6 0.0 copy-start.2
  16.6 0.0 copy-start.3
  16.6 0.0 copy-start.4
  16.6 0.0 copy-start.5
  16.6 0.0 copy-start.6
  16.6 0.6 %collective-permute-start.9 = (bf16[96,1536]{1,0:T(8,128)(2,1)S(1)}, bf16[96,1536]{1,0:T(8,128)(2,1)S(1)}, u32[]{:S(2)}, u32[]{:S(2)}) collective-permute-start(bf16[96,1536]{1,0:T(8,128)(2,1)S(1)} %far_rest.1), channel_id=1, source_target_pairs={{0,2},{1,3},{2,0},{3,1},{4,6},{5,7},{6,4},{7,5},{8,10},{9,11},{10,... | collective-permute-start | bytes 884744 | tf_op jit(solution)/shard_map/ppermute | solution.py:407
  17.2 0.0 copy-done.1
  17.2 0.0 collective-permute-start.7
  17.2 2.2 %collective-permute-done.8.in_ref = bf16[96,512]{1,0:T(8,128)(2,1)S(1)} collective-permute-done((bf16[96,512]{1,0:T(8,128)(2,1)S(1)}, bf16[96,512]{1,0:T(8,128)(2,1)S(1)}, u32[]{:S(2)}, u32[]{:S(2)}) %collective-permute-start.8) | collective-permute-done | bytes 98336 | tf_op jit(solution)/shard_map/ppermute | solution.py:402
  19.5 0.0 collective-permute-done.7.other_ref
  19.5 0.0 copy-done
  19.5 0.0 copy-done.2
  19.5 0.0 copy-done.3
  19.5 0.0 copy-done.4
  19.5 0.0 copy-done.5
  19.5 0.0 copy-done.6
  19.5 3.4 %near_chunk.1 = (f32[96,2048]{1,0:T(8,128)S(1)}, bf16[6,8,256]{2,1,0:T(8,128)(2,1)}) custom-call(s32[6]{0:T(128)S(1)} %copy-done.5, s32[6]{0:T(128)S(1)} %copy-done.6, bf16[384,512]{1,0:T(8,128)(2,1)S(1)} %copy-done.1, bf16[384,512]{1,0:T(8,128)(2,1)S(1)} %collective-permute-done.7.other_ref, s32[6,64]{1,0:T(8,128)S(1)} %copy-done.3, s32[6,8]{1,0:T(8,128)S(1)} %copy-done.4, ...), custom_call_target="tpu_custom_call" | custom-call | flops 500000000 | bytes 1000000 | tf_op jit(solution)/shard_map/near_chunk/pallas_call | solution.py:360
  22.9 2.8 %collective-permute-done.9.rest_1_ = bf16[96,1536]{1,0:T(8,128)(2,1)S(1)} collective-permute-done((bf16[96,1536]{1,0:T(8,128)(2,1)S(1)}, bf16[96,1536]{1,0:T(8,128)(2,1)S(1)}, u32[]{:S(2)}, u32[]{:S(2)}) %collective-permute-start.9) | collective-permute-done | bytes 294944 | tf_op jit(solution)/shard_map/ppermute | solution.py:407
  25.7 0.8 %sum.1 = bf16[96,2048]{1,0:T(8,128)(2,1)} custom-call(f32[96,2048]{1,0:T(8,128)S(1)} %get-tuple-element.33.near_ref, bf16[96,512]{1,0:T(8,128)(2,1)S(1)} %touch.3.rest_0_, bf16[96,1536]{1,0:T(8,128)(2,1)S(1)} %collective-permute-done.9.rest_1_), custom_call_target="tpu_custom_call" | custom-call | flops 1000000 | bytes 1000000 | tf_op jit(solution)/shard_map/sum/pallas_call | solution.py:131
  (6 shorter events, 0.0 us)
Async XLA Ops:
  0.6 12.8 %collective-permute-start.6 = (bf16[512,2048]{1,0:T(8,128)(2,1)}, bf16[512,2048]{1,0:T(8,128)(2,1)S(1)}, u32[]{:S(2)}, u32[]{:S(2)}) collective-permute-start(bf16[512,2048]{1,0:T(8,128)(2,1)} %weight_hbm.1), channel_id=1, source_target_pairs={{0,1},{1,0},{2,3},{3,2},{4,5},{5,4},{6,7},{7,6},{8,9},{9,8},{10,11... | collective-permute-start | bytes 6291464 | tf_op jit(solution)/shard_map/ppermute | solution.py:52
  1.1 9.1 %collective-permute-start.1 = (bf16[2,32,256]{2,1,0:T(8,128)(2,1)}, bf16[2,32,256]{2,1,0:T(8,128)(2,1)S(1)}, u32[]{:S(2)}, u32[]{:S(2)}) collective-permute-start(bf16[2,32,256]{2,1,0:T(8,128)(2,1)} %shard_hbm.1), channel_id=1, source_target_pairs={{0,16},{1,25},{2,18},{3,27},{4,20},{5,29},{6,22},{7,31},{8,24},{9,... | collective-permute-start | bytes 98312 | tf_op jit(solution)/shard_map/ppermute | solution.py:26
  4.8 6.3 %collective-permute-start.2 = (bf16[2,32,256]{2,1,0:T(8,128)(2,1)}, bf16[2,32,256]{2,1,0:T(8,128)(2,1)S(1)}, u32[]{:S(2)}, u32[]{:S(2)}) collective-permute-start(bf16[2,32,256]{2,1,0:T(8,128)(2,1)} %shard_hbm.1), channel_id=1, source_target_pairs={{0,20},{1,29},{2,22},{3,31},{4,16},{5,25},{6,18},{7,27},{8,28},{9,... | collective-permute-start | bytes 98312 | tf_op jit(solution)/shard_map/ppermute | solution.py:26
  6.1 5.1 %collective-permute-start.3 = (bf16[2,32,256]{2,1,0:T(8,128)(2,1)}, bf16[2,32,256]{2,1,0:T(8,128)(2,1)S(1)}, u32[]{:S(2)}, u32[]{:S(2)}) collective-permute-start(bf16[2,32,256]{2,1,0:T(8,128)(2,1)} %shard_hbm.1), channel_id=1, source_target_pairs={{0,12},{1,9},{2,14},{3,11},{4,8},{5,13},{6,10},{7,15},{8,4},{9,1},... | collective-permute-start | bytes 98312 | tf_op jit(solution)/shard_map/ppermute | solution.py:26
  7.6 3.5 %collective-permute-start.4 = (bf16[2,32,256]{2,1,0:T(8,128)(2,1)}, bf16[2,32,256]{2,1,0:T(8,128)(2,1)S(1)}, u32[]{:S(2)}, u32[]{:S(2)}) collective-permute-start(bf16[2,32,256]{2,1,0:T(8,128)(2,1)} %shard_hbm.1), channel_id=1, source_target_pairs={{1,5},{3,7},{5,1},{7,3},{9,13},{11,15},{13,9},{15,11},{17,21},{19,... | collective-permute-start | bytes 98312 | tf_op jit(solution)/shard_map/ppermute | solution.py:26
  10.2 1.9 %collective-permute-start = (bf16[96,512]{1,0:T(8,128)(2,1)S(1)}, bf16[96,512]{1,0:T(8,128)(2,1)S(1)}, u32[]{:S(2)}, u32[]{:S(2)}) collective-permute-start(bf16[96,512]{1,0:T(8,128)(2,1)S(1)} %get-tuple-element.20), channel_id=1, source_target_pairs={{0,1},{1,0},{2,3},{3,2},{4,5},{5,4},{6,7},{7,6},{8,9},{9,8},{10,11... | collective-permute-start | bytes 294920 | tf_op jit(solution)/shard_map/ppermute | solution.py:52
  11.2 2.2 %collective-permute-start.5 = (bf16[8,32,256]{2,1,0:T(8,128)(2,1)S(1)}, bf16[8,32,256]{2,1,0:T(8,128)(2,1)S(1)}, u32[]{:S(2)}, u32[]{:S(2)}) collective-permute-start(bf16[8,32,256]{2,1,0:T(8,128)(2,1)S(1)} %constant_dynamic-update-slice_fusion.rest_1_.rest_0_), channel_id=1, source_target_pairs={{0,1},{1,0},{2,3},{3,2},{4,5},{5,4},{6,7},{7,6},{8,9},{9,8},{10,11... | collective-permute-start | bytes 393224 | tf_op jit(solution)/shard_map/ppermute | solution.py:52
  14.4 5.1 %collective-permute-start.8 = (bf16[96,512]{1,0:T(8,128)(2,1)S(1)}, bf16[96,512]{1,0:T(8,128)(2,1)S(1)}, u32[]{:S(2)}, u32[]{:S(2)}) collective-permute-start(bf16[96,512]{1,0:T(8,128)(2,1)S(1)} %get-tuple-element.34), channel_id=1, source_target_pairs={{0,2},{1,3},{2,0},{3,1},{4,6},{5,7},{6,4},{7,5},{8,10},{9,11},{10,... | collective-permute-start | bytes 294920 | tf_op jit(solution)/shard_map/ppermute | solution.py:402
  15.9 1.3 %copy-start.1 = (bf16[384,512]{1,0:T(8,128)(2,1)S(1)}, bf16[384,512]{1,0:T(8,128)(2,1)}, u32[]{:S(2)}) copy-start(bf16[384,512]{1,0:T(8,128)(2,1)} %own_ref.1) | copy-start | bytes 1179652
  16.6 2.9 %copy-start = (bf16[6,256,256]{2,1,0:T(8,128)(2,1)S(1)}, bf16[6,256,256]{2,1,0:T(8,128)(2,1)}, u32[]{:S(2)}) copy-start(bf16[6,256,256]{2,1,0:T(8,128)(2,1)} %suffix_ref.1) | copy-start | bytes 2359300
  16.6 2.9 %copy-start.2 = (bf16[384,256]{1,0:T(8,128)(2,1)S(1)}, bf16[384,256]{1,0:T(8,128)(2,1)}, u32[]{:S(2)}) copy-start(bf16[384,256]{1,0:T(8,128)(2,1)} %tree_ref.1) | copy-start | bytes 589828
  16.6 2.9 %copy-start.3 = (s32[6,64]{1,0:T(8,128)S(1)}, s32[6,64]{1,0:T(8,128)}, u32[]{:S(2)}) copy-start(s32[6,64]{1,0:T(8,128)} %parents_ref.1) | copy-start | bytes 4612
  16.6 2.9 %copy-start.4 = (s32[6,8]{1,0:T(8,128)S(1)}, s32[6,8]{1,0:T(8,128)}, u32[]{:S(2)}) copy-start(s32[6,8]{1,0:T(8,128)} %accepted_ref.1) | copy-start | bytes 580
  16.6 2.9 %copy-start.5 = (s32[6]{0:T(128)S(1)}, s32[6]{0:T(128)}, u32[]{:S(2)}) copy-start(s32[6]{0:T(128)} %length_ref.1) | copy-start | bytes 76
  16.6 2.9 %copy-start.6 = (s32[6]{0:T(128)S(1)}, s32[6]{0:T(128)}, u32[]{:S(2)}) copy-start(s32[6]{0:T(128)} %group_ref.1) | copy-start | bytes 76
  16.6 9.1 %collective-permute-start.9 = (bf16[96,1536]{1,0:T(8,128)(2,1)S(1)}, bf16[96,1536]{1,0:T(8,128)(2,1)S(1)}, u32[]{:S(2)}, u32[]{:S(2)}) collective-permute-start(bf16[96,1536]{1,0:T(8,128)(2,1)S(1)} %far_rest.1), channel_id=1, source_target_pairs={{0,2},{1,3},{2,0},{3,1},{4,6},{5,7},{6,4},{7,5},{8,10},{9,11},{10,... | collective-permute-start | bytes 884744 | tf_op jit(solution)/shard_map/ppermute | solution.py:407
  17.2 2.3 %collective-permute-start.7 = (bf16[384,512]{1,0:T(8,128)(2,1)S(1)}, bf16[384,512]{1,0:T(8,128)(2,1)S(1)}, u32[]{:S(2)}, u32[]{:S(2)}) collective-permute-start(bf16[384,512]{1,0:T(8,128)(2,1)S(1)} %copy-done.1), channel_id=1, source_target_pairs={{0,1},{1,0},{2,3},{3,2},{4,5},{5,4},{6,7},{7,6},{8,9},{9,8},{10,11... | collective-permute-start | bytes 1179656 | tf_op jit(solution)/shard_map/ppermute | solution.py:52

commit v9 on v7

--- a/solution.py
+++ b/solution.py
@@ -14,7 +14,7 @@
 
 
 def fetch_shards(shard, req_count, tp_count):
-    masks = ((4, 5, 3), (6, 7, 2, 1))
+    masks = ((5, 4, 3), (7, 6, 2, 1))
     arrived = []
     for step in range(fetches):
         pairs = []

time: 26.7 us -> 26.7 us (level)
  no operation moved by 1% of the time
where the time goes in v9:
time: 26.7 us; the launch traced here: 26.5 us
  starting transfers between devices  11.6 us (43%)
  Pallas kernels  8.97 us (34%)
  waiting for transfers between devices  5.05 us (19%)
  between operations  0.81 us (3%)
    ppermute x4, starting transfers between devices, fetch_shards(): arrived.append(lax.ppermute(shard, ('req', 'tp'), pairs))  7.12 us
    pallas_call x4, Pallas kernels, chunk(): pl.pallas_call(kernel, in_specs=[in_smem()] * len(scalars) + [in_vmem()]...  5.82 us
    ppermute x1, waiting for transfers between devices, local(): late_arrived = lax.ppermute(late_far, 'tp', across)  2.78 us
    ppermute x4, starting transfers between devices, swap_in_pair(): return lax.ppermute(array, 'tp', [(t, t ^ 1) for t in range(tp_count)])  2.38 us
    ppermute x1, waiting for transfers between devices, local(): early_arrived = touched(lax.ppermute(early_far, 'tp', across))  2.25 us
    pallas_call x1, Pallas kernels, load(): pl.pallas_call(functools.partial(load_kernel, chunk_rows), in_specs=[pl.B...  1.95 us
    ppermute x1, starting transfers between devices, local(): early_arrived = touched(lax.ppermute(early_far, 'tp', across))  1.54 us
    pallas_call x1, Pallas kernels, private(): pl.pallas_call(functools.partial(private_kernel, unit, chunk_rows, node_c...  1.2 us
  transfers between devices with their start and end apart: 10, of which 2 were waited for; matrix products, arithmetic and copies ran while one was open for 0% of the time, Pallas kernels for 27%

profile of v9, /device:TPU:0, one launch (start us, length us, event | category | flops | bytes accessed | tf_op | source)
XLA Modules:
  0.0 26.5 jit_solution(17226473092401431334)
XLA Ops:
  0.6 0.5 %collective-permute-start.6 = (bf16[512,2048]{1,0:T(8,128)(2,1)}, bf16[512,2048]{1,0:T(8,128)(2,1)S(1)}, u32[]{:S(2)}, u32[]{:S(2)}) collective-permute-start(bf16[512,2048]{1,0:T(8,128)(2,1)} %weight_hbm.1), channel_id=1, source_target_pairs={{0,1},{1,0},{2,3},{3,2},{4,5},{5,4},{6,7},{7,6},{8,9},{9,8},{10,11... | collective-permute-start | bytes 6291464 | tf_op jit(solution)/shard_map/ppermute | solution.py:52
  1.1 4.6 %collective-permute-start.1 = (bf16[2,32,256]{2,1,0:T(8,128)(2,1)}, bf16[2,32,256]{2,1,0:T(8,128)(2,1)S(1)}, u32[]{:S(2)}, u32[]{:S(2)}) collective-permute-start(bf16[2,32,256]{2,1,0:T(8,128)(2,1)} %shard_hbm.1), channel_id=1, source_target_pairs={{0,20},{1,29},{2,22},{3,31},{4,16},{5,25},{6,18},{7,27},{8,28},{9,... | collective-permute-start | bytes 98312 | tf_op jit(solution)/shard_map/ppermute | solution.py:26
  5.8 0.3 %collective-permute-start.2 = (bf16[2,32,256]{2,1,0:T(8,128)(2,1)}, bf16[2,32,256]{2,1,0:T(8,128)(2,1)S(1)}, u32[]{:S(2)}, u32[]{:S(2)}) collective-permute-start(bf16[2,32,256]{2,1,0:T(8,128)(2,1)} %shard_hbm.1), channel_id=1, source_target_pairs={{0,16},{1,25},{2,18},{3,27},{4,20},{5,29},{6,22},{7,31},{8,24},{9,... | collective-permute-start | bytes 98312 | tf_op jit(solution)/shard_map/ppermute | solution.py:26
  6.1 1.5 %collective-permute-start.3 = (bf16[2,32,256]{2,1,0:T(8,128)(2,1)}, bf16[2,32,256]{2,1,0:T(8,128)(2,1)S(1)}, u32[]{:S(2)}, u32[]{:S(2)}) collective-permute-start(bf16[2,32,256]{2,1,0:T(8,128)(2,1)} %shard_hbm.1), channel_id=1, source_target_pairs={{0,12},{1,9},{2,14},{3,11},{4,8},{5,13},{6,10},{7,15},{8,4},{9,1},... | collective-permute-start | bytes 98312 | tf_op jit(solution)/shard_map/ppermute | solution.py:26
  7.6 0.7 %collective-permute-start.4 = (bf16[2,32,256]{2,1,0:T(8,128)(2,1)}, bf16[2,32,256]{2,1,0:T(8,128)(2,1)S(1)}, u32[]{:S(2)}, u32[]{:S(2)}) collective-permute-start(bf16[2,32,256]{2,1,0:T(8,128)(2,1)} %shard_hbm.1), channel_id=1, source_target_pairs={{1,5},{3,7},{5,1},{7,3},{9,13},{11,15},{13,9},{15,11},{17,21},{19,... | collective-permute-start | bytes 98312 | tf_op jit(solution)/shard_map/ppermute | solution.py:26
  8.3 1.9 %load.1 = (f32[128,64]{1,0:T(8,128)S(1)}, f32[2,8,256]{2,1,0:T(8,128)S(1)}, bf16[96,512]{1,0:T(8,128)(2,1)S(1)}, bf16[128,256]{1,0:T(8,128)(2,1)S(1)}, bf16[2,25...) custom-call(s32[6,64]{1,0:T(8,128)} %parents_ref.1, ...), custom_call_target="tpu_custom_call" | custom-call | flops 100000000 | bytes 2000000 | tf_op jit(solution)/shard_map/load/pallas_call | solution.py:231
  10.2 0.0 collective-permute-done.1
  10.2 0.9 %collective-permute-start = (bf16[96,512]{1,0:T(8,128)(2,1)S(1)}, bf16[96,512]{1,0:T(8,128)(2,1)S(1)}, u32[]{:S(2)}, u32[]{:S(2)}) collective-permute-start(bf16[96,512]{1,0:T(8,128)(2,1)S(1)} %get-tuple-element.20), channel_id=1, source_target_pairs={{0,1},{1,0},{2,3},{3,2},{4,5},{5,4},{6,7},{7,6},{8,9},{9,8},{10,11... | collective-permute-start | bytes 294920 | tf_op jit(solution)/shard_map/ppermute | solution.py:52
  11.2 0.0 collective-permute-done.2
  11.2 0.0 collective-permute-done.3
  11.2 0.0 collective-permute-done.4
  11.2 1.0 %collective-permute-start.5 = (bf16[8,32,256]{2,1,0:T(8,128)(2,1)S(1)}, bf16[8,32,256]{2,1,0:T(8,128)(2,1)S(1)}, u32[]{:S(2)}, u32[]{:S(2)}) collective-permute-start(bf16[8,32,256]{2,1,0:T(8,128)(2,1)S(1)} %constant_dynamic-update-slice_fusion.rest_1_.rest_0_), channel_id=1, source_target_pairs={{0,1},{1,0},{2,3},{3,2},{4,5},{5,4},{6,7},{7,6},{8,9},{9,8},{10,11... | collective-permute-start | bytes 393224 | tf_op jit(solution)/shard_map/ppermute | solution.py:52
  12.2 0.0 collective-permute-done.in_ref
  12.2 1.2 %private.1.state_ref = f32[768,512]{1,0:T(8,128)S(1)} custom-call(f32[128,64]{1,0:T(8,128)S(1)} %get-tuple-element.21.bias_ref, f32[2,8,256]{2,1,0:T(8,128)S(1)} %get-tuple-element.22.notes_ref, bf16[96,512]{1,0:T(8,128)(2,1)S(1)} %get-tuple-element.19.own_ref, bf16[128,256]{1,0:T(8,128)(2,1)S(1)} %get-tuple-element.23.tree_ref, ...), custom_call_target="tpu_custom_call" | custom-call | flops 300000000 | bytes 500000 | tf_op jit(solution)/shard_map/private/pallas_call | solution.py:261
  13.4 0.0 collective-permute-done.5.rest_1_.rest_2_
  13.4 0.0 collective-permute-done.6.rest_3_.weight_other_ref.rest_4_
  13.4 1.0 %far_chunk.1 = (bf16[96,512]{1,0:T(8,128)(2,1)S(1)}, bf16[96,1024]{1,0:T(8,128)(2,1)S(1)}) custom-call(bf16[96,512]{1,0:T(8,128)(2,1)S(1)} %get-tuple-element.19.own_ref, bf16[96,512]{1,0:T(8,128)(2,1)S(1)} %touch.2.other_ref, f32[768,512]{1,0:T(8,128)S(1)} %private.1.state_ref, bf16[8,32,256]{2,1,0:T(8,128)(2,1)S(1)} %constant_dynamic-update-slice_fusion.rest_1_.rest_0_, ...), custom_call_target="tpu_custom_call" | custom-call | flops 200000000 | bytes 1000000 | tf_op jit(solution)/shard_map/far_chunk/pallas_call | solution.py:340
  14.4 1.5 %collective-permute-start.8 = (bf16[96,512]{1,0:T(8,128)(2,1)S(1)}, bf16[96,512]{1,0:T(8,128)(2,1)S(1)}, u32[]{:S(2)}, u32[]{:S(2)}) collective-permute-start(bf16[96,512]{1,0:T(8,128)(2,1)S(1)} %get-tuple-element.34), channel_id=1, source_target_pairs={{0,2},{1,3},{2,0},{3,1},{4,6},{5,7},{6,4},{7,5},{8,10},{9,11},{10,... | collective-permute-start | bytes 294920 | tf_op jit(solution)/shard_map/ppermute | solution.py:382
  15.9 0.0 copy-start.1
  15.9 0.6 %far_rest.1 = bf16[96,1536]{1,0:T(8,128)(2,1)S(1)} custom-call(bf16[96,1024]{1,0:T(8,128)(2,1)S(1)} %get-tuple-element.31.attended_ref, bf16[512,2048]{1,0:T(8,128)(2,1)S(1)} %get-tuple-element.30.rest_2_.weight_own_ref.rest_3_, bf16[512,2048]{1,0:T(8,128)(2,1)S(1)} %collective-permute-done.6.rest_3_.weight_other_ref.rest_4_), custom_call_target="tpu_custom_call" | custom-call | flops 300000000 | bytes 1000000 | tf_op jit(solution)/shard_map/far_rest/pallas_call | solution.py:340
  16.6 0.0 copy-start
  16.6 0.0 copy-start.2
  16.6 0.0 copy-start.3
  16.6 0.0 copy-start.4
  16.6 0.0 copy-start.5
  16.6 0.0 copy-start.6
  16.6 0.6 %collective-permute-start.9 = (bf16[96,1536]{1,0:T(8,128)(2,1)S(1)}, bf16[96,1536]{1,0:T(8,128)(2,1)S(1)}, u32[]{:S(2)}, u32[]{:S(2)}) collective-permute-start(bf16[96,1536]{1,0:T(8,128)(2,1)S(1)} %far_rest.1), channel_id=1, source_target_pairs={{0,2},{1,3},{2,0},{3,1},{4,6},{5,7},{6,4},{7,5},{8,10},{9,11},{10,... | collective-permute-start | bytes 884744 | tf_op jit(solution)/shard_map/ppermute | solution.py:387
  17.2 0.0 copy-done.1
  17.2 0.0 collective-permute-start.7
  17.2 2.2 %collective-permute-done.8.in_ref = bf16[96,512]{1,0:T(8,128)(2,1)S(1)} collective-permute-done((bf16[96,512]{1,0:T(8,128)(2,1)S(1)}, bf16[96,512]{1,0:T(8,128)(2,1)S(1)}, u32[]{:S(2)}, u32[]{:S(2)}) %collective-permute-start.8) | collective-permute-done | bytes 98336 | tf_op jit(solution)/shard_map/ppermute | solution.py:382
  19.5 0.0 collective-permute-done.7.other_ref
  19.5 0.0 copy-done
  19.5 0.0 copy-done.2
  19.5 0.0 copy-done.3
  19.5 0.0 copy-done.4
  19.5 0.0 copy-done.5
  19.5 0.0 copy-done.6
  19.5 3.4 %near_chunk.1 = (f32[96,2048]{1,0:T(8,128)S(1)}, bf16[6,8,256]{2,1,0:T(8,128)(2,1)}) custom-call(s32[6]{0:T(128)S(1)} %copy-done.5, s32[6]{0:T(128)S(1)} %copy-done.6, bf16[384,512]{1,0:T(8,128)(2,1)S(1)} %copy-done.1, bf16[384,512]{1,0:T(8,128)(2,1)S(1)} %collective-permute-done.7.other_ref, s32[6,64]{1,0:T(8,128)S(1)} %copy-done.3, s32[6,8]{1,0:T(8,128)S(1)} %copy-done.4, ...), custom_call_target="tpu_custom_call" | custom-call | flops 500000000 | bytes 1000000 | tf_op jit(solution)/shard_map/near_chunk/pallas_call | solution.py:340
  22.9 2.8 %collective-permute-done.9.rest_1_ = bf16[96,1536]{1,0:T(8,128)(2,1)S(1)} collective-permute-done((bf16[96,1536]{1,0:T(8,128)(2,1)S(1)}, bf16[96,1536]{1,0:T(8,128)(2,1)S(1)}, u32[]{:S(2)}, u32[]{:S(2)}) %collective-permute-start.9) | collective-permute-done | bytes 294944 | tf_op jit(solution)/shard_map/ppermute | solution.py:387
  25.7 0.8 %sum.1 = bf16[96,2048]{1,0:T(8,128)(2,1)} custom-call(f32[96,2048]{1,0:T(8,128)S(1)} %get-tuple-element.33.near_ref, bf16[96,512]{1,0:T(8,128)(2,1)S(1)} %touch.3.rest_0_, bf16[96,1536]{1,0:T(8,128)(2,1)S(1)} %collective-permute-done.9.rest_1_), custom_call_target="tpu_custom_call" | custom-call | flops 1000000 | bytes 1000000 | tf_op jit(solution)/shard_map/sum/pallas_call | solution.py:340
  (6 shorter events, 0.0 us)
Async XLA Ops:
  0.6 12.8 %collective-permute-start.6 = (bf16[512,2048]{1,0:T(8,128)(2,1)}, bf16[512,2048]{1,0:T(8,128)(2,1)S(1)}, u32[]{:S(2)}, u32[]{:S(2)}) collective-permute-start(bf16[512,2048]{1,0:T(8,128)(2,1)} %weight_hbm.1), channel_id=1, source_target_pairs={{0,1},{1,0},{2,3},{3,2},{4,5},{5,4},{6,7},{7,6},{8,9},{9,8},{10,11... | collective-permute-start | bytes 6291464 | tf_op jit(solution)/shard_map/ppermute | solution.py:52
  1.1 9.1 %collective-permute-start.1 = (bf16[2,32,256]{2,1,0:T(8,128)(2,1)}, bf16[2,32,256]{2,1,0:T(8,128)(2,1)S(1)}, u32[]{:S(2)}, u32[]{:S(2)}) collective-permute-start(bf16[2,32,256]{2,1,0:T(8,128)(2,1)} %shard_hbm.1), channel_id=1, source_target_pairs={{0,20},{1,29},{2,22},{3,31},{4,16},{5,25},{6,18},{7,27},{8,28},{9,... | collective-permute-start | bytes 98312 | tf_op jit(solution)/shard_map/ppermute | solution.py:26
  5.8 5.4 %collective-permute-start.2 = (bf16[2,32,256]{2,1,0:T(8,128)(2,1)}, bf16[2,32,256]{2,1,0:T(8,128)(2,1)S(1)}, u32[]{:S(2)}, u32[]{:S(2)}) collective-permute-start(bf16[2,32,256]{2,1,0:T(8,128)(2,1)} %shard_hbm.1), channel_id=1, source_target_pairs={{0,16},{1,25},{2,18},{3,27},{4,20},{5,29},{6,22},{7,31},{8,24},{9,... | collective-permute-start | bytes 98312 | tf_op jit(solution)/shard_map/ppermute | solution.py:26
  6.1 5.1 %collective-permute-start.3 = (bf16[2,32,256]{2,1,0:T(8,128)(2,1)}, bf16[2,32,256]{2,1,0:T(8,128)(2,1)S(1)}, u32[]{:S(2)}, u32[]{:S(2)}) collective-permute-start(bf16[2,32,256]{2,1,0:T(8,128)(2,1)} %shard_hbm.1), channel_id=1, source_target_pairs={{0,12},{1,9},{2,14},{3,11},{4,8},{5,13},{6,10},{7,15},{8,4},{9,1},... | collective-permute-start | bytes 98312 | tf_op jit(solution)/shard_map/ppermute | solution.py:26
  7.6 3.5 %collective-permute-start.4 = (bf16[2,32,256]{2,1,0:T(8,128)(2,1)}, bf16[2,32,256]{2,1,0:T(8,128)(2,1)S(1)}, u32[]{:S(2)}, u32[]{:S(2)}) collective-permute-start(bf16[2,32,256]{2,1,0:T(8,128)(2,1)} %shard_hbm.1), channel_id=1, source_target_pairs={{1,5},{3,7},{5,1},{7,3},{9,13},{11,15},{13,9},{15,11},{17,21},{19,... | collective-permute-start | bytes 98312 | tf_op jit(solution)/shard_map/ppermute | solution.py:26
  10.2 1.9 %collective-permute-start = (bf16[96,512]{1,0:T(8,128)(2,1)S(1)}, bf16[96,512]{1,0:T(8,128)(2,1)S(1)}, u32[]{:S(2)}, u32[]{:S(2)}) collective-permute-start(bf16[96,512]{1,0:T(8,128)(2,1)S(1)} %get-tuple-element.20), channel_id=1, source_target_pairs={{0,1},{1,0},{2,3},{3,2},{4,5},{5,4},{6,7},{7,6},{8,9},{9,8},{10,11... | collective-permute-start | bytes 294920 | tf_op jit(solution)/shard_map/ppermute | solution.py:52
  11.2 2.2 %collective-permute-start.5 = (bf16[8,32,256]{2,1,0:T(8,128)(2,1)S(1)}, bf16[8,32,256]{2,1,0:T(8,128)(2,1)S(1)}, u32[]{:S(2)}, u32[]{:S(2)}) collective-permute-start(bf16[8,32,256]{2,1,0:T(8,128)(2,1)S(1)} %constant_dynamic-update-slice_fusion.rest_1_.rest_0_), channel_id=1, source_target_pairs={{0,1},{1,0},{2,3},{3,2},{4,5},{5,4},{6,7},{7,6},{8,9},{9,8},{10,11... | collective-permute-start | bytes 393224 | tf_op jit(solution)/shard_map/ppermute | solution.py:52
  14.4 5.1 %collective-permute-start.8 = (bf16[96,512]{1,0:T(8,128)(2,1)S(1)}, bf16[96,512]{1,0:T(8,128)(2,1)S(1)}, u32[]{:S(2)}, u32[]{:S(2)}) collective-permute-start(bf16[96,512]{1,0:T(8,128)(2,1)S(1)} %get-tuple-element.34), channel_id=1, source_target_pairs={{0,2},{1,3},{2,0},{3,1},{4,6},{5,7},{6,4},{7,5},{8,10},{9,11},{10,... | collective-permute-start | bytes 294920 | tf_op jit(solution)/shard_map/ppermute | solution.py:382
  15.9 1.3 %copy-start.1 = (bf16[384,512]{1,0:T(8,128)(2,1)S(1)}, bf16[384,512]{1,0:T(8,128)(2,1)}, u32[]{:S(2)}) copy-start(bf16[384,512]{1,0:T(8,128)(2,1)} %own_ref.1) | copy-start | bytes 1179652
  16.6 2.9 %copy-start = (bf16[6,256,256]{2,1,0:T(8,128)(2,1)S(1)}, bf16[6,256,256]{2,1,0:T(8,128)(2,1)}, u32[]{:S(2)}) copy-start(bf16[6,256,256]{2,1,0:T(8,128)(2,1)} %suffix_ref.1) | copy-start | bytes 2359300
  16.6 2.9 %copy-start.2 = (bf16[384,256]{1,0:T(8,128)(2,1)S(1)}, bf16[384,256]{1,0:T(8,128)(2,1)}, u32[]{:S(2)}) copy-start(bf16[384,256]{1,0:T(8,128)(2,1)} %tree_ref.1) | copy-start | bytes 589828
  16.6 2.9 %copy-start.3 = (s32[6,64]{1,0:T(8,128)S(1)}, s32[6,64]{1,0:T(8,128)}, u32[]{:S(2)}) copy-start(s32[6,64]{1,0:T(8,128)} %parents_ref.1) | copy-start | bytes 4612
  16.6 2.9 %copy-start.4 = (s32[6,8]{1,0:T(8,128)S(1)}, s32[6,8]{1,0:T(8,128)}, u32[]{:S(2)}) copy-start(s32[6,8]{1,0:T(8,128)} %accepted_ref.1) | copy-start | bytes 580
  16.6 2.9 %copy-start.5 = (s32[6]{0:T(128)S(1)}, s32[6]{0:T(128)}, u32[]{:S(2)}) copy-start(s32[6]{0:T(128)} %length_ref.1) | copy-start | bytes 76
  16.6 2.9 %copy-start.6 = (s32[6]{0:T(128)S(1)}, s32[6]{0:T(128)}, u32[]{:S(2)}) copy-start(s32[6]{0:T(128)} %group_ref.1) | copy-start | bytes 76
  16.6 9.1 %collective-permute-start.9 = (bf16[96,1536]{1,0:T(8,128)(2,1)S(1)}, bf16[96,1536]{1,0:T(8,128)(2,1)S(1)}, u32[]{:S(2)}, u32[]{:S(2)}) collective-permute-start(bf16[96,1536]{1,0:T(8,128)(2,1)S(1)} %far_rest.1), channel_id=1, source_target_pairs={{0,2},{1,3},{2,0},{3,1},{4,6},{5,7},{6,4},{7,5},{8,10},{9,11},{10,... | collective-permute-start | bytes 884744 | tf_op jit(solution)/shard_map/ppermute | solution.py:387
  17.2 2.3 %collective-permute-start.7 = (bf16[384,512]{1,0:T(8,128)(2,1)S(1)}, bf16[384,512]{1,0:T(8,128)(2,1)S(1)}, u32[]{:S(2)}, u32[]{:S(2)}) collective-permute-start(bf16[384,512]{1,0:T(8,128)(2,1)S(1)} %copy-done.1), channel_id=1, source_target_pairs={{0,1},{1,0},{2,3},{3,2},{4,5},{5,4},{6,7},{7,6},{8,9},{9,8},{10,11... | collective-permute-start | bytes 1179656 | tf_op jit(solution)/shard_map/ppermute | solution.py:52
